TPU v7x, 32 devices: a whole 2x2x4 slice. The times are simulated.
32 devices in a mesh: dp: 8 (over y, x, core), tp: 4 (over z).
Axes of the slice: x: 2, y: 2, z: 4, core: 2. Of those that a mesh axis runs over, the one named last changes fastest.
Arguments:
- hidden_in: bfloat16 [8, 2048, 2048], P('dp', 'tp'), may hold values from -6 to 6
- triple_projection_weight: bfloat16 [2048, 3, 2048], P('dp', None, 'tp'), may hold values from -0.125 to 0.125
- triple_projection_bias: bfloat16 [3, 256, 8], P(None, 'tp', 'dp'), may hold values from -1 to 1
- attention_out_weight: bfloat16 [2048, 2048], P('tp', 'dp'), may hold values from -1.5 to 1.5
- b_dense: bfloat16 [2048], P('dp'), may hold values from -1 to 1
- feedforward_in_weight: bfloat16 [2048, 8192], P('dp', 'tp'), may hold values from -0.125 to 0.125
- feedforward_in_bias: bfloat16 [1024, 8], P('tp', 'dp'), may hold values from -1 to 1
- feedforward_out_weight: bfloat16 [8192, 2048], P('tp', 'dp'), may hold values from -0.0625 to 0.0625
- b_fc2: bfloat16 [2048], P('dp'), may hold values from -1 to 1
- ln1_gain: bfloat16 [2048], P('dp'), may hold values from 0.5 to 1.5
- ln1_bias: bfloat16 [2048], P('dp'), may hold values from -1 to 1
- ln2_gain: bfloat16 [2048], P('dp'), may hold values from 0.5 to 1.5
- ln2_bias: bfloat16 [2048], P('dp'), may hold values from -1 to 1
- grad_out: bfloat16 [8, 2048, 2048], P('dp', 'tp'), may hold values from -6 to 6
Outputs:
- hidden_out: bfloat16 [8, 2048, 2048], P('dp', 'tp')
- grad_in: float32 [8, 2048, 2048], P('dp', 'tp')
- grad_w_qkv: float32 [2048, 3, 2048], P('dp', None, 'tp')
- grad_b_qkv: float32 [3, 256, 8], P(None, 'tp', 'dp')
- grad_w_dense: float32 [2048, 2048], P('tp', 'dp')
- grad_b_dense: float32 [2048], P('dp')
- grad_w_fc1: float32 [2048, 8192], P('dp', 'tp')
- grad_b_fc1: float32 [1024, 8], P('tp', 'dp')
- grad_w_fc2: float32 [8192, 2048], P('tp', 'dp')
- grad_b_fc2: float32 [2048], P('dp')
- grad_ln1_gain: float32 [2048], P('dp')
- grad_ln1_bias: float32 [2048], P('dp')
- grad_ln2_gain: float32 [2048], P('dp')
- grad_ln2_bias: float32 [2048], P('dp')
All inputs are finite; a program needn't handle non-finite values.
Results may differ from a plain program's by a relative error of at most 0.0097.
Values may be sent and summed in bfloat16 or wider, within the bound.
A program may use at most 320 MiB of HBM per device.

v0:
```python
import math

import jax
import jax.numpy as jnp
from jax import lax
from jax.sharding import PartitionSpec as P

HD = 256
ROT = 64


EPSILON = 1e-05
MASKED = -1e30


def norm_rows(resid, gain_vec, shift_vec):
    row_mean = jnp.mean(resid, axis=-1, keepdims=True)
    centered = resid - row_mean
    variance = jnp.mean(centered * centered, axis=-1, keepdims=True)
    return centered * lax.rsqrt(variance + EPSILON) * gain_vec + shift_vec


def norm_pull(resid, gain_vec, shift_vec, upstream):
    _, pullback = jax.vjp(norm_rows, resid, gain_vec, shift_vec)
    return pullback(upstream)


def rotary_tables(length, rot_dims):
    half_rot = rot_dims // 2
    exponent = jnp.arange(half_rot, dtype=jnp.float32) * (2.0 / rot_dims)
    inverse = jnp.exp(exponent * -math.log(10000.0))
    position = jnp.arange(length, dtype=jnp.float32)
    angle = position[:, None] * inverse[None, :]
    angle = jnp.concatenate([angle, angle], axis=1)
    return (jnp.cos(angle), jnp.sin(angle))


def rotate(part, cosine, sine_tab):
    rot_dims = cosine.shape[1]
    half_rot = rot_dims // 2
    rot_part = part[..., :rot_dims]
    turned = jnp.concatenate([-rot_part[..., half_rot:], rot_part[..., :half_rot]], axis=-1)
    moved = rot_part * cosine[:, None, :] + turned * sine_tab[:, None, :]
    return jnp.concatenate([moved, part[..., rot_dims:]], axis=-1)


def rotate_back(upstream, cosine, sine_tab):
    rot_dims = cosine.shape[1]
    half_rot = rot_dims // 2
    rot_part = upstream[..., :rot_dims]
    turned = rot_part * sine_tab[:, None, :]
    swapped = jnp.concatenate([turned[..., half_rot:], -turned[..., :half_rot]], axis=-1)
    moved = rot_part * cosine[:, None, :] + swapped
    return jnp.concatenate([moved, upstream[..., rot_dims:]], axis=-1)


def gelu_exact(value):
    return 0.5 * value * (1.0 + lax.erf(value * (1.0 / math.sqrt(2.0))))


def mask_scores(scores, row_start, key_count):
    row_pos = row_start + jnp.arange(scores.shape[1], dtype=jnp.int32)
    col_pos = jnp.arange(key_count, dtype=jnp.int32)
    return jnp.where(col_pos[None, None, :] <= row_pos[None, :, None], scores, MASKED)


def attend_forward(query_rows, key_rows, value_rows, block_rows, score_scale):
    head_parts = []
    log_parts = []
    for row_start in range(0, query_rows.shape[0], block_rows):
        query_blk = query_rows[row_start : row_start + block_rows]
        scores = (
            jnp.einsum("qhd,khd->hqk", query_blk, key_rows, preferred_element_type=jnp.float32)
            * score_scale
        )
        scores = mask_scores(scores, row_start, key_rows.shape[0])
        row_max = jnp.max(scores, axis=-1, keepdims=True)
        exp_scores = jnp.exp(scores - row_max)
        row_total = jnp.sum(exp_scores, axis=-1, keepdims=True)
        probabilities = (exp_scores / row_total).astype(jnp.bfloat16)
        attended = jnp.einsum(
            "hqk,khd->qhd", probabilities, value_rows, preferred_element_type=jnp.float32
        )
        head_parts.append(attended.astype(jnp.bfloat16))
        log_parts.append(row_max + jnp.log(row_total))
    return (jnp.concatenate(head_parts, axis=0), jnp.concatenate(log_parts, axis=1))


def attend_backward(query_rows, key_rows, value_rows, log_total, d_heads, block_rows, score_scale):
    query_parts = []
    d_keys = jnp.zeros(key_rows.shape, jnp.float32)
    d_values = jnp.zeros(value_rows.shape, jnp.float32)
    for row_start in range(0, query_rows.shape[0], block_rows):
        query_blk = query_rows[row_start : row_start + block_rows]
        grad_blk = d_heads[row_start : row_start + block_rows]
        scores = (
            jnp.einsum("qhd,khd->hqk", query_blk, key_rows, preferred_element_type=jnp.float32)
            * score_scale
        )
        scores = mask_scores(scores, row_start, key_rows.shape[0])
        probabilities = jnp.exp(scores - log_total[:, row_start : row_start + block_rows])
        low_probs = probabilities.astype(jnp.bfloat16)
        d_probs = jnp.einsum(
            "qhd,khd->hqk", grad_blk, value_rows, preferred_element_type=jnp.float32
        )
        inner = jnp.sum(probabilities * d_probs, axis=-1, keepdims=True)
        d_scores = (probabilities * (d_probs - inner)).astype(jnp.bfloat16)
        query_parts.append(
            jnp.einsum("hqk,khd->qhd", d_scores, key_rows, preferred_element_type=jnp.float32)
            * score_scale
        )
        d_keys = (
            d_keys
            + jnp.einsum("hqk,qhd->khd", d_scores, query_blk, preferred_element_type=jnp.float32)
            * score_scale
        )
        d_values = d_values + jnp.einsum(
            "hqk,qhd->khd", low_probs, grad_blk, preferred_element_type=jnp.float32
        )
    return (jnp.concatenate(query_parts, axis=0), d_keys, d_values)


def unpack(gathered):
    return (
        gathered[0].reshape(gathered[0].shape[0], -1),
        gathered[1].reshape(-1),
        gathered[2],
        gathered[3],
        gathered[4],
        gathered[5].reshape(-1),
        gathered[6],
        gathered[7],
        gathered[8],
        gathered[9],
        gathered[10],
        gathered[11],
    )


def body(
    hidden_in,
    triple_projection_weight,
    triple_projection_bias,
    attention_out_weight,
    b_dense,
    feedforward_in_weight,
    feedforward_in_bias,
    feedforward_out_weight,
    b_fc2,
    ln1_gain,
    ln1_bias,
    ln2_gain,
    ln2_bias,
    grad_out,
):
    seq_count, piece_len, hidden_width = hidden_in.shape
    tp_count = lax.axis_size("tp")
    dp_count = lax.axis_size("dp")
    length = piece_len * tp_count
    local_heads = triple_projection_weight.shape[2] // HD
    block_rows = min(512, length)
    score_scale = HD ** (-0.5)
    cosine, sine_tab = rotary_tables(length, ROT)
    fetched = (
        lax.all_gather(triple_projection_weight, "dp", axis=0, tiled=True),
        lax.all_gather(triple_projection_bias, "dp", axis=2, tiled=True),
        lax.all_gather(attention_out_weight, "dp", axis=1, tiled=True),
        lax.all_gather(b_dense, "dp", axis=0, tiled=True),
        lax.all_gather(feedforward_in_weight, "dp", axis=0, tiled=True),
        lax.all_gather(feedforward_in_bias, "dp", axis=1, tiled=True),
        lax.all_gather(feedforward_out_weight, "dp", axis=1, tiled=True),
        lax.all_gather(b_fc2, "dp", axis=0, tiled=True),
        lax.all_gather(ln1_gain, "dp", axis=0, tiled=True),
        lax.all_gather(ln1_bias, "dp", axis=0, tiled=True),
        lax.all_gather(ln2_gain, "dp", axis=0, tiled=True),
        lax.all_gather(ln2_bias, "dp", axis=0, tiled=True),
    )
    (
        full_qkv,
        full_bqkv,
        full_dense,
        full_bdense,
        full_fc1,
        full_bfc1,
        full_fc2,
        full_bfc2,
        gain_one,
        shift_one,
        gain_two,
        shift_two,
    ) = unpack(fetched)
    resid_f32 = hidden_in.astype(jnp.float32)
    piece_one = norm_rows(
        resid_f32, gain_one.astype(jnp.float32), shift_one.astype(jnp.float32)
    ).astype(jnp.bfloat16)
    piece_two = norm_rows(
        resid_f32, gain_two.astype(jnp.float32), shift_two.astype(jnp.float32)
    ).astype(jnp.bfloat16)
    norm_one_all, norm_two_all = (
        lax.all_gather(piece_one, "tp", axis=1, tiled=True),
        lax.all_gather(piece_two, "tp", axis=1, tiled=True),
    )
    seq_index = 0
    attention_norm = norm_one_all[seq_index]
    feedforward_norm = norm_two_all[seq_index]
    triple_linear = jnp.dot(
        attention_norm, full_qkv, preferred_element_type=jnp.float32
    ) + full_bqkv.astype(jnp.float32)
    triple_linear = triple_linear.reshape(length, 3, local_heads, HD)
    query_rows = rotate(triple_linear[:, 0], cosine, sine_tab).astype(jnp.bfloat16)
    key_rows = rotate(triple_linear[:, 1], cosine, sine_tab).astype(jnp.bfloat16)
    value_rows = triple_linear[:, 2].astype(jnp.bfloat16)
    head_output_rows, log_total = attend_forward(
        query_rows, key_rows, value_rows, block_rows, score_scale
    )
    heads_flat = head_output_rows.reshape(length, -1)
    feedforward_entry = jnp.dot(
        feedforward_norm, full_fc1, preferred_element_type=jnp.float32
    ) + full_bfc1.astype(jnp.float32)
    activation_result = gelu_exact(feedforward_entry).astype(jnp.bfloat16)
    partial_value = jnp.dot(heads_flat, full_dense, preferred_element_type=jnp.float32)
    partial_value = partial_value + jnp.dot(
        activation_result, full_fc2, preferred_element_type=jnp.float32
    )
    summed = lax.psum_scatter(partial_value, "tp", scatter_dimension=0, tiled=True)
    layer_out = (
        resid_f32[seq_index]
        + summed
        + full_bdense.astype(jnp.float32)
        + full_bfc2.astype(jnp.float32)
    )
    results = [layer_out.astype(jnp.bfloat16)]
    stored = [
        (
            query_rows,
            key_rows,
            value_rows,
            heads_flat,
            log_total,
            feedforward_entry,
            activation_result,
        )
    ]
    hidden_out = jnp.stack(results)
    refetched = (
        lax.all_gather(triple_projection_weight, "dp", axis=0, tiled=True),
        lax.all_gather(triple_projection_bias, "dp", axis=2, tiled=True),
        lax.all_gather(attention_out_weight, "dp", axis=1, tiled=True),
        lax.all_gather(b_dense, "dp", axis=0, tiled=True),
        lax.all_gather(feedforward_in_weight, "dp", axis=0, tiled=True),
        lax.all_gather(feedforward_in_bias, "dp", axis=1, tiled=True),
        lax.all_gather(feedforward_out_weight, "dp", axis=1, tiled=True),
        lax.all_gather(b_fc2, "dp", axis=0, tiled=True),
        lax.all_gather(ln1_gain, "dp", axis=0, tiled=True),
        lax.all_gather(ln1_bias, "dp", axis=0, tiled=True),
        lax.all_gather(ln2_gain, "dp", axis=0, tiled=True),
        lax.all_gather(ln2_bias, "dp", axis=0, tiled=True),
    )
    (
        full_qkv,
        full_bqkv,
        full_dense,
        full_bdense,
        full_fc1,
        full_bfc1,
        full_fc2,
        full_bfc2,
        gain_one,
        shift_one,
        gain_two,
        shift_two,
    ) = unpack(refetched)
    gain_f32_one = gain_one.astype(jnp.float32)
    shift_f32_one = shift_one.astype(jnp.float32)
    gain_f32_two = gain_two.astype(jnp.float32)
    shift_f32_two = shift_two.astype(jnp.float32)
    cot_all = lax.all_gather(grad_out, "tp", axis=1, tiled=True)
    seq_index = 0
    (
        query_rows,
        key_rows,
        value_rows,
        heads_flat,
        log_total,
        feedforward_entry,
        activation_result,
    ) = stored[seq_index]
    cot_seq = cot_all[seq_index]
    attention_norm = norm_one_all[seq_index]
    feedforward_norm = norm_two_all[seq_index]
    d_heads = jnp.einsum(
        "ld,jd->lj", cot_seq, full_dense, preferred_element_type=jnp.float32
    ).astype(jnp.bfloat16)
    d_act = jnp.einsum("ld,fd->lf", cot_seq, full_fc2, preferred_element_type=jnp.float32)
    _, gelu_pull = jax.vjp(gelu_exact, feedforward_entry)
    d_fc = gelu_pull(d_act)[0].astype(jnp.bfloat16)
    sum_fc2 = jnp.einsum(
        "lf,ld->fd", activation_result, cot_seq, preferred_element_type=jnp.float32
    )
    sum_dense = jnp.einsum("lj,ld->jd", heads_flat, cot_seq, preferred_element_type=jnp.float32)
    sum_bias_out = jnp.sum(cot_seq.astype(jnp.float32), axis=0)
    sum_fc1 = jnp.einsum("ld,lf->df", feedforward_norm, d_fc, preferred_element_type=jnp.float32)
    sum_bfc1 = jnp.sum(d_fc.astype(jnp.float32), axis=0)
    d_norm_two = jnp.einsum("lf,df->ld", d_fc, full_fc1, preferred_element_type=jnp.float32)
    d_query, d_keys, d_values = attend_backward(
        query_rows,
        key_rows,
        value_rows,
        log_total,
        d_heads.reshape(length, local_heads, HD),
        block_rows,
        score_scale,
    )
    d_qkv = jnp.stack(
        [rotate_back(d_query, cosine, sine_tab), rotate_back(d_keys, cosine, sine_tab), d_values],
        axis=1,
    )
    d_qkv = d_qkv.astype(jnp.bfloat16).reshape(length, -1)
    sum_wqkv = jnp.einsum("ld,lj->dj", attention_norm, d_qkv, preferred_element_type=jnp.float32)
    sum_bqkv = jnp.sum(d_qkv.astype(jnp.float32), axis=0)
    d_norm_one = jnp.einsum("lj,dj->ld", d_qkv, full_qkv, preferred_element_type=jnp.float32)
    cot_piece = grad_out[seq_index].astype(jnp.float32)
    piece_grad_one = lax.psum_scatter(d_norm_one, "tp", scatter_dimension=0, tiled=True)
    piece_grad_two = lax.psum_scatter(d_norm_two, "tp", scatter_dimension=0, tiled=True)
    back_one, gain_grad_one, shift_grad_one = norm_pull(
        resid_f32[seq_index], gain_f32_one, shift_f32_one, piece_grad_one
    )
    back_two, gain_grad_two, shift_grad_two = norm_pull(
        resid_f32[seq_index], gain_f32_two, shift_f32_two, piece_grad_two
    )
    input_rows = [cot_piece + back_one + back_two]
    sum_norms = jnp.stack([gain_grad_one, shift_grad_one, gain_grad_two, shift_grad_two])
    grad_in = jnp.stack(input_rows)
    norm_totals = lax.psum(sum_norms, "tp")
    owned = (
        lax.psum_scatter(
            sum_wqkv.reshape(hidden_width, 3, -1), "dp", scatter_dimension=0, tiled=True
        ),
        lax.psum_scatter(sum_bqkv.reshape(3, -1, dp_count), "dp", scatter_dimension=2, tiled=True),
        lax.psum_scatter(sum_dense, "dp", scatter_dimension=1, tiled=True),
        lax.psum_scatter(sum_bias_out, "dp", scatter_dimension=0, tiled=True),
        lax.psum_scatter(sum_fc1, "dp", scatter_dimension=0, tiled=True),
        lax.psum_scatter(sum_bfc1.reshape(-1, dp_count), "dp", scatter_dimension=1, tiled=True),
        lax.psum_scatter(sum_fc2, "dp", scatter_dimension=1, tiled=True),
        lax.psum_scatter(norm_totals[0], "dp", scatter_dimension=0, tiled=True),
        lax.psum_scatter(norm_totals[1], "dp", scatter_dimension=0, tiled=True),
        lax.psum_scatter(norm_totals[2], "dp", scatter_dimension=0, tiled=True),
        lax.psum_scatter(norm_totals[3], "dp", scatter_dimension=0, tiled=True),
    )
    return (
        hidden_out,
        grad_in,
        owned[0],
        owned[1],
        owned[2],
        owned[3],
        owned[4],
        owned[5],
        owned[6],
        owned[3],
        owned[7],
        owned[8],
        owned[9],
        owned[10],
    )


def solution(mesh):
    return jax.shard_map(
        body,
        mesh=mesh,
        in_specs=(
            P("dp", "tp", None),
            P("dp", None, "tp"),
            P(None, "tp", "dp"),
            P("tp", "dp"),
            P("dp"),
            P("dp", "tp"),
            P("tp", "dp"),
            P("tp", "dp"),
            P("dp"),
            P("dp"),
            P("dp"),
            P("dp"),
            P("dp"),
            P("dp", "tp", None),
        ),
        out_specs=(
            P("dp", "tp", None),
            P("dp", "tp", None),
            P("dp", None, "tp"),
            P(None, "tp", "dp"),
            P("tp", "dp"),
            P("dp"),
            P("dp", "tp"),
            P("tp", "dp"),
            P("tp", "dp"),
            P("dp"),
            P("dp"),
            P("dp"),
            P("dp"),
            P("dp"),
        ),
        check_vma=False,
    )
```

profile of v0, /device:TPU:0, one launch (start us, length us, event | category | flops | bytes accessed | tf_op | source)
XLA Modules:
  0.0 1904.2 jit_solution(17394619816596397380)
XLA Ops:
  12.4 10.3 all-gather.3
  77.8 133.9 %all-gather.15.cloned.1.call-done = bf16[1,2048,2048]{2,1,0:T(8,128)(2,1)} async-done(((bf16[1,512,2048]{2,1,0:T(8,128)(2,1)}), bf16[1,2048,2048]{2,1,0:T(8,128)(2,1)}) %all-gather.15.cloned.1.call-update) | async-done | bytes 8388624 | tf_op jit(solution)/shard_map/all_gather | solution.py:200
  211.7 17.8 convolution_add_fusion
  263.4 127.7 %all-gather.27.cloned.1.call-done = bf16[1,2048,2048]{2,1,0:T(8,128)(2,1)} async-done(((bf16[1,512,2048]{2,1,0:T(8,128)(2,1)}), bf16[1,2048,2048]{2,1,0:T(8,128)(2,1)}) %all-gather.27.cloned.1.call-update) | async-done | bytes 8388624 | tf_op jit(solution)/shard_map/all_gather | solution.py:277
  523.0 9.8 multiply_bitcast_fusion
  595.4 20.5 %fusion.128 = f32[2048,2048]{1,0:T(8,128)} fusion(bf16[2048,1536]{0,1:T(8,128)(2,1)} %bitcast.226, bf16[2048,1536]{0,1:T(8,128)(2,1)} %bitcast.263), kind=kOutput, calls=%fused_computation.202 | convolution fusion | flops 12884901888 | bytes 29360128 | tf_op jit(solution)/shard_map/lj,dj->ld/dot_general | solution.py:321
  625.5 27.7 %multiply_convert_fusion = (bf16[2048,2048]{1,0:T(8,128)(2,1)}, f32[2048,2048]{1,0:T(8,128)}) fusion(f32[2048]{0:T(1024)S(1)} %reshape.364, bf16[2048,2048]{1,0:T(8,128)(2,1)} %all-gather.23.cloned.1.call-done, bf16[1,2048,2048]{2,1,0:T(8,128)(2,1)} %all-gather.21.cloned.1.call-done), kind=kOutput, calls=%fused_computation.3 | convolution fusion | flops 17205035008 | bytes 41951232 | tf_op jit(solution)/shard_map/dot_general | solution.py:217
  653.3 32.2 %convert_reduce_fusion = (f32[2048]{0:T(1024)}, bf16[2048,2048]{1,0:T(8,128)(2,1)S(1)}) fusion(bf16[2048,2048]{1,0:T(8,128)(2,1)} %all-gather.25.cloned.1.call-done, bf16[1,2048,2048]{2,1,0:T(8,128)(2,1)} %all-gather.27.cloned.1.call-done, f32[2048,2048]{1,0:T(8,128)} %get-tuple-element.141, f32[2048]{0:T(1024)S(1)} %reshape.364), kind=kOutput, calls=%fused_computation | convolution fusion | flops 17246976000 | bytes 41959424 | tf_op jit(solution)/shard_map/ld,fd->lf/dot_general | solution.py:294
  688.8 20.9 %fusion.129 = f32[2048,2048]{1,0:T(8,128)} fusion(bf16[2048,2048]{1,0:T(8,128)(2,1)S(1)} %get-tuple-element.143, bf16[2048,2048]{1,0:T(8,128)(2,1)S(1)} %copy-done.67), kind=kOutput, calls=%fused_computation.203 | convolution fusion | flops 17179869184 | bytes 33554432 | tf_op jit(solution)/shard_map/lf,df->ld/dot_general | solution.py:304
  741.0 24.4 %convolution_add_fusion.1 = f32[2048,2048]{1,0:T(8,128)} fusion(f32[2048,2048]{1,0:T(8,128)} %fusion.127, bf16[2048,2048]{1,0:T(8,128)(2,1)} %get-tuple-element.140, bf16[2048,2048]{1,0:T(8,128)(2,1)S(1)} %bitcast.261), kind=kOutput, calls=%fused_computation.8 | convolution fusion | flops 17184063488 | bytes 50331648 | tf_op jit(solution)/shard_map/dot_general | solution.py:222
  765.5 9.4 fusion.4
  775.0 19.3 %fusion = f32[2048,3,512]{2,0,1:T(8,128)} fusion(bf16[3,512,2048]{2,1,0:T(8,128)(2,1)} %bitcast.227, bf16[1,2048,2048]{2,1,0:T(8,128)(2,1)} %all-gather.15.cloned.1.call-done), kind=kOutput, calls=%fused_computation.9 | convolution fusion | flops 12884901888 | bytes 27262976 | tf_op jit(solution)/shard_map/ld,lj->dj/dot_general | solution.py:319
  794.3 24.5 %fusion.2 = f32[2048,2048]{1,0:T(8,128)} fusion(bf16[2048,2048]{1,0:T(8,128)(2,1)} %get-tuple-element.140, bf16[1,2048,2048]{2,1,0:T(8,128)(2,1)} %all-gather.27.cloned.1.call-done), kind=kOutput, calls=%fused_computation.11 | convolution fusion | flops 17179869184 | bytes 33554432 | tf_op jit(solution)/shard_map/lf,ld->fd/dot_general | solution.py:297
  818.9 24.5 %fusion.12 = f32[2048,2048]{1,0:T(8,128)} fusion(bf16[2048,2048]{1,0:T(8,128)(2,1)} %copy-done.72, bf16[1,2048,2048]{2,1,0:T(8,128)(2,1)} %all-gather.21.cloned.1.call-done), kind=kOutput, calls=%fused_computation.19 | convolution fusion | flops 17179869184 | bytes 33554432 | tf_op jit(solution)/shard_map/ld,lf->df/dot_general | solution.py:302
  844.1 9.1 all-gather.6
  868.2 67.8 %reduce-scatter.11.cloned.1.call-done = f32[512,2048]{1,0:T(8,128)} async-done(((f32[2048,2048]{1,0:T(8,128)}), f32[512,2048]{1,0:T(8,128)}) %reduce-scatter.11.cloned.1.call-update) | async-done | bytes 4194320 | tf_op jit(solution)/shard_map/reduce_scatter | solution.py:323
  936.0 283.5 %reduce-scatter.13.cloned.1.call-done = f32[512,2048]{1,0:T(8,128)} async-done(((f32[2048,2048]{1,0:T(8,128)}), f32[512,2048]{1,0:T(8,128)}) %reduce-scatter.13.cloned.1.call-update) | async-done | bytes 4194320 | tf_op jit(solution)/shard_map/reduce_scatter | solution.py:324
  1229.5 19.5 %psum.7 = f32[4,2048]{1,0:T(4,128)S(1)} all-reduce(f32[4,2048]{1,0:T(4,128)S(1)} %pad_maximum_fusion.5), channel_id=1, replica_groups=mesh['dp'=8,'tp'=4] {'tp'}, use_global_device_ids=true, to_apply=%region_36.37 | all-reduce | flops 8192 | bytes 65536 | tf_op jit(solution)/shard_map/psum | solution.py:334
  1249.0 25.1 %all-reduce.7 = (f32[3,64,8]{1,0,2:T(4,128)S(1)}, f32[2048]{0:T(1024)S(1)}, f32[256,8]{1,0:T(8,128)S(1)}, f32[2048]{0:T(1024)S(1)}, f32[2048]{0:T(1024)S(1)}, /*index=5*/f32[2048]{0:T(1024)S(1)}, f32[2048]{0:T(1024)S(1)}) all-reduce(f32[3,64,8]{1,0,2:T(4,128)S(1)} %copy.206, ...), channel_id=6, replica_groups=mesh['dp'=8,'tp'=4] {'dp'}, use_global_device_ids=true, to_apply=%region_24.25.clone | all-reduce | flops 13824 | bytes 110592
  1279.4 224.5 %reduce-scatter.9.cloned.1.call-done = f32[512,2048]{1,0:T(8,128)} async-done(((f32[2048,2048]{1,0:T(8,128)}), f32[512,2048]{1,0:T(8,128)}) %reduce-scatter.9.cloned.1.call-update) | async-done | bytes 4194320 | tf_op jit(solution)/shard_map/reduce_scatter | solution.py:225
  1512.7 47.6 %reduce-scatter.17.cloned.1.call-done = f32[512,256]{1,0:T(8,128)} async-done(((f32[512,2048]{1,0:T(8,128)}), f32[512,256]{1,0:T(8,128)}) %reduce-scatter.17.cloned.1.call-update) | async-done | bytes 524304 | tf_op jit(solution)/shard_map/reduce_scatter | solution.py:340
  1560.3 96.4 %reduce-scatter.15.cloned.1.call-done = f32[256,3,512]{2,0,1:T(8,128)} async-done(((f32[2048,3,512]{2,0,1:T(8,128)}), f32[256,3,512]{2,0,1:T(8,128)}) %reduce-scatter.15.cloned.1.call-update) | async-done | bytes 1572880 | tf_op jit(solution)/shard_map/reduce_scatter | solution.py:336
  1656.7 120.1 %reduce-scatter.21.cloned.1.call-done = f32[2048,256]{1,0:T(8,128)} async-done(((f32[2048,2048]{1,0:T(8,128)}), f32[2048,256]{1,0:T(8,128)}) %reduce-scatter.21.cloned.1.call-update) | async-done | bytes 2097168 | tf_op jit(solution)/shard_map/reduce_scatter | solution.py:344
  1776.8 120.0 %reduce-scatter.19.cloned.1.call-done = f32[256,2048]{1,0:T(8,128)} async-done(((f32[2048,2048]{1,0:T(8,128)}), f32[256,2048]{1,0:T(8,128)}) %reduce-scatter.19.cloned.1.call-update) | async-done | bytes 2097168 | tf_op jit(solution)/shard_map/reduce_scatter | solution.py:342
  (325 shorter events, 371.7 us)
Async XLA Ops:
  7.2 43.3 %copy-start.2 = (bf16[1,512,2048]{2,1,0:T(8,128)(2,1)S(1)}, bf16[1,512,2048]{2,1,0:T(8,128)(2,1)}, u32[]{:S(2)}) copy-start(bf16[1,512,2048]{2,1,0:T(8,128)(2,1)} %param.14) | copy-start | bytes 6291460
  7.2 70.6 %all-gather.17.cloned.1.call-start = ((), (), s32[]{:S(2)}) async-start(), calls=%async_computation.8 | async-start | bytes 7077888 | tf_op jit(solution)/shard_map/all_gather | solution.py:165
  9.7 202.0 %all-gather.15.cloned.1.call-start = ((), (), s32[]{:S(2)}) async-start(), calls=%async_computation.7 | async-start | bytes 10485760 | tf_op jit(solution)/shard_map/all_gather | solution.py:200
  54.7 208.8 %all-gather.19.cloned.1.call-start = ((), (), s32[]{:S(2)}) async-start(), calls=%async_computation.9 | async-start | bytes 2359296 | tf_op jit(solution)/shard_map/all_gather | solution.py:167
  55.4 335.8 %all-gather.27.cloned.1.call-start = ((), (), s32[]{:S(2)}) async-start(), calls=%async_computation.14 | async-start | bytes 10485760 | tf_op jit(solution)/shard_map/all_gather | solution.py:277
  56.0 569.5 %all-gather.21.cloned.1.call-start = ((), (), s32[]{:S(2)}) async-start(), calls=%async_computation.10 | async-start | bytes 10485760 | tf_op jit(solution)/shard_map/all_gather | solution.py:201
  56.6 568.9 %all-gather.23.cloned.1.call-start = ((), (), s32[]{:S(2)}) async-start(), calls=%async_computation.11 | async-start | bytes 9437184 | tf_op jit(solution)/shard_map/all_gather | solution.py:169
  57.1 596.2 %all-gather.25.cloned.1.call-start = ((), (), s32[]{:S(2)}) async-start(), calls=%async_computation.12 | async-start | bytes 9437184 | tf_op jit(solution)/shard_map/all_gather | solution.py:171
  57.9 878.1 %reduce-scatter.11.cloned.1.call-start = ((), (), s32[]{:S(2)}) async-start(), calls=%async_computation.15 | async-start | bytes 20971520 | tf_op jit(solution)/shard_map/reduce_scatter | solution.py:323
  413.3 145.5 %copy-start = (f32[2,512,2048]{2,1,0:T(8,128)}, f32[2,512,2048]{2,1,0:T(8,128)S(1)}, u32[]{:S(2)}) copy-start(f32[2,512,2048]{2,1,0:T(8,128)S(1)} %get-tuple-element.125) | copy-start | bytes 25165828
  418.2 68.1 %copy-start.51 = (f32[2,512]{1,0:T(2,128)}, f32[2,512]{1,0:T(2,128)S(1)}, u32[]{:S(2)}) copy-start(f32[2,512]{1,0:T(2,128)S(1)} %get-tuple-element.126) | copy-start | bytes 12292
  418.2 144.9 %copy-start.1 = (f32[2,512,2048]{2,1,0:T(8,128)}, f32[2,512,2048]{2,1,0:T(8,128)S(1)}, u32[]{:S(2)}) copy-start(f32[2,512,2048]{2,1,0:T(8,128)S(1)} %get-tuple-element.127) | copy-start | bytes 25165828
  615.9 603.7 %reduce-scatter.13.cloned.1.call-start = ((), (), s32[]{:S(2)}) async-start(), calls=%async_computation.16 | async-start | bytes 20971520 | tf_op jit(solution)/shard_map/reduce_scatter | solution.py:324
  653.3 35.5 %copy-start.67 = (bf16[2048,2048]{1,0:T(8,128)(2,1)S(1)}, bf16[2048,2048]{1,0:T(8,128)(2,1)}, u32[]{:S(2)}) copy-start(bf16[2048,2048]{1,0:T(8,128)(2,1)} %all-gather.23.cloned.1.call-done) | copy-start | bytes 25165828
  709.8 794.1 %reduce-scatter.9.cloned.1.call-start = ((), (), s32[]{:S(2)}) async-start(), calls=%async_computation.13 | async-start | bytes 20971520 | tf_op jit(solution)/shard_map/reduce_scatter | solution.py:225
  765.4 794.9 %reduce-scatter.17.cloned.1.call-start = ((), (), s32[]{:S(2)}) async-start(), calls=%async_computation.18 | async-start | bytes 4718592 | tf_op jit(solution)/shard_map/reduce_scatter | solution.py:340
  774.9 881.7 %reduce-scatter.15.cloned.1.call-start = ((), (), s32[]{:S(2)}) async-start(), calls=%async_computation.17 | async-start | bytes 14155776 | tf_op jit(solution)/shard_map/reduce_scatter | solution.py:336
  794.3 982.5 %reduce-scatter.21.cloned.1.call-start = ((), (), s32[]{:S(2)}) async-start(), calls=%async_computation.20 | async-start | bytes 18874368 | tf_op jit(solution)/shard_map/reduce_scatter | solution.py:344
  818.9 1078.0 %reduce-scatter.19.cloned.1.call-start = ((), (), s32[]{:S(2)}) async-start(), calls=%async_computation.19 | async-start | bytes 18874368 | tf_op jit(solution)/shard_map/reduce_scatter | solution.py:342
  863.2 356.4 %copy-start.3 = (bf16[1,512,2048]{2,1,0:T(8,128)(2,1)S(1)}, bf16[1,512,2048]{2,1,0:T(8,128)(2,1)}, u32[]{:S(2)}) copy-start(bf16[1,512,2048]{2,1,0:T(8,128)(2,1)} %param.14) | copy-start | bytes 6291460
  863.2 356.4 %copy-start.41 = (f32[8,1,256]{2,1,0:T(1,128)S(1)}, f32[8,1,256]{2,1,0:T(1,128)}, u32[]{:S(2)}) copy-start(f32[8,1,256]{2,1,0:T(1,128)} %copy-done.40) | copy-start | bytes 24580
  863.2 356.4 %copy-start.43 = (f32[8,1,256]{2,1,0:T(1,128)S(1)}, f32[8,1,256]{2,1,0:T(1,128)}, u32[]{:S(2)}) copy-start(f32[8,1,256]{2,1,0:T(1,128)} %copy-done.42) | copy-start | bytes 24580
  863.2 356.4 %copy-start.45 = (f32[512]{0:T(512)S(1)}, f32[512]{0:T(512)}, u32[]{:S(2)}) copy-start(f32[512]{0:T(512)} %copy-done.44) | copy-start | bytes 6148
  1276.9 620.0 %copy-start.64 = (f32[256]{0:T(256)}, f32[256]{0:T(256)S(1)}, u32[]{:S(2)}) copy-start(f32[256]{0:T(256)S(1)} %dynamic-slice.3) | copy-start | bytes 3076
  (73 other events, 429.8 us)
Sparse Core Ops, SparseCore 0:
  10.5 49.3 all-gather.16
  62.1 149.6 all-gather.14
  213.6 26.4 all-gather.18
  241.5 149.6 all-gather.26
  393.2 147.8 all-gather.20
  542.8 52.5 all-gather.22
  597.3 55.9 all-gather.24
  655.7 280.2 reduce-scatter.10
  938.5 281.0 reduce-scatter.12
  1221.8 282.0 reduce-scatter.8
  1508.2 52.0 reduce-scatter.16
  1564.2 92.3 reduce-scatter.14
  1660.8 115.9 reduce-scatter.20
  1780.8 115.9 reduce-scatter.18
where the time goes:
time: 1910 us; the launch traced here: 1900 us
  waiting for transfers between devices  1220 us (64%)
  matrix products  356 us (19%)
  other arithmetic  121 us (6%)
  blocking collectives  115 us (6%)
  local copies, waits for them, and re-layouts  70.3 us (4%)
    reduce_scatter x1, waiting for transfers between devices, body(): lax.psum_scatter(d_norm_two, 'tp', scatter_dimension=0, tiled=True)  284 us
    reduce_scatter x1, waiting for transfers between devices, body(): lax.psum_scatter(partial_value, 'tp', scatter_dimension=0, tiled=True)  225 us
    all_gather x1, waiting for transfers between devices, body(): lax.all_gather(piece_one, 'tp', axis=1, tiled=True)  134 us
    all_gather x1, waiting for transfers between devices, body(): cot_all = lax.all_gather(grad_out, 'tp', axis=1, tiled=True)  128 us
    reduce_scatter x1, waiting for transfers between devices, body(): lax.psum_scatter(sum_fc2, 'dp', scatter_dimension=1, tiled=True)  120 us
    reduce_scatter x1, waiting for transfers between devices, body(): lax.psum_scatter(sum_fc1, 'dp', scatter_dimension=0, tiled=True)  120 us
    reduce_scatter x1, waiting for transfers between devices, body(): lax.psum_scatter(sum_wqkv.reshape(hidden_width, 3, -1), 'dp', scatter_dim...  96.4 us
    reduce_scatter x1, waiting for transfers between devices, body(): lax.psum_scatter(d_norm_one, 'tp', scatter_dimension=0, tiled=True)  67.8 us
  transfers between devices with their start and end apart: 14, of which 10 were waited for; matrix products, arithmetic and copies ran while one was open for 28% of the time, Pallas kernels for 0%

commit v1 on v0

v1 whole, which is shorter than its diff:
```python
import math

import jax
import jax.numpy as jnp
from jax import lax
from jax.sharding import PartitionSpec as P

HD = 256
ROT = 64


EPSILON = 1e-05
MASKED = -1e30


def norm_rows(resid, gain_vec, shift_vec):
    row_mean = jnp.mean(resid, axis=-1, keepdims=True)
    centered = resid - row_mean
    variance = jnp.mean(centered * centered, axis=-1, keepdims=True)
    return centered * lax.rsqrt(variance + EPSILON) * gain_vec + shift_vec


def norm_pull(resid, gain_vec, shift_vec, upstream):
    _, pullback = jax.vjp(norm_rows, resid, gain_vec, shift_vec)
    return pullback(upstream)


def rotary_tables(length, rot_dims):
    half_rot = rot_dims // 2
    exponent = jnp.arange(half_rot, dtype=jnp.float32) * (2.0 / rot_dims)
    inverse = jnp.exp(exponent * -math.log(10000.0))
    position = jnp.arange(length, dtype=jnp.float32)
    angle = position[:, None] * inverse[None, :]
    angle = jnp.concatenate([angle, angle], axis=1)
    return (jnp.cos(angle), jnp.sin(angle))


def rotate(part, cosine, sine_tab):
    rot_dims = cosine.shape[1]
    half_rot = rot_dims // 2
    rot_part = part[..., :rot_dims]
    turned = jnp.concatenate([-rot_part[..., half_rot:], rot_part[..., :half_rot]], axis=-1)
    moved = rot_part * cosine[:, None, :] + turned * sine_tab[:, None, :]
    return jnp.concatenate([moved, part[..., rot_dims:]], axis=-1)


def rotate_back(upstream, cosine, sine_tab):
    rot_dims = cosine.shape[1]
    half_rot = rot_dims // 2
    rot_part = upstream[..., :rot_dims]
    turned = rot_part * sine_tab[:, None, :]
    swapped = jnp.concatenate([turned[..., half_rot:], -turned[..., :half_rot]], axis=-1)
    moved = rot_part * cosine[:, None, :] + swapped
    return jnp.concatenate([moved, upstream[..., rot_dims:]], axis=-1)


def gelu_exact(value):
    return 0.5 * value * (1.0 + lax.erf(value * (1.0 / math.sqrt(2.0))))


def mask_scores(scores, row_start, key_count):
    row_pos = row_start + jnp.arange(scores.shape[1], dtype=jnp.int32)
    col_pos = jnp.arange(key_count, dtype=jnp.int32)
    return jnp.where(col_pos[None, None, :] <= row_pos[None, :, None], scores, MASKED)


def attend_forward(query_rows, key_rows, value_rows, block_rows, score_scale):
    head_parts = []
    log_parts = []
    for row_start in range(0, query_rows.shape[0], block_rows):
        query_blk = query_rows[row_start : row_start + block_rows]
        scores = (
            jnp.einsum("qhd,khd->hqk", query_blk, key_rows, preferred_element_type=jnp.float32)
            * score_scale
        )
        scores = mask_scores(scores, row_start, key_rows.shape[0])
        row_max = jnp.max(scores, axis=-1, keepdims=True)
        exp_scores = jnp.exp(scores - row_max)
        row_total = jnp.sum(exp_scores, axis=-1, keepdims=True)
        probabilities = (exp_scores / row_total).astype(jnp.bfloat16)
        attended = jnp.einsum(
            "hqk,khd->qhd", probabilities, value_rows, preferred_element_type=jnp.float32
        )
        head_parts.append(attended.astype(jnp.bfloat16))
        log_parts.append(row_max + jnp.log(row_total))
    return (jnp.concatenate(head_parts, axis=0), jnp.concatenate(log_parts, axis=1))


def attend_backward(query_rows, key_rows, value_rows, log_total, d_heads, block_rows, score_scale):
    query_parts = []
    d_keys = jnp.zeros(key_rows.shape, jnp.float32)
    d_values = jnp.zeros(value_rows.shape, jnp.float32)
    for row_start in range(0, query_rows.shape[0], block_rows):
        query_blk = query_rows[row_start : row_start + block_rows]
        grad_blk = d_heads[row_start : row_start + block_rows]
        scores = (
            jnp.einsum("qhd,khd->hqk", query_blk, key_rows, preferred_element_type=jnp.float32)
            * score_scale
        )
        scores = mask_scores(scores, row_start, key_rows.shape[0])
        probabilities = jnp.exp(scores - log_total[:, row_start : row_start + block_rows])
        low_probs = probabilities.astype(jnp.bfloat16)
        d_probs = jnp.einsum(
            "qhd,khd->hqk", grad_blk, value_rows, preferred_element_type=jnp.float32
        )
        inner = jnp.sum(probabilities * d_probs, axis=-1, keepdims=True)
        d_scores = (probabilities * (d_probs - inner)).astype(jnp.bfloat16)
        query_parts.append(
            jnp.einsum("hqk,khd->qhd", d_scores, key_rows, preferred_element_type=jnp.float32)
            * score_scale
        )
        d_keys = (
            d_keys
            + jnp.einsum("hqk,qhd->khd", d_scores, query_blk, preferred_element_type=jnp.float32)
            * score_scale
        )
        d_values = d_values + jnp.einsum(
            "hqk,qhd->khd", low_probs, grad_blk, preferred_element_type=jnp.float32
        )
    return (jnp.concatenate(query_parts, axis=0), d_keys, d_values)


def low(value):
    return value.astype(jnp.bfloat16)


def gather_small(parts):
    flat = jnp.concatenate([part.reshape(-1) for part in parts])
    every = lax.all_gather(flat, "dp", axis=0, tiled=False)
    out = []
    start = 0
    for part in parts:
        out.append(every[:, start : start + part.size])
        start += part.size
    return out


def body(
    hidden_in,
    triple_projection_weight,
    triple_projection_bias,
    attention_out_weight,
    b_dense,
    feedforward_in_weight,
    feedforward_in_bias,
    feedforward_out_weight,
    b_fc2,
    ln1_gain,
    ln1_bias,
    ln2_gain,
    ln2_bias,
    grad_out,
):
    seq_count, piece_len, hidden_width = hidden_in.shape
    tp_count = lax.axis_size("tp")
    dp_count = lax.axis_size("dp")
    length = piece_len * tp_count
    local_heads = triple_projection_weight.shape[2] // HD
    block_rows = min(512, length)
    score_scale = HD ** (-0.5)
    cosine, sine_tab = rotary_tables(length, ROT)
    small = gather_small(
        [
            triple_projection_bias,
            feedforward_in_bias,
            b_dense,
            b_fc2,
            ln1_gain,
            ln1_bias,
            ln2_gain,
            ln2_bias,
        ]
    )
    full_bqkv = small[0].T.reshape(-1).astype(jnp.float32)
    full_bfc1 = small[1].T.reshape(-1).astype(jnp.float32)
    full_bdense, full_bfc2, gain_one, shift_one, gain_two, shift_two = [
        part.reshape(-1).astype(jnp.float32) for part in small[2:]
    ]
    x_seq = lax.all_gather(hidden_in, "tp", axis=1, tiled=True)[0]
    full_qkv = lax.all_gather(triple_projection_weight, "dp", axis=0, tiled=True)
    full_qkv = full_qkv.reshape(hidden_width, -1)
    full_fc1 = lax.all_gather(feedforward_in_weight, "dp", axis=0, tiled=True)
    full_dense = lax.all_gather(attention_out_weight, "dp", axis=1, tiled=True)
    full_fc2 = lax.all_gather(feedforward_out_weight, "dp", axis=1, tiled=True)
    cot_seq = lax.all_gather(grad_out, "tp", axis=1, tiled=True)[0]

    x_f32 = x_seq.astype(jnp.float32)
    mean = jnp.mean(x_f32, axis=-1, keepdims=True)
    centered = x_f32 - mean
    rstd = lax.rsqrt(jnp.mean(centered * centered, axis=-1, keepdims=True) + EPSILON)
    xhat = centered * rstd
    attention_norm = low(xhat * gain_one + shift_one)
    feedforward_norm = low(xhat * gain_two + shift_two)

    triple_linear = (
        jnp.dot(attention_norm, full_qkv, preferred_element_type=jnp.float32) + full_bqkv
    )
    triple_linear = triple_linear.reshape(length, 3, local_heads, HD)
    query_rows = low(rotate(triple_linear[:, 0], cosine, sine_tab))
    key_rows = low(rotate(triple_linear[:, 1], cosine, sine_tab))
    value_rows = low(triple_linear[:, 2])
    head_output_rows, log_total = attend_forward(
        query_rows, key_rows, value_rows, block_rows, score_scale
    )
    heads_flat = head_output_rows.reshape(length, -1)
    feedforward_entry = (
        jnp.dot(feedforward_norm, full_fc1, preferred_element_type=jnp.float32) + full_bfc1
    )
    activation_result = low(gelu_exact(feedforward_entry))
    partial_value = jnp.dot(heads_flat, full_dense, preferred_element_type=jnp.float32)
    partial_value = partial_value + jnp.dot(
        activation_result, full_fc2, preferred_element_type=jnp.float32
    )
    summed = lax.psum_scatter(low(partial_value), "tp", scatter_dimension=0, tiled=True)
    layer_out = (
        hidden_in[0].astype(jnp.float32) + summed.astype(jnp.float32) + full_bdense + full_bfc2
    )
    hidden_out = low(layer_out)[None]

    d_heads = low(
        jnp.einsum("ld,jd->lj", cot_seq, full_dense, preferred_element_type=jnp.float32)
    )
    d_act = jnp.einsum("ld,fd->lf", cot_seq, full_fc2, preferred_element_type=jnp.float32)
    _, gelu_pull = jax.vjp(gelu_exact, feedforward_entry)
    d_fc = low(gelu_pull(d_act)[0])
    d_norm_two = jnp.einsum("lf,df->ld", d_fc, full_fc1, preferred_element_type=jnp.float32)
    d_query, d_keys, d_values = attend_backward(
        query_rows,
        key_rows,
        value_rows,
        log_total,
        d_heads.reshape(length, local_heads, HD),
        block_rows,
        score_scale,
    )
    d_qkv = jnp.stack(
        [rotate_back(d_query, cosine, sine_tab), rotate_back(d_keys, cosine, sine_tab), d_values],
        axis=1,
    )
    d_qkv = low(d_qkv).reshape(length, -1)
    d_norm_one = jnp.einsum("lj,dj->ld", d_qkv, full_qkv, preferred_element_type=jnp.float32)
    e_sum = low(d_norm_one * gain_one + d_norm_two * gain_two)
    ln_sums = jnp.stack(
        [
            jnp.sum(d_norm_one * xhat, axis=0),
            jnp.sum(d_norm_one, axis=0),
            jnp.sum(d_norm_two * xhat, axis=0),
            jnp.sum(d_norm_two, axis=0),
        ]
    )
    e_piece = lax.psum_scatter(e_sum, "tp", scatter_dimension=0, tiled=True).astype(jnp.float32)

    sum_fc2 = low(
        jnp.einsum("lf,ld->fd", activation_result, cot_seq, preferred_element_type=jnp.float32)
    )
    sum_dense = low(
        jnp.einsum("lj,ld->jd", heads_flat, cot_seq, preferred_element_type=jnp.float32)
    )
    sum_fc1 = low(
        jnp.einsum("ld,lf->df", feedforward_norm, d_fc, preferred_element_type=jnp.float32)
    )
    sum_wqkv = low(
        jnp.einsum("ld,lj->dj", attention_norm, d_qkv, preferred_element_type=jnp.float32)
    )
    own_fc2 = lax.psum_scatter(sum_fc2, "dp", scatter_dimension=1, tiled=True)
    own_dense = lax.psum_scatter(sum_dense, "dp", scatter_dimension=1, tiled=True)
    own_fc1 = lax.psum_scatter(sum_fc1, "dp", scatter_dimension=0, tiled=True)
    own_wqkv = lax.psum_scatter(
        sum_wqkv.reshape(hidden_width, 3, -1), "dp", scatter_dimension=0, tiled=True
    )

    cot_piece = grad_out[0].astype(jnp.float32)
    x_own = hidden_in[0].astype(jnp.float32)
    own_mean = jnp.mean(x_own, axis=-1, keepdims=True)
    own_centered = x_own - own_mean
    own_rstd = lax.rsqrt(
        jnp.mean(own_centered * own_centered, axis=-1, keepdims=True) + EPSILON
    )
    own_xhat = own_centered * own_rstd
    back = (
        e_piece
        - jnp.mean(e_piece, axis=-1, keepdims=True)
        - own_xhat * jnp.mean(e_piece * own_xhat, axis=-1, keepdims=True)
    ) * own_rstd
    grad_in = (cot_piece + back)[None]

    me = lax.axis_index("dp")
    sum_bias_out = jnp.sum(cot_piece, axis=0)
    shared = jnp.concatenate([ln_sums.reshape(-1), sum_bias_out])
    shared = lax.psum(shared, ("dp", "tp")).reshape(5, dp_count, -1)
    shared = lax.dynamic_index_in_dim(shared, me, axis=1, keepdims=False)
    sum_bqkv = jnp.sum(d_qkv.astype(jnp.float32), axis=0)
    sum_bfc1 = jnp.sum(d_fc.astype(jnp.float32), axis=0)
    split = sum_bqkv.size
    mine = lax.psum(jnp.concatenate([sum_bqkv, sum_bfc1]), "dp").reshape(-1, dp_count)
    mine = lax.dynamic_index_in_dim(mine, me, axis=1, keepdims=True)
    own_bqkv = mine[: split // dp_count].reshape(3, -1, 1)
    own_bfc1 = mine[split // dp_count :]
    wide = jnp.float32
    return (
        hidden_out,
        grad_in,
        own_wqkv.astype(wide),
        own_bqkv,
        own_dense.astype(wide),
        shared[4],
        own_fc1.astype(wide),
        own_bfc1,
        own_fc2.astype(wide),
        shared[4],
        shared[0],
        shared[1],
        shared[2],
        shared[3],
    )


def solution(mesh):
    return jax.shard_map(
        body,
        mesh=mesh,
        in_specs=(
            P("dp", "tp", None),
            P("dp", None, "tp"),
            P(None, "tp", "dp"),
            P("tp", "dp"),
            P("dp"),
            P("dp", "tp"),
            P("tp", "dp"),
            P("tp", "dp"),
            P("dp"),
            P("dp"),
            P("dp"),
            P("dp"),
            P("dp"),
            P("dp", "tp", None),
        ),
        out_specs=(
            P("dp", "tp", None),
            P("dp", "tp", None),
            P("dp", None, "tp"),
            P(None, "tp", "dp"),
            P("tp", "dp"),
            P("dp"),
            P("dp", "tp"),
            P("tp", "dp"),
            P("tp", "dp"),
            P("dp"),
            P("dp"),
            P("dp"),
            P("dp"),
            P("dp"),
        ),
        check_vma=False,
    )
```

time: 1910 us -> 1190 us (0.62)
  waiting for transfers between devices: 1220 us -> 492 us
  blocking collectives: 115 us -> 93.9 us
    reduce_scatter x5 -> x4, waiting for transfers between devices: 816 us -> 214 us  [the longest x1 144 us: body(): lax.psum_scatter(low(partial_value), 'tp', scatter_dimension=0, tiled=True)]
    reduce_scatter x1, waiting for transfers between devices: 96.4 us -> 0.01 us  [body(): lax.psum_scatter(sum_wqkv.reshape(hidden_width, 3, -1), 'dp', scatter_dim...]
    all_gather x8 -> x0, blocking collectives: 70.6 us -> none  [the longest x1 10.3 us: body(): lax.all_gather(ln2_bias, 'dp', axis=0, tiled=True)]
    psum x1 -> x2, blocking collectives: 19.5 us -> 67.6 us  [the longest x1 41.5 us: body(): shared = lax.psum(shared, ('dp', 'tp')).reshape(5, dp_count, -1)]
    reduce_scatter x1, waiting for transfers between devices: 47.6 us -> 0.01 us  [body(): lax.psum_scatter(sum_dense, 'dp', scatter_dimension=1, tiled=True)]
    all_gather x1, waiting for transfers between devices: 0.01 us -> 39.3 us  [body(): lax.all_gather(triple_projection_weight, 'dp', axis=0, tiled=True)]
    all_gather x6 -> x5, waiting for transfers between devices: 262 us -> 236 us  [the longest x1 127 us: body(): cot_seq = lax.all_gather(grad_out, 'tp', axis=1, tiled=True)[0]]
    unnamed x186 -> x169, local copies, waits for them, and re-layouts: 40.7 us -> 35.6 us
  transfers between devices with their start and end apart: 14 -> 12, of which waited for: 10 -> 5; matrix products, arithmetic and copies ran while one was open for 28% -> 47% of each run, Pallas kernels for 0% -> 0%
where the time goes in v1:
time: 1190 us; the launch traced here: 1180 us
  waiting for transfers between devices  492 us (41%)
  matrix products  374 us (31%)
  other arithmetic  123 us (10%)
  blocking collectives  93.9 us (8%)
  local copies, waits for them, and re-layouts  77.4 us (7%)
  between operations  15.9 us (1%)
    reduce_scatter x1, waiting for transfers between devices, body(): lax.psum_scatter(low(partial_value), 'tp', scatter_dimension=0, tiled=True)  144 us
    all_gather x1, waiting for transfers between devices, body(): cot_seq = lax.all_gather(grad_out, 'tp', axis=1, tiled=True)[0]  127 us
    all_gather x1, waiting for transfers between devices, body(): x_seq = lax.all_gather(hidden_in, 'tp', axis=1, tiled=True)[0]  108 us
    reduce_scatter x1, waiting for transfers between devices, body(): lax.psum_scatter(e_sum, 'tp', scatter_dimension=0, tiled=True)  69.4 us
    psum x1, blocking collectives, body(): shared = lax.psum(shared, ('dp', 'tp')).reshape(5, dp_count, -1)  41.5 us
    all_gather x1, waiting for transfers between devices, body(): lax.all_gather(triple_projection_weight, 'dp', axis=0, tiled=True)  39.3 us
    unnamed x169, local copies, waits for them, and re-layouts  35.6 us
    dot_general x1, matrix products, body(): jnp.einsum('ld,fd->lf', cot_seq, full_fc2, preferred_element_type=jnp.flo...  32.4 us
  transfers between devices with their start and end apart: 12, of which 5 were waited for; matrix products, arithmetic and copies ran while one was open for 47% of the time, Pallas kernels for 0%

profile of v1, /device:TPU:0, one launch (start us, length us, event | category | flops | bytes accessed | tf_op | source)
XLA Modules:
  0.0 1176.7 jit_solution(18108985562183337736)
XLA Ops:
  14.8 26.3 %all-reduce = bf16[15872]{0:T(1024)(128)(2,1)S(1)} all-reduce(bf16[15872]{0:T(1024)(128)(2,1)S(1)} %dynamic-update-slice), channel_id=2, replica_groups=mesh['dp'=8,'tp'=4] {'dp'}, use_global_device_ids=true, to_apply=%add | all-reduce | flops 15872 | bytes 63488
  53.6 108.4 %all-gather.8.cloned.1.call-done = bf16[1,2048,2048]{2,1,0:T(8,128)(2,1)} async-done(((bf16[1,512,2048]{2,1,0:T(8,128)(2,1)}), bf16[1,2048,2048]{2,1,0:T(8,128)(2,1)}) %all-gather.8.cloned.1.call-update) | async-done | bytes 8388624 | tf_op jit(solution)/shard_map/all_gather | solution.py:179
  170.2 39.3 %all-gather.10.cloned.1.call-done = bf16[2048,3,512]{0,2,1:T(8,128)(2,1)} async-done(((bf16[256,3,512]{0,2,1:T(8,128)(2,1)}), bf16[2048,3,512]{0,2,1:T(8,128)(2,1)}) %all-gather.10.cloned.1.call-update) | async-done | bytes 6291472 | tf_op jit(solution)/shard_map/all_gather | solution.py:180
  209.4 19.0 %convolution_add_fusion = f32[2048,1536]{0,1:T(8,128)S(1)} fusion(bf16[2048,1536]{0,1:T(8,128)(2,1)} %bitcast.278, f32[1536]{0:T(1024)S(1)} %reshape.433, bf16[1,2048,2048]{2,1,0:T(8,128)(2,1)} %all-gather.8.cloned.1.call-done, f32[2048]{0:T(1024)S(1)} %bitcast.259, f32[2048]{0:T(1024)S(1)} %bitcast.256, f32[2048]{0:T(1024)S(1)} %add_rsqrt_fusion, ...), kind=kOutput, calls=%fused_computation.25 | convolution fusion | flops 12913213440 | bytes 27301888 | tf_op jit(solution)/shard_map/dot_general | solution.py:196
  263.4 127.2 %all-gather.18.cloned.1.call-done = bf16[1,2048,2048]{2,1,0:T(8,128)(2,1)} async-done(((bf16[1,512,2048]{2,1,0:T(8,128)(2,1)}), bf16[1,2048,2048]{2,1,0:T(8,128)(2,1)}) %all-gather.18.cloned.1.call-update) | async-done | bytes 8388624 | tf_op jit(solution)/shard_map/all_gather | solution.py:185
  390.6 8.7 fusion.67
  429.2 8.3 multiply_reduce_fusion.3
  456.1 9.0 multiply_convert_fusion.3
  528.8 9.9 multiply_bitcast_fusion
  618.7 8.7 copy.127
  627.5 20.0 %convolution_convert_fusion = bf16[2048,1536]{0,1:T(8,128)(2,1)} fusion(bf16[2048,1536]{0,1:T(8,128)(2,1)} %bitcast.240, bf16[1,2048,2048]{2,1,0:T(8,128)(2,1)} %all-gather.8.cloned.1.call-done, f32[2048]{0:T(1024)S(1)} %bitcast.260, f32[2048]{0:T(1024)S(1)} %bitcast.257, f32[2048]{0:T(1024)S(1)} %copy-done.55, f32[2048]{0:T(1024)S(1)} %copy-done.49), kind=kOutput, calls=%fused_computation.60 | convolution fusion | flops 12913213440 | bytes 21004288 | tf_op jit(solution)/shard_map/ld,lj->dj/dot_general | solution.py:263
  647.5 8.6 copy.128
  657.1 26.9 %multiply_convert_fusion = (bf16[2048,2048]{1,0:T(8,128)(2,1)S(1)}, f32[2048,2048]{1,0:T(8,128)}) fusion(f32[2048]{0:T(1024)S(1)} %reshape.436, bf16[2048,2048]{1,0:T(8,128)(2,1)} %all-gather.14.cloned.1.call-done, bf16[1,2048,2048]{2,1,0:T(8,128)(2,1)} %all-gather.8.cloned.1.call-done, f32[2048]{0:T(1024)S(1)} %bitcast.264, f32[2048]{0:T(1024)S(1)} %bitcast.261, ...), kind=kOutput, calls=%fused_computation.22 | convolution fusion | flops 17230200832 | bytes 41984000 | tf_op jit(solution)/shard_map/dot_general | solution.py:207
  687.3 21.4 %fusion.26 = bf16[2048,2048]{1,0:T(8,128)(2,1)} fusion(bf16[2048,2048]{1,0:T(8,128)(2,1)S(1)} %get-tuple-element.105, bf16[1,2048,2048]{2,1,0:T(8,128)(2,1)} %all-gather.18.cloned.1.call-done), kind=kOutput, calls=%fused_computation.59 | convolution fusion | flops 17184063488 | bytes 25165824 | tf_op jit(solution)/shard_map/lf,ld->fd/dot_general | solution.py:254
  708.8 32.4 %convert_reduce_fusion.1 = (f32[2048]{0:T(1024)}, bf16[2048,2048]{1,0:T(8,128)(2,1)S(1)}) fusion(bf16[2048,2048]{1,0:T(8,128)(2,1)} %all-gather.16.cloned.1.call-done, bf16[1,2048,2048]{2,1,0:T(8,128)(2,1)} %all-gather.18.cloned.1.call-done, f32[2048,2048]{1,0:T(8,128)} %get-tuple-element.106, f32[2048]{0:T(1024)S(1)} %reshape.436), kind=kOutput, calls=%fused_computation.18 | convolution fusion | flops 17246976000 | bytes 41959424 | tf_op jit(solution)/shard_map/ld,fd->lf/dot_general | solution.py:223
  744.4 24.0 %convolution_convert_fusion.1 = bf16[2048,2048]{1,0:T(8,128)(2,1)} fusion(bf16[2048,2048]{1,0:T(8,128)(2,1)S(1)} %get-tuple-element.108, bf16[1,2048,2048]{2,1,0:T(8,128)(2,1)} %all-gather.8.cloned.1.call-done, f32[2048]{0:T(1024)S(1)} %bitcast.265, f32[2048]{0:T(1024)S(1)} %bitcast.262, f32[2048]{0:T(1024)S(1)} %copy-done.55, f32[2048]{0:T(1024)S(1)} %copy-done.49), kind=kOutput, calls=%fused_computation.61 | convolution fusion | flops 17209229312 | bytes 25198592 | tf_op jit(solution)/shard_map/ld,lf->df/dot_general | solution.py:260
  768.6 24.8 %fusion.134 = f32[2048,2048]{1,0:T(8,128)} fusion(bf16[2048,2048]{1,0:T(8,128)(2,1)} %copy-done.70, bf16[2048,2048]{1,0:T(8,128)(2,1)} %all-gather.14.cloned.1.call-done), kind=kOutput, calls=%fused_computation.217 | convolution fusion | flops 17179869184 | bytes 33554432 | tf_op jit(solution)/shard_map/lf,df->ld/dot_general | solution.py:226
  793.4 30.3 %fusion.12 = (f32[2048]{0:T(1024)S(1)}, f32[2048]{0:T(1024)S(1)}, f32[2048]{0:T(1024)S(1)}, f32[2048]{0:T(1024)S(1)}, bf16[2048,2048]{1,0:T(8,128)(2,1)}) fusion(bf16[1,2048,2048]{2,1,0:T(8,128)(2,1)} %all-gather.8.cloned.1.call-done, f32[2048]{0:T(1024)S(1)} %copy-done.55, f32[2048]{0:T(1024)S(1)} %copy-done.49, f32[2048,2048]{1,0:T(8,128)} %fusion.134, ...), kind=kOutput, calls=%fused_computation.15 | convolution fusion | flops 12939419648 | bytes 46202880 | tf_op jit(solution)/shard_map/lj,dj->ld/dot_general | solution.py:241
  825.2 10.4 fusion.133
  835.6 25.6 %add_convert_fusion.2 = bf16[2048,2048]{1,0:T(8,128)(2,1)} fusion(f32[2048,2048]{1,0:T(8,128)} %fusion.133, bf16[2048,2048]{1,0:T(8,128)(2,1)} %copy-done.69, bf16[2048,2048]{1,0:T(8,128)(2,1)} %all-gather.16.cloned.1.call-done), kind=kOutput, calls=%fused_computation.21 | convolution fusion | flops 17188257792 | bytes 41943040 | tf_op jit(solution)/shard_map/dot_general | solution.py:211
  866.2 26.1 %psum.14 = f32[448,8]{1,0:T(8,128)S(1)} all-reduce(f32[448,8]{1,0:T(8,128)S(1)} %reshape.427), channel_id=1, replica_groups=mesh['dp'=8,'tp'=4] {'dp'}, use_global_device_ids=true, to_apply=%region_23.24 | all-reduce | flops 3584 | bytes 28672 | tf_op jit(solution)/shard_map/psum | solution.py:295
  894.0 41.5 %psum.15 = f32[5,8,256]{2,1,0:T(8,128)S(1)} all-reduce(f32[5,8,256]{2,1,0:T(8,128)S(1)} %reshape.430), channel_id=1, replica_groups=mesh['dp'=8,'tp'=4] {'dp','tp'}, use_global_device_ids=true, to_apply=%region_30.31 | all-reduce | flops 10240 | bytes 81920 | tf_op jit(solution)/shard_map/psum | solution.py:290
  945.9 69.4 %reduce-scatter.9.cloned.1.call-done = bf16[512,2048]{1,0:T(8,128)(2,1)} async-done(((bf16[2048,2048]{1,0:T(8,128)(2,1)}), bf16[512,2048]{1,0:T(8,128)(2,1)}) %reduce-scatter.9.cloned.1.call-update) | async-done | bytes 2097168 | tf_op jit(solution)/shard_map/reduce_scatter | solution.py:251
  1018.6 144.2 %reduce-scatter.7.cloned.1.call-done = bf16[512,2048]{1,0:T(8,128)(2,1)} async-done(((bf16[2048,2048]{1,0:T(8,128)(2,1)}), bf16[512,2048]{1,0:T(8,128)(2,1)}) %reduce-scatter.7.cloned.1.call-update) | async-done | bytes 2097168 | tf_op jit(solution)/shard_map/reduce_scatter | solution.py:214
  (303 shorter events, 290.3 us)
Async XLA Ops:
  7.3 154.8 %all-gather.8.cloned.1.call-start = ((), (), s32[]{:S(2)}) async-start(), calls=%async_computation.6 | async-start | bytes 10485760 | tf_op jit(solution)/shard_map/all_gather | solution.py:179
  8.0 201.4 %all-gather.10.cloned.1.call-start = ((), (), s32[]{:S(2)}) async-start(), calls=%async_computation.7 | async-start | bytes 7077888 | tf_op jit(solution)/shard_map/all_gather | solution.py:180
  10.4 253.1 %all-gather.12.cloned.1.call-start = ((), (), s32[]{:S(2)}) async-start(), calls=%async_computation.8 | async-start | bytes 2359296 | tf_op jit(solution)/shard_map/all_gather | solution.py:183
  11.1 379.5 %all-gather.18.cloned.1.call-start = ((), (), s32[]{:S(2)}) async-start(), calls=%async_computation.12 | async-start | bytes 10485760 | tf_op jit(solution)/shard_map/all_gather | solution.py:185
  11.7 645.5 %all-gather.14.cloned.1.call-start = ((), (), s32[]{:S(2)}) async-start(), calls=%async_computation.9 | async-start | bytes 9437184 | tf_op jit(solution)/shard_map/all_gather | solution.py:182
  12.3 696.5 %all-gather.16.cloned.1.call-start = ((), (), s32[]{:S(2)}) async-start(), calls=%async_computation.10 | async-start | bytes 9437184 | tf_op jit(solution)/shard_map/all_gather | solution.py:184
  12.8 923.2 %reduce-scatter.13.cloned.1.call-start = ((), (), s32[]{:S(2)}) async-start(), calls=%async_computation.15 | async-start | bytes 2359296 | tf_op jit(solution)/shard_map/reduce_scatter | solution.py:266
  43.4 166.0 %copy-start.56 = (f32[1,2,8,128]{3,1,2,0:T(2,128)}, f32[1,2,8,128]{3,1,2,0:T(2,128)S(1)}, u32[]{:S(2)}) copy-start(f32[1,2,8,128]{3,1,2,0:T(2,128)S(1)} %copy.162) | copy-start | bytes 24580
  43.4 166.0 %copy-start.51 = (f32[1,2,8,128]{3,1,2,0:T(2,128)}, f32[1,2,8,128]{3,1,2,0:T(2,128)S(1)}, u32[]{:S(2)}) copy-start(f32[1,2,8,128]{3,1,2,0:T(2,128)S(1)} %copy.161) | copy-start | bytes 24580
  53.6 347.0 %copy-start.19 = (f32[2048,64]{1,0:T(8,128)}, f32[2048,64]{1,0:T(8,128)S(1)}, u32[]{:S(2)}) copy-start(f32[2048,64]{1,0:T(8,128)S(1)} %get-tuple-element.76) | copy-start | bytes 1572868
  167.8 60.7 %copy-start.48 = (f32[2048]{0:T(1024)}, f32[2048]{0:T(1024)S(1)}, u32[]{:S(2)}) copy-start(f32[2048]{0:T(1024)S(1)} %broadcast_multiply_fusion) | copy-start | bytes 24580
  170.2 58.3 %copy-start.54 = (f32[2048]{0:T(1024)}, f32[2048]{0:T(1024)S(1)}, u32[]{:S(2)}) copy-start(f32[2048]{0:T(1024)S(1)} %add_rsqrt_fusion) | copy-start | bytes 24580
  255.9 156.2 %copy-start.3 = (bf16[2048,2,192]{2,0,1:T(8,128)(2,1)}, bf16[2048,2,192]{2,0,1:T(8,128)(2,1)S(1)}, u32[]{:S(2)}) copy-start(bf16[2048,2,192]{2,0,1:T(8,128)(2,1)S(1)} %slice.306) | copy-start | bytes 4718596
  427.8 130.6 %copy-start = (f32[2,512,2048]{2,1,0:T(8,128)}, f32[2,512,2048]{2,1,0:T(8,128)S(1)}, u32[]{:S(2)}) copy-start(f32[2,512,2048]{2,1,0:T(8,128)S(1)} %get-tuple-element.96) | copy-start | bytes 25165828
  564.7 18.3 %copy-start.34 = (bf16[2048,2,256]{0,2,1:T(8,128)(2,1)}, bf16[2048,2,256]{0,2,1:T(8,128)(2,1)S(1)}, u32[]{:S(2)}) copy-start(bf16[2048,2,256]{0,2,1:T(8,128)(2,1)S(1)} %pad_maximum_fusion.3) | copy-start | bytes 6291460
  589.8 348.1 %reduce-scatter.11.cloned.1.call-start = ((), (), s32[]{:S(2)}) async-start(), calls=%async_computation.14 | async-start | bytes 7077888 | tf_op jit(solution)/shard_map/reduce_scatter | solution.py:268
  589.9 15.6 %slice-start = ((s8[8388608]{0:T(1024)(128)(4,1)}), s8[4194304]{0:T(1024)(128)(4,1)S(1)}, s32[]{:S(2)}) async-start(s8[8388608]{0:T(1024)(128)(4,1)} %bitcast.221), calls=%async_computation.18 | async-start | bytes 8388608
  589.9 15.5 %slice-start.1 = ((s8[8388608]{0:T(1024)(128)(4,1)}), s8[4194304]{0:T(1024)(128)(4,1)S(1)}, s32[]{:S(2)}) async-start(s8[8388608]{0:T(1024)(128)(4,1)} %bitcast.221), calls=%async_computation.19 | async-start | bytes 8388608
  656.2 284.2 %reduce-scatter.17.cloned.1.call-start = ((), (), s32[]{:S(2)}) async-start(), calls=%async_computation.17 | async-start | bytes 9437184 | tf_op jit(solution)/shard_map/reduce_scatter | solution.py:265
  708.7 234.4 %reduce-scatter.15.cloned.1.call-start = ((), (), s32[]{:S(2)}) async-start(), calls=%async_computation.16 | async-start | bytes 9437184 | tf_op jit(solution)/shard_map/reduce_scatter | solution.py:267
  768.5 24.8 %copy-start.53 = (f32[1,2,8,128]{3,1,2,0:T(2,128)S(1)}, f32[1,2,8,128]{3,1,2,0:T(2,128)}, u32[]{:S(2)}) copy-start(f32[1,2,8,128]{3,1,2,0:T(2,128)} %copy-done.51) | copy-start | bytes 24580
  768.5 246.8 %reduce-scatter.9.cloned.1.call-start = ((), (), s32[]{:S(2)}) async-start(), calls=%async_computation.13 | async-start | bytes 10485760 | tf_op jit(solution)/shard_map/reduce_scatter | solution.py:251
  823.7 339.1 %reduce-scatter.7.cloned.1.call-start = ((), (), s32[]{:S(2)}) async-start(), calls=%async_computation.11 | async-start | bytes 10485760 | tf_op jit(solution)/shard_map/reduce_scatter | solution.py:214
  936.1 233.1 %copy-start.59 = (f32[1,1,256]{2,1,0:T(1,128)}, f32[1,1,256]{2,1,0:T(1,128)S(1)}, u32[]{:S(2)}) copy-start(f32[1,1,256]{2,1,0:T(1,128)S(1)} %get-tuple-element.81) | copy-start | bytes 3076
  (65 other events, 344.6 us)
Sparse Core Ops, SparseCore 0:
  9.7 152.3 all-gather.7
  164.5 44.8 all-gather.9
  211.3 28.1 all-gather.11
  241.0 149.6 all-gather.17
  392.4 52.6 all-gather.13
  446.7 55.9 all-gather.15
  589.9 40.8 reduce-scatter.12
  656.3 61.3 reduce-scatter.10
  721.1 71.2 reduce-scatter.16
  796.1 71.2 reduce-scatter.14
  869.8 145.4 reduce-scatter.8
  1017.5 145.1 reduce-scatter.6

commit v2 on v1

v2 whole, which is shorter than its diff:
```python
import functools
import math

import jax
import jax.numpy as jnp
import numpy as np
from jax import lax
from jax.experimental import pallas as pl
from jax.experimental.pallas import tpu as pltpu
from jax.sharding import PartitionSpec as P

MESH = pl.DeviceIdType.MESH
EPSILON = 1e-05
MASKED = -1e30
HD = 256
ROT = 64
VMEM_LIMIT = 60 * 1024 * 1024
LOG2E = 1.4426950408889634


def low(value):
    return value.astype(jnp.bfloat16)


def dot_nn(a, b):
    return lax.dot_general(a, b, (((1,), (0,)), ((), ())), preferred_element_type=jnp.float32)


def dot_nt(a, b):
    return lax.dot_general(a, b, (((1,), (1,)), ((), ())), preferred_element_type=jnp.float32)


def dot_tn(a, b):
    return lax.dot_general(a, b, (((0,), (0,)), ((), ())), preferred_element_type=jnp.float32)


def rotary_tables(length):
    half = ROT // 2
    exponent = np.arange(half, dtype=np.float32) * np.float32(2.0 / ROT)
    inverse = np.exp(exponent * np.float32(-math.log(10000.0)), dtype=np.float32)
    angle = np.arange(length, dtype=np.float32)[:, None] * inverse[None, :]
    cosine = np.ones((length, 128), np.float32)
    sine = np.zeros((length, 128), np.float32)
    cosine[:, :half] = cosine[:, half:ROT] = np.cos(angle)
    sine[:, :half] = -np.sin(angle)
    sine[:, half:ROT] = np.sin(angle)
    return jnp.asarray(cosine), jnp.asarray(sine)


def turned(part):
    half = ROT // 2
    lane = lax.broadcasted_iota(jnp.int32, part.shape, 1)
    return jnp.where(
        lane < half, pltpu.roll(part, 128 - half, 1), pltpu.roll(part, half, 1)
    )


def front_kernel(
    heads, x_ref, gains_ref, wq_ref, bq_ref, w1_ref, b1_ref, cos_ref, sin_ref,
    n1_ref, n2_ref, q_ref, k_ref, v_ref, act_ref, slope_ref, stat_ref,
):
    x = x_ref[...].astype(jnp.float32)
    mean = jnp.mean(x, axis=1, keepdims=True)
    centered = x - mean
    rstd = lax.rsqrt(jnp.mean(centered * centered, axis=1, keepdims=True) + EPSILON)
    xhat = centered * rstd
    n1_ref[...] = low(xhat * gains_ref[0:1] + gains_ref[1:2])
    n2_ref[...] = low(xhat * gains_ref[2:3] + gains_ref[3:4])
    lane = lax.broadcasted_iota(jnp.int32, stat_ref.shape, 1)
    stat_ref[...] = jnp.where(lane == 0, mean, rstd)
    width = heads * HD
    cosine, sine = cos_ref[...], sin_ref[...]
    for which, out in enumerate((q_ref, k_ref, v_ref)):
        for head in range(heads):
            at = which * width + head * HD
            raw = dot_nn(n1_ref[...], wq_ref[:, at : at + HD]) + bq_ref[:, at : at + HD]
            if which < 2:
                first = raw[:, :128]
                first = first * cosine + turned(first) * sine
                out[:, head * HD : head * HD + 128] = low(first)
                out[:, head * HD + 128 : (head + 1) * HD] = low(raw[:, 128:])
            else:
                out[:, head * HD : (head + 1) * HD] = low(raw)
    step = 256
    for at in range(0, w1_ref.shape[1], step):
        u = dot_nn(n2_ref[...], w1_ref[:, at : at + step]) + b1_ref[:, at : at + step]
        cdf = 0.5 * (1.0 + lax.erf(u * (1.0 / math.sqrt(2.0))))
        pdf = jnp.exp(-0.5 * u * u) * (1.0 / math.sqrt(2.0 * math.pi))
        act_ref[:, at : at + step] = low(u * cdf)
        slope_ref[:, at : at + step] = low(cdf + u * pdf)


def front(x, gains, wq, bq, w1, b1, cosine, sine, heads, rows=256):
    length, width = x.shape
    ff = w1.shape[1]
    qw = heads * HD
    bf = jnp.bfloat16
    whole = lambda *shape: pl.BlockSpec(shape, lambda i: (0,) * len(shape), pipeline_mode=pl.Buffered(1))
    row = lambda n: pl.BlockSpec((rows, n), lambda i: (i, 0))
    sds = lambda n, t: jax.ShapeDtypeStruct((length, n), t)
    return pl.pallas_call(
        functools.partial(front_kernel, heads),
        grid=(length // rows,),
        in_specs=[
            row(width), whole(*gains.shape), whole(*wq.shape), whole(*bq.shape),
            whole(*w1.shape), whole(*b1.shape), row(128), row(128),
        ],
        out_specs=[row(width), row(width), row(qw), row(qw), row(qw), row(ff), row(ff), row(128)],
        out_shape=[
            sds(width, bf), sds(width, bf), sds(qw, bf), sds(qw, bf), sds(qw, bf),
            sds(ff, bf), sds(ff, bf), sds(128, jnp.float32),
        ],
        compiler_params=pltpu.CompilerParams(vmem_limit_bytes=VMEM_LIMIT),
        cost_estimate=pl.CostEstimate(
            flops=2 * length * width * (3 * qw + ff), bytes_accessed=60_000_000,
            transcendentals=2 * length * ff),
        name="front",
    )(x, gains, wq, bq, w1, b1, cosine, sine)


def attend_kernel(heads, block, q_ref, k_ref, v_ref, o_ref, lse_ref):
    i = pl.program_id(0)
    scale = LOG2E * HD ** -0.5
    qs = [q_ref[:, h * HD : (h + 1) * HD] for h in range(heads)]

    def one(h, j, state, diagonal):
        top, total, acc = state
        rows = pl.ds(pl.multiple_of(j * block, block), block)
        key = k_ref[rows, h * HD : (h + 1) * HD]
        value = v_ref[rows, h * HD : (h + 1) * HD]
        s = dot_nt(key, qs[h]) * scale
        if diagonal:
            kp = lax.broadcasted_iota(jnp.int32, s.shape, 0)
            qp = lax.broadcasted_iota(jnp.int32, s.shape, 1)
            s = jnp.where(kp <= qp, s, MASKED)
        new_top = jnp.maximum(top, jnp.max(s, axis=0, keepdims=True))
        p = jnp.exp2(s - new_top)
        shrink = jnp.exp2(top - new_top)
        total = total * shrink + jnp.sum(p, axis=0, keepdims=True)
        acc = acc * shrink + dot_tn(value, low(p))
        return new_top, total, acc

    def start():
        return (
            jnp.full((1, block), MASKED, jnp.float32),
            jnp.zeros((1, block), jnp.float32),
            jnp.zeros((HD, block), jnp.float32),
        )

    def step(j, states):
        return tuple(one(h, j, states[h], False) for h in range(heads))

    states = lax.fori_loop(0, i, step, tuple(start() for _ in range(heads)))
    states = [one(h, i, states[h], True) for h in range(heads)]
    for h in range(heads):
        top, total, acc = states[h]
        o_ref[:, h * HD : (h + 1) * HD] = low((acc / total).T)
        lse_ref[h : h + 1, :] = top + jnp.log2(total)


def attend(q, k, v, heads, block=512):
    length, width = q.shape
    block = min(block, length)
    whole = pl.BlockSpec((length, width), lambda i: (0, 0), pipeline_mode=pl.Buffered(1))
    row = pl.BlockSpec((block, width), lambda i: (i, 0))
    return pl.pallas_call(
        functools.partial(attend_kernel, heads, block),
        grid=(length // block,),
        in_specs=[row, whole, whole],
        out_specs=[row, pl.BlockSpec((heads, block), lambda i: (0, i))],
        out_shape=[
            jax.ShapeDtypeStruct((length, width), jnp.bfloat16),
            jax.ShapeDtypeStruct((heads, length), jnp.float32),
        ],
        compiler_params=pltpu.CompilerParams(vmem_limit_bytes=VMEM_LIMIT),
        cost_estimate=pl.CostEstimate(
            flops=2 * length * length * width, bytes_accessed=8 * length * width,
            transcendentals=length * length * heads // 2),
        name="attend",
    )(q, k, v)


def attend_back_kernel(
    heads, block, q_ref, k_ref, v_ref, o_ref, do_ref, lse_ref, cos_ref, sin_ref,
    dqkv_ref, sums_ref, dq_acc, dk_acc, dv_acc, delta_ref,
):
    length = q_ref.shape[0]
    blocks = length // block
    scale = HD ** -0.5
    width = heads * HD
    for i in range(blocks):
        rows = slice(i * block, (i + 1) * block)
        for h in range(heads):
            cols = slice(h * HD, (h + 1) * HD)
            inner = jnp.sum(
                do_ref[rows, cols].astype(jnp.float32) * o_ref[rows, cols].astype(jnp.float32),
                axis=1, keepdims=True)
            delta_ref[h : h + 1, rows] = jnp.broadcast_to(inner, (block, 128)).T[0:1]
    dq_acc[...] = jnp.zeros_like(dq_acc)

    def one(h, i, j, diagonal):
        cols = slice(h * HD, (h + 1) * HD)
        qrows = pl.ds(pl.multiple_of(i * block, block), block)
        krows = pl.ds(pl.multiple_of(j * block, block), block)
        query, grad = q_ref[qrows, cols], do_ref[qrows, cols]
        key, value = k_ref[krows, cols], v_ref[krows, cols]
        s = dot_nt(key, query) * (scale * LOG2E)
        p = jnp.exp2(s - lse_ref[h : h + 1, qrows])
        if diagonal:
            kp = lax.broadcasted_iota(jnp.int32, s.shape, 0)
            qp = lax.broadcasted_iota(jnp.int32, s.shape, 1)
            p = jnp.where(kp <= qp, p, 0.0)
        dp = dot_nt(value, grad)
        ds = low(p * (dp - delta_ref[h : h + 1, qrows]))
        dv = dot_nn(low(p), grad)
        dk = dot_nn(ds, query)
        dq_acc[qrows, cols] += dot_tn(ds, key)
        if diagonal:
            dv_acc[krows, cols] = dv
            dk_acc[krows, cols] = dk
        else:
            dv_acc[krows, cols] += dv
            dk_acc[krows, cols] += dk

    def outer(j, carry):
        for h in range(heads):
            one(h, j, j, True)

        def inner(i, c):
            for h in range(heads):
                one(h, i, j, False)
            return c

        lax.fori_loop(j + 1, blocks, inner, 0)
        return carry

    lax.fori_loop(0, blocks, outer, 0)
    sums_ref[...] = jnp.zeros_like(sums_ref)

    def finish(i, carry):
        rows = pl.ds(pl.multiple_of(i * block, block), block)
        cosine, sine = cos_ref[rows, :], sin_ref[rows, :]
        for which, acc in enumerate((dq_acc, dk_acc, dv_acc)):
            for h in range(heads):
                at = which * width + h * HD
                g = acc[rows, h * HD : (h + 1) * HD]
                if which < 2:
                    g = g * scale
                    first = g[:, :128]
                    first = low(first * cosine - turned(first) * sine)
                    rest = low(g[:, 128:])
                    dqkv_ref[rows, at : at + 128] = first
                    dqkv_ref[rows, at + 128 : at + HD] = rest
                    sums_ref[:, at : at + 128] += jnp.sum(first.astype(jnp.float32), axis=0, keepdims=True)
                    sums_ref[:, at + 128 : at + HD] += jnp.sum(rest.astype(jnp.float32), axis=0, keepdims=True)
                else:
                    g = low(g)
                    dqkv_ref[rows, at : at + HD] = g
                    sums_ref[:, at : at + HD] += jnp.sum(g.astype(jnp.float32), axis=0, keepdims=True)
        return carry

    lax.fori_loop(0, blocks, finish, 0)


def attend_back(q, k, v, o, do, lse, cosine, sine, heads, block=512):
    length, width = q.shape
    block = min(block, length)
    vm = pl.BlockSpec(memory_space=pltpu.VMEM)
    f32 = jnp.float32
    return pl.pallas_call(
        functools.partial(attend_back_kernel, heads, block),
        in_specs=[vm] * 8,
        out_specs=[vm, vm],
        out_shape=[
            jax.ShapeDtypeStruct((length, 3 * width), jnp.bfloat16),
            jax.ShapeDtypeStruct((1, 3 * width), f32),
        ],
        scratch_shapes=[
            pltpu.VMEM((length, width), f32), pltpu.VMEM((length, width), f32),
            pltpu.VMEM((length, width), f32), pltpu.VMEM((heads, length), f32),
        ],
        compiler_params=pltpu.CompilerParams(vmem_limit_bytes=VMEM_LIMIT),
        cost_estimate=pl.CostEstimate(
            flops=5 * length * length * width, bytes_accessed=20 * length * width,
            transcendentals=length * length * heads // 2),
        name="attend_back",
    )(q, k, v, o, do, lse, cosine, sine)


def out_kernel(h_ref, a_ref, wd_ref, w2_ref, o_ref):
    step = 512
    for at in range(0, o_ref.shape[1], step):
        o_ref[:, at : at + step] = low(
            dot_nn(h_ref[...], wd_ref[:, at : at + step])
            + dot_nn(a_ref[...], w2_ref[:, at : at + step]))


def out_proj(h, a, wd, w2, rows=512):
    length = h.shape[0]
    width = wd.shape[1]
    whole = lambda w: pl.BlockSpec(w.shape, lambda i: (0, 0), pipeline_mode=pl.Buffered(1))
    row = lambda n: pl.BlockSpec((rows, n), lambda i: (i, 0))
    return pl.pallas_call(
        out_kernel,
        grid=(length // rows,),
        in_specs=[row(h.shape[1]), row(a.shape[1]), whole(wd), whole(w2)],
        out_specs=row(width),
        out_shape=jax.ShapeDtypeStruct((length, width), jnp.bfloat16),
        compiler_params=pltpu.CompilerParams(vmem_limit_bytes=VMEM_LIMIT),
        cost_estimate=pl.CostEstimate(
            flops=2 * length * width * (h.shape[1] + a.shape[1]), bytes_accessed=30_000_000,
            transcendentals=0),
        name="out_proj",
    )(h, a, wd, w2)


def back_in_kernel(c_ref, slope_ref, wd_ref, w2_ref, dh_ref, dfc_ref, sums_ref):
    @pl.when(pl.program_id(0) == 0)
    def _():
        sums_ref[...] = jnp.zeros_like(sums_ref)

    dh_ref[...] = low(dot_nt(c_ref[...], wd_ref[...]))
    step = 512
    for at in range(0, dfc_ref.shape[1], step):
        d = low(dot_nt(c_ref[...], w2_ref[at : at + step, :])
                * slope_ref[:, at : at + step].astype(jnp.float32))
        dfc_ref[:, at : at + step] = d
        sums_ref[:, at : at + step] += jnp.sum(d.astype(jnp.float32), axis=0, keepdims=True)


def back_in(cot, slope, wd, w2, rows=512):
    length, width = cot.shape
    qw, ff = wd.shape[0], w2.shape[0]
    whole = lambda w: pl.BlockSpec(w.shape, lambda i: (0, 0), pipeline_mode=pl.Buffered(1))
    row = lambda n: pl.BlockSpec((rows, n), lambda i: (i, 0))
    return pl.pallas_call(
        back_in_kernel,
        grid=(length // rows,),
        in_specs=[row(width), row(ff), whole(wd), whole(w2)],
        out_specs=[row(qw), row(ff), pl.BlockSpec((1, ff), lambda i: (0, 0))],
        out_shape=[
            jax.ShapeDtypeStruct((length, qw), jnp.bfloat16),
            jax.ShapeDtypeStruct((length, ff), jnp.bfloat16),
            jax.ShapeDtypeStruct((1, ff), jnp.float32),
        ],
        compiler_params=pltpu.CompilerParams(vmem_limit_bytes=VMEM_LIMIT),
        cost_estimate=pl.CostEstimate(
            flops=2 * length * width * (qw + ff), bytes_accessed=40_000_000, transcendentals=0),
        name="back_in",
    )(cot, slope, wd, w2)


def back_out_kernel(dqkv_ref, dfc_ref, x_ref, stat_ref, gains_ref, wq_ref, w1_ref, e_ref, sums_ref):
    @pl.when(pl.program_id(0) == 0)
    def _():
        sums_ref[...] = jnp.zeros_like(sums_ref)

    mean, rstd = stat_ref[:, 0:1], stat_ref[:, 1:2]
    step = 512
    for at in range(0, e_ref.shape[1], step):
        cols = slice(at, at + step)
        d1 = dot_nt(dqkv_ref[...], wq_ref[cols, :])
        d2 = dot_nt(dfc_ref[...], w1_ref[cols, :])
        xhat = (x_ref[:, cols].astype(jnp.float32) - mean) * rstd
        e_ref[:, cols] = low(d1 * gains_ref[0:1, cols] + d2 * gains_ref[2:3, cols])
        sums_ref[0:1, cols] += jnp.sum(d1 * xhat, axis=0, keepdims=True)
        sums_ref[1:2, cols] += jnp.sum(d1, axis=0, keepdims=True)
        sums_ref[2:3, cols] += jnp.sum(d2 * xhat, axis=0, keepdims=True)
        sums_ref[3:4, cols] += jnp.sum(d2, axis=0, keepdims=True)


def back_out(dqkv, dfc, x, stat, gains, wq, w1, rows=512):
    length, width = x.shape
    whole = lambda w: pl.BlockSpec(w.shape, lambda i: (0, 0), pipeline_mode=pl.Buffered(1))
    row = lambda n: pl.BlockSpec((rows, n), lambda i: (i, 0))
    return pl.pallas_call(
        back_out_kernel,
        grid=(length // rows,),
        in_specs=[row(dqkv.shape[1]), row(dfc.shape[1]), row(width), row(128), whole(gains), whole(wq), whole(w1)],
        out_specs=[row(width), pl.BlockSpec((4, width), lambda i: (0, 0))],
        out_shape=[
            jax.ShapeDtypeStruct((length, width), jnp.bfloat16),
            jax.ShapeDtypeStruct((4, width), jnp.float32),
        ],
        compiler_params=pltpu.CompilerParams(vmem_limit_bytes=VMEM_LIMIT),
        cost_estimate=pl.CostEstimate(
            flops=2 * length * width * (dqkv.shape[1] + dfc.shape[1]), bytes_accessed=50_000_000,
            transcendentals=0),
        name="back_out",
    )(dqkv, dfc, x, stat, gains, wq, w1)


def weight_grad_kernel(split, a_ref, b_ref, o_ref):
    if split == 1:
        o_ref[...] = low(dot_tn(a_ref[...], b_ref[...]))
        return
    cols = o_ref.shape[2]
    for shard in range(split):
        o_ref[shard] = low(dot_tn(a_ref[...], b_ref[:, shard * cols : (shard + 1) * cols]))


def weight_grad(a, b, split=1, tile_m=512):
    length, m = a.shape
    n = b.shape[1]
    tile_m = min(tile_m, m)
    if split == 1:
        out_spec = pl.BlockSpec((tile_m, n), lambda i: (i, 0))
        out_shape = jax.ShapeDtypeStruct((m, n), jnp.bfloat16)
    else:
        out_spec = pl.BlockSpec((split, tile_m, n // split), lambda i: (0, i, 0))
        out_shape = jax.ShapeDtypeStruct((split, m, n // split), jnp.bfloat16)
    return pl.pallas_call(
        functools.partial(weight_grad_kernel, split),
        grid=(m // tile_m,),
        in_specs=[
            pl.BlockSpec((length, tile_m), lambda i: (0, i)),
            pl.BlockSpec((length, n), lambda i: (0, 0), pipeline_mode=pl.Buffered(1)),
        ],
        out_specs=out_spec,
        out_shape=out_shape,
        compiler_params=pltpu.CompilerParams(vmem_limit_bytes=VMEM_LIMIT),
        cost_estimate=pl.CostEstimate(
            flops=2 * length * m * n, bytes_accessed=2 * (length * (m + n) + m * n), transcendentals=0),
        name="weight_grad",
    )(a, b)


def ring_place(chip, chips):
    half = chips // 2
    return jnp.where(chip < half, chip, 3 * half - 1 - chip)


def shard_view(ref, kind, owner, part, extent):
    if kind == "row":
        rows = extent[0]
        if part == 0:
            return ref.at[pl.ds(owner * rows, rows)]
        half = rows // 2
        return ref.at[pl.ds(owner * rows + (part - 1) * half, half)]
    rows, cols = extent
    if part == 0:
        return ref.at[:, pl.ds(owner * cols, cols)]
    half = rows // 2
    return ref.at[pl.ds((part - 1) * half, half), pl.ds(owner * cols, cols)]


def own_view(ref, part, extent):
    if part == 0:
        return ref
    half = extent[0] // 2
    return ref.at[pl.ds((part - 1) * half, half)]


def gather_kernel(kinds, extents, pieces, chips, line, *refs):
    count = len(kinds)
    shards = refs[:count]
    rows_in = refs[count : count + pieces]
    fulls = refs[count + pieces : 2 * count + pieces]
    rows_all = refs[2 * count + pieces : 2 * count + 2 * pieces]
    ring_send, ring_recv, pair_send, pair_recv, line_send, line_recv, local = refs[
        2 * count + 2 * pieces :
    ]
    dp = lax.axis_index("dp")
    tp = lax.axis_index("tp")
    core = lax.rem(dp, 2)
    place = ring_place(lax.div(dp, 2), chips)
    hops = chips // 2

    def device(ring_pos):
        pos = lax.rem(ring_pos + chips, chips)
        return ring_place(pos, chips) * 2 + core

    right, left = device(place + 1), device(place - 1)
    sibling = dp + 1 - 2 * core
    barrier = pltpu.get_barrier_semaphore()
    for partner in (right, left, sibling):
        pl.semaphore_signal(barrier, 1, device_id={"dp": partner}, device_id_type=MESH)
    peers = 3
    if pieces:
        @pl.when(tp > 0)
        def _():
            pl.semaphore_signal(barrier, 1, device_id={"tp": tp - 1}, device_id_type=MESH)

        @pl.when(tp < line - 1)
        def _():
            pl.semaphore_signal(barrier, 1, device_id={"tp": tp + 1}, device_id_type=MESH)

        peers = peers + jnp.where(tp > 0, 1, 0) + jnp.where(tp < line - 1, 1, 0)
    pl.semaphore_wait(barrier, peers)

    def ring_copy(a, way, hop):
        owner = device(place - hop) if way == 0 else device(place + hop)
        part = 0 if hop < hops - 1 else 1 + way
        if hop == 0:
            src = own_view(shards[a], part, extents[a])
        else:
            src = shard_view(fulls[a], kinds[a], owner, part, extents[a])
        return pltpu.make_async_remote_copy(
            src_ref=src,
            dst_ref=shard_view(fulls[a], kinds[a], owner, part, extents[a]),
            send_sem=ring_send.at[a, way, hop],
            recv_sem=ring_recv.at[a, way, hop],
            device_id={"dp": right if way == 0 else left},
            device_id_type=MESH,
        )

    def ring_arrival(a, way, hop):
        owner = device(place - 1 - hop) if way == 0 else device(place + 1 + hop)
        part = 0 if hop < hops - 1 else 1 + way
        view = shard_view(fulls[a], kinds[a], owner, part, extents[a])
        return pltpu.make_async_remote_copy(
            src_ref=view,
            dst_ref=view,
            send_sem=ring_send.at[a, way, hop],
            recv_sem=ring_recv.at[a, way, hop],
            device_id={"dp": right if way == 0 else left},
            device_id_type=MESH,
        )

    def pair_copy(a, slot, owner_here, owner_there, part, arriving):
        owner = owner_there if arriving else owner_here
        view = shard_view(fulls[a], kinds[a], owner, part, extents[a])
        src = own_view(shards[a], part, extents[a]) if slot == 0 and not arriving else view
        return pltpu.make_async_remote_copy(
            src_ref=src,
            dst_ref=view,
            send_sem=pair_send.at[a, slot],
            recv_sem=pair_recv.at[a, slot],
            device_id={"dp": sibling},
            device_id_type=MESH,
        )

    def other(owner):
        return owner + 1 - 2 * core

    def line_copy(b, way, hop):
        length = rows_in[b].shape[0]
        piece = tp - hop if way == 0 else tp + hop
        view = rows_all[b].at[pl.ds(piece * length, length)]
        return pltpu.make_async_remote_copy(
            src_ref=rows_in[b] if hop == 0 else view,
            dst_ref=view,
            send_sem=line_send.at[b, way, hop],
            recv_sem=line_recv.at[b, way, hop],
            device_id={"tp": tp + 1 if way == 0 else tp - 1},
            device_id_type=MESH,
        )

    def line_arrival(b, way, hop):
        length = rows_in[b].shape[0]
        piece = tp - 1 - hop if way == 0 else tp + 1 + hop
        view = rows_all[b].at[pl.ds(piece * length, length)]
        return pltpu.make_async_remote_copy(
            src_ref=view,
            dst_ref=view,
            send_sem=line_send.at[b, way, hop],
            recv_sem=line_recv.at[b, way, hop],
            device_id={"tp": tp - 1 if way == 0 else tp + 1},
            device_id_type=MESH,
        )

    def sends(way, hop):
        if way == 0:
            return (tp < line - 1) & (tp - hop >= 0)
        return (tp > 0) & (tp + hop <= line - 1)

    def arrives(way, hop):
        if way == 0:
            return tp - 1 - hop >= 0
        return tp + 1 + hop <= line - 1

    def start_line(hop):
        for b in range(pieces):
            for way in range(2):
                @pl.when(sends(way, hop))
                def _():
                    line_copy(b, way, hop).start()

    def step_line(hop):
        for b in range(pieces):
            for way in range(2):
                @pl.when(arrives(way, hop))
                def _():
                    line_arrival(b, way, hop).wait_recv()

                if hop + 1 < line - 1:
                    @pl.when(sends(way, hop + 1))
                    def _():
                        line_copy(b, way, hop + 1).start()

    start_line(0)
    for a in range(count):
        for way in range(2):
            ring_copy(a, way, 0).start()
        pair_copy(a, 0, dp, sibling, 0, False).start()
    locals_ = []
    for a in range(count):
        locals_.append(
            pltpu.make_async_copy(
                shards[a], shard_view(fulls[a], kinds[a], dp, 0, extents[a]), local.at[a]
            )
        )
    for b in range(pieces):
        length = rows_in[b].shape[0]
        locals_.append(
            pltpu.make_async_copy(
                rows_in[b], rows_all[b].at[pl.ds(tp * length, length)], local.at[count + b]
            )
        )
    for copy in locals_:
        copy.start()
    line_hop = 0
    for hop in range(hops):
        for a in range(count):
            for way in range(2):
                ring_arrival(a, way, hop).wait_recv()
                if hop + 1 < hops:
                    ring_copy(a, way, hop + 1).start()
                owner = device(place - 1 - hop) if way == 0 else device(place + 1 + hop)
                part = 0 if hop < hops - 1 else 1 + way
                pair_copy(a, 1 + 2 * hop + way, owner, other(owner), part, False).start()
            if a == count // 2 and line_hop < line - 1:
                step_line(line_hop)
                line_hop += 1
    for hop in range(line_hop, line - 1):
        step_line(hop)
    for a in range(count):
        own = pair_copy(a, 0, dp, sibling, 0, False)
        own.wait_send()
        pair_copy(a, 0, dp, sibling, 0, True).wait_recv()
        for hop in range(hops):
            for way in range(2):
                owner = device(place - 1 - hop) if way == 0 else device(place + 1 + hop)
                part = 0 if hop < hops - 1 else 1 + way
                slot = 1 + 2 * hop + way
                pair_copy(a, slot, owner, other(owner), part, False).wait_send()
                pair_copy(a, slot, owner, other(owner), part, True).wait_recv()
                ring_copy(a, way, hop).wait_send()
    for b in range(pieces):
        for hop in range(line - 1):
            for way in range(2):
                @pl.when(sends(way, hop))
                def _():
                    line_copy(b, way, hop).wait_send()
    for copy in locals_:
        copy.wait()


def gather_all(shards, kinds, rows, dp_count, tp_count, collective_id):
    extents = [shard.shape for shard in shards]
    full_shapes = []
    for kind, extent in zip(kinds, extents):
        if kind == "row":
            full_shapes.append((extent[0] * dp_count,) + tuple(extent[1:]))
        else:
            full_shapes.append((extent[0], extent[1] * dp_count))
    chips = dp_count // 2
    hops = chips // 2
    count, pieces = len(shards), len(rows)
    out_shape = [jax.ShapeDtypeStruct(shape, s.dtype) for shape, s in zip(full_shapes, shards)]
    out_shape += [
        jax.ShapeDtypeStruct((r.shape[0] * tp_count, r.shape[1]), r.dtype) for r in rows
    ]
    dma = pltpu.SemaphoreType.DMA
    return pl.pallas_call(
        functools.partial(gather_kernel, kinds, extents, pieces, chips, tp_count),
        out_shape=out_shape,
        in_specs=[pl.BlockSpec(memory_space=pl.ANY)] * (count + pieces),
        out_specs=[pl.BlockSpec(memory_space=pl.ANY)] * (count + pieces),
        scratch_shapes=[
            dma((max(count, 1), 2, hops)),
            dma((max(count, 1), 2, hops)),
            dma((max(count, 1), 1 + 2 * hops)),
            dma((max(count, 1), 1 + 2 * hops)),
            dma((max(pieces, 1), 2, max(tp_count - 1, 1))),
            dma((max(pieces, 1), 2, max(tp_count - 1, 1))),
            dma((count + pieces,)),
        ],
        compiler_params=pltpu.CompilerParams(
            collective_id=collective_id, has_side_effects=True
        ),
        name="gather_all",
    )(*shards, *rows)


def scatter_kernel(count, chips, line, *refs):
    hops = chips // 2
    refs = list(refs)

    def take(n):
        out, refs[:n] = refs[:n], []
        return out

    grads = take(count - 1)
    line_ref, flat_ref = take(2)
    outs = take(count)
    held = take(count)
    paired = take(count)
    landed = take(count)
    small, line_land = take(2)
    pair_send, pair_recv, load_sem, ring_send, ring_recv, line_send, line_recv = refs
    dp = lax.axis_index("dp")
    tp = lax.axis_index("tp")
    core = lax.rem(dp, 2)
    place = ring_place(lax.div(dp, 2), chips)

    def chip_at(ring_pos):
        return ring_place(lax.rem(ring_pos + chips, chips), chips)

    right, left = chip_at(place + 1) * 2 + core, chip_at(place - 1) * 2 + core
    sibling = dp + 1 - 2 * core
    barrier = pltpu.get_barrier_semaphore()
    for partner in (right, left, sibling):
        pl.semaphore_signal(barrier, 1, device_id={"dp": partner}, device_id_type=MESH)
    for n in range(1, line):
        pl.semaphore_signal(
            barrier, 1, device_id={"tp": lax.rem(tp + n, line)}, device_id_type=MESH)
    pl.semaphore_wait(barrier, 3 + line - 1)

    def line_copy(n):
        return pltpu.make_async_remote_copy(
            src_ref=line_ref, dst_ref=line_land.at[n - 1],
            send_sem=line_send.at[n - 1], recv_sem=line_recv.at[n - 1],
            device_id={"tp": lax.rem(tp + n, line)}, device_id_type=MESH)

    for n in range(1, line):
        line_copy(n).start()

    offsets = [hops]
    for near in range(hops - 1, 0, -1):
        offsets += [near, -near]
    offsets.append(0)

    def source(a):
        return small if a == count - 1 else grads[a]

    def pair_copy(a, slot):
        chip = chip_at(place + offsets[slot])
        return pltpu.make_async_remote_copy(
            src_ref=source(a).at[chip * 2 + 1 - core], dst_ref=paired[a].at[slot],
            send_sem=pair_send.at[a, slot], recv_sem=pair_recv.at[a, slot],
            device_id={"dp": sibling}, device_id_type=MESH)

    def load(a, slot):
        chip = chip_at(place + offsets[slot])
        return pltpu.make_async_copy(
            source(a).at[chip * 2 + core], held[a].at[slot], load_sem.at[a, slot])

    big = range(count - 1)
    for slot in range(chips):
        for a in big:
            load(a, slot).start()
            pair_copy(a, slot).start()
    for n in range(1, line):
        line_copy(n).wait_recv()
    total = line_ref[...]
    for n in range(1, line):
        total = total + line_land[n - 1]
    rows_z = line_ref.shape[1]
    small[:, :rows_z] = total
    small[:, rows_z:] = flat_ref[...]
    last = count - 1
    for slot in range(chips):
        load(last, slot).start()
        pair_copy(last, slot).start()

    def tiles(a, rows, body):
        cols = held[a].shape[2]
        step = min(rows, max(16, 1 << ((32768 // cols).bit_length() - 1)))

        def run(t, carry):
            body(pl.ds(pl.multiple_of(t * step, step), step))
            return carry

        lax.fori_loop(0, rows // step, run, 0)

    def f32(value):
        return value.astype(jnp.float32)

    def pair_sum(a, slot):
        load(a, slot).wait()
        pair_copy(a, slot).wait_recv()

        def body(at):
            held[a][slot, at] = (f32(held[a][slot, at]) + f32(paired[a][slot, at])).astype(
                held[a].dtype)

        tiles(a, held[a].shape[1], body)

    def part_of(a, way, step):
        rows = held[a].shape[1]
        if step == 0:
            return way * (rows // 2), rows // 2
        return 0, rows

    def ring_copy(a, way, step):
        slot = offsets.index((hops - step) * (1 if way == 0 or step == 0 else -1))
        first, rows = part_of(a, way, step)
        return pltpu.make_async_remote_copy(
            src_ref=held[a].at[slot, pl.ds(first, rows)],
            dst_ref=landed[a].at[way, step, pl.ds(first, rows)],
            send_sem=ring_send.at[a, way, step], recv_sem=ring_recv.at[a, way, step],
            device_id={"dp": right if way == 0 else left}, device_id_type=MESH)

    def add_landed(a, way, step, slot):
        first, rows = part_of(a, way, step)
        ring_copy(a, way, step).wait_recv()

        def body(at):
            at = pl.ds(pl.multiple_of(at.start + first, 16), at.size)
            held[a][slot, at] = (f32(held[a][slot, at]) + f32(landed[a][way, step, at])).astype(
                held[a].dtype)

        tiles(a, rows, body)

    for a in range(count):
        pair_sum(a, 0)
        for way in range(2):
            ring_copy(a, way, 0).start()
    for step in range(1, hops):
        for a in range(count):
            for way in range(2):
                slot = offsets.index((hops - step) * (1 if way == 0 else -1))
                pair_sum(a, slot)
                add_landed(a, way, step - 1, slot)
                ring_copy(a, way, step).start()
    own = chips - 1
    for a in range(count):
        pair_sum(a, own)
        for way in range(2):
            ring_copy(a, way, hops - 1).wait_recv()

        def body(at):
            outs[a][at] = (
                f32(held[a][own, at]) + f32(landed[a][0, hops - 1, at]) + f32(landed[a][1, hops - 1, at]))

        tiles(a, held[a].shape[1], body)
    for a in range(count):
        for slot in range(chips):
            pair_copy(a, slot).wait_send()
        for way in range(2):
            for step in range(hops):
                ring_copy(a, way, step).wait_send()
    for n in range(1, line):
        line_copy(n).wait_send()


def scatter_grads(grads, line_sums, flat_sums, dp_count, tp_count, collective_id):
    chips = dp_count // 2
    hops = chips // 2
    count = len(grads) + 1
    rows_z, rows_d = line_sums.shape[1], flat_sums.shape[1]
    shapes = [g.shape[1:] for g in grads] + [(rows_z + rows_d, line_sums.shape[2])]
    dtypes = [g.dtype for g in grads] + [jnp.float32]
    dma = pltpu.SemaphoreType.DMA
    vm = pl.BlockSpec(memory_space=pltpu.VMEM)
    per = lambda lead: [pltpu.VMEM(lead + tuple(s), t) for s, t in zip(shapes, dtypes)]
    return pl.pallas_call(
        functools.partial(scatter_kernel, count, chips, tp_count),
        out_shape=[jax.ShapeDtypeStruct(s, jnp.float32) for s in shapes],
        in_specs=[pl.BlockSpec(memory_space=pl.ANY)] * len(grads) + [vm, vm],
        out_specs=[vm] * count,
        scratch_shapes=per((chips,)) + per((chips,)) + per((2, hops)) + [
            pltpu.VMEM((dp_count, rows_z + rows_d, line_sums.shape[2]), jnp.float32),
            pltpu.VMEM((max(tp_count - 1, 1),) + line_sums.shape, jnp.float32),
            dma((count, chips)), dma((count, chips)), dma((count, chips)),
            dma((count, 2, hops)), dma((count, 2, hops)),
            dma((max(tp_count - 1, 1),)), dma((max(tp_count - 1, 1),)),
        ],
        compiler_params=pltpu.CompilerParams(
            collective_id=collective_id, has_side_effects=True,
            vmem_limit_bytes=60 * 1024 * 1024),
        name="scatter_grads",
    )(*grads, line_sums, flat_sums)


def pack_small(parts):
    flat = jnp.concatenate([part.reshape(-1) for part in parts])
    rows = -(-flat.size // 4096) * 32
    return jnp.pad(flat, (0, rows * 128 - flat.size)).reshape(rows, 128)


def unpack_small(full, parts, dp_count):
    full = full.reshape(dp_count, -1).astype(jnp.float32)
    out, start = [], 0
    for part in parts:
        out.append(full[:, start : start + part.size])
        start += part.size
    return out


def by_owner(rows, dp_count):
    count = -(-rows.shape[1] // 2048) * 16
    padded = jnp.pad(rows, ((0, 0), (0, count * 128 - rows.shape[1])))
    return padded.reshape(dp_count, count, 128)


def body(
    hidden_in,
    triple_projection_weight,
    triple_projection_bias,
    attention_out_weight,
    b_dense,
    feedforward_in_weight,
    feedforward_in_bias,
    feedforward_out_weight,
    b_fc2,
    ln1_gain,
    ln1_bias,
    ln2_gain,
    ln2_bias,
    grad_out,
):
    _, piece_len, width = hidden_in.shape
    tp_count = lax.axis_size("tp")
    dp_count = lax.axis_size("dp")
    length = piece_len * tp_count
    heads = triple_projection_weight.shape[2] // HD
    cosine, sine = rotary_tables(length)
    small = [
        triple_projection_bias,
        feedforward_in_bias,
        b_dense,
        b_fc2,
        ln1_gain,
        ln1_bias,
        ln2_gain,
        ln2_bias,
    ]
    small_all, full_qkv, full_fc1, full_dense, full_fc2, x_seq = gather_all(
        [
            pack_small(small),
            triple_projection_weight.reshape(width // dp_count, -1),
            feedforward_in_weight,
            attention_out_weight,
            feedforward_out_weight,
        ],
        ["row", "row", "row", "col", "col"],
        [hidden_in[0]],
        dp_count,
        tp_count,
        0,
    )
    grad_own, x_seq = lax.optimization_barrier((grad_out, x_seq))
    cot_seq = lax.all_gather(grad_own, "tp", axis=1, tiled=True)[0]
    vectors = unpack_small(small_all, small, dp_count)
    bqkv = vectors[0].T.reshape(1, -1)
    bfc1 = vectors[1].T.reshape(1, -1)
    full_bdense, full_bfc2 = vectors[2].reshape(-1), vectors[3].reshape(-1)
    gains = jnp.stack([part.reshape(-1) for part in vectors[4:]])

    norm_one, norm_two, query, key, value, act, slope, stat = front(
        x_seq, gains, full_qkv, bqkv, full_fc1, bfc1, cosine, sine, heads
    )
    head_out, lse = attend(query, key, value, heads)
    partial_value = out_proj(head_out, act, full_dense, full_fc2)
    summed = lax.psum_scatter(partial_value, "tp", scatter_dimension=0, tiled=True)
    layer_out = (
        hidden_in[0].astype(jnp.float32) + summed.astype(jnp.float32) + full_bdense + full_bfc2
    )
    hidden_out = low(layer_out)[None]

    d_heads, d_fc, sum_bfc1 = back_in(cot_seq, slope, full_dense, full_fc2)
    d_qkv, sum_bqkv = attend_back(query, key, value, head_out, d_heads, lse, cosine, sine, heads)
    e_sum, ln_sums = back_out(d_qkv, d_fc, x_seq, stat, gains, full_qkv, full_fc1)
    e_piece = lax.psum_scatter(e_sum, "tp", scatter_dimension=0, tiled=True).astype(jnp.float32)

    grad_fc2 = weight_grad(act, cot_seq, dp_count)
    grad_dense = weight_grad(head_out, cot_seq, dp_count)
    grad_fc1 = weight_grad(norm_two, d_fc).reshape(dp_count, -1, d_fc.shape[1])
    grad_qkv = weight_grad(norm_one, d_qkv).reshape(dp_count, -1, d_qkv.shape[1])

    cot_piece = grad_out[0].astype(jnp.float32)
    sum_out = jnp.sum(cot_piece, axis=0, keepdims=True)
    line_sums = jnp.concatenate([ln_sums, sum_out], axis=0)
    line_sums = line_sums.reshape(5, dp_count, -1).transpose(1, 0, 2).reshape(dp_count, -1)
    flat_sums = jnp.concatenate([sum_bqkv, sum_bfc1], axis=1).reshape(-1, dp_count).T
    line_rows, flat_rows = by_owner(line_sums, dp_count), by_owner(flat_sums, dp_count)
    own_fc2, own_dense, own_fc1, own_qkv, own_small = scatter_grads(
        [grad_fc2, grad_dense, grad_fc1, grad_qkv], line_rows, flat_rows, dp_count, tp_count, 1
    )
    own_line = own_small[: line_rows.shape[1]].reshape(-1)[: line_sums.shape[1]].reshape(5, -1)
    own_flat = own_small[line_rows.shape[1] :].reshape(-1)[: flat_sums.shape[1]]
    split = sum_bqkv.size // dp_count

    x_own = hidden_in[0].astype(jnp.float32)
    mean = jnp.mean(x_own, axis=-1, keepdims=True)
    centered = x_own - mean
    rstd = lax.rsqrt(jnp.mean(centered * centered, axis=-1, keepdims=True) + EPSILON)
    xhat = centered * rstd
    back = (
        e_piece
        - jnp.mean(e_piece, axis=-1, keepdims=True)
        - xhat * jnp.mean(e_piece * xhat, axis=-1, keepdims=True)
    ) * rstd
    grad_in = (cot_piece + back)[None]
    return (
        hidden_out,
        grad_in,
        own_qkv.reshape(triple_projection_weight.shape),
        own_flat[:split].reshape(triple_projection_bias.shape),
        own_dense,
        own_line[4],
        own_fc1,
        own_flat[split:].reshape(feedforward_in_bias.shape),
        own_fc2,
        own_line[4],
        own_line[0],
        own_line[1],
        own_line[2],
        own_line[3],
    )


def solution(mesh):
    return jax.shard_map(
        body,
        mesh=mesh,
        in_specs=(
            P("dp", "tp", None),
            P("dp", None, "tp"),
            P(None, "tp", "dp"),
            P("tp", "dp"),
            P("dp"),
            P("dp", "tp"),
            P("tp", "dp"),
            P("tp", "dp"),
            P("dp"),
            P("dp"),
            P("dp"),
            P("dp"),
            P("dp"),
            P("dp", "tp", None),
        ),
        out_specs=(
            P("dp", "tp", None),
            P("dp", "tp", None),
            P("dp", None, "tp"),
            P(None, "tp", "dp"),
            P("tp", "dp"),
            P("dp"),
            P("dp", "tp"),
            P("tp", "dp"),
            P("tp", "dp"),
            P("dp"),
            P("dp"),
            P("dp"),
            P("dp"),
            P("dp"),
        ),
        check_vma=False,
    )
```

time: 1190 us -> 753 us (0.63)
  Pallas kernels: 0 us -> 560 us
  matrix products: 374 us -> 0 us
  waiting for transfers between devices: 492 us -> 129 us
  other arithmetic: 123 us -> 14.3 us
  blocking collectives: 93.9 us -> 0 us
  local copies, waits for them, and re-layouts: 77.4 us -> 24.5 us
    pallas_call x0 -> x12, Pallas kernels: none -> 560 us  [the longest x1 164 us: gather_all(): pl.pallas_call(functools.partial(gather_kernel, kinds, extents, pieces, c...]
    dot_general x36 -> x0, matrix products: 374 us -> none  [the longest x1 32.4 us: body(): jnp.einsum('ld,fd->lf', cot_seq, full_fc2, preferred_element_type=jnp.flo...]
    all_gather x6 -> x1, waiting for transfers between devices: 275 us -> 76.7 us  [body(): cot_seq = lax.all_gather(grad_own, 'tp', axis=1, tiled=True)[0]]
    reduce_scatter x5 -> x1, waiting for transfers between devices: 144 us -> 52.3 us  [body(): lax.psum_scatter(partial_value, 'tp', scatter_dimension=0, tiled=True)]
    reduce_scatter x1, waiting for transfers between devices: 69.4 us -> 0.01 us  [body(): lax.psum_scatter(e_sum, 'tp', scatter_dimension=0, tiled=True)]
    psum x2 -> x0, blocking collectives: 67.6 us -> none  [the longest x1 41.5 us: body(): shared = lax.psum(shared, ('dp', 'tp')).reshape(5, dp_count, -1)]
    convert_element_type x9 -> x0, other arithmetic: 36.8 us -> none  [the longest x4 27 us: attend_backward(): d_scores = (probabilities * (d_probs - inner)).astype(jnp.bfloat16)]
    unnamed x1 -> x0, blocking collectives: 26.3 us -> none
  transfers between devices with their start and end apart: 12 -> 3, of which waited for: 5 -> 2; matrix products, arithmetic and copies ran while one was open for 47% -> 3% of each run, Pallas kernels for 0% -> 40%
where the time goes in v2:
time: 753 us; the launch traced here: 743 us
  Pallas kernels  560 us (74%)
  waiting for transfers between devices  129 us (17%)
  local copies, waits for them, and re-layouts  24.5 us (3%)
  between operations  14.4 us (2%)
  other arithmetic  14.3 us (2%)
    pallas_call x1, Pallas kernels, gather_all(): pl.pallas_call(functools.partial(gather_kernel, kinds, extents, pieces, c...  164 us
    pallas_call x1, Pallas kernels, scatter_grads(): pl.pallas_call(functools.partial(scatter_kernel, count, chips, tp_count),...  121 us
    all_gather x1, waiting for transfers between devices, body(): cot_seq = lax.all_gather(grad_own, 'tp', axis=1, tiled=True)[0]  76.7 us
    pallas_call x4, Pallas kernels, weight_grad(): pl.pallas_call(functools.partial(weight_grad_kernel, split), grid=(m // t...  75.9 us
    reduce_scatter x1, waiting for transfers between devices, body(): lax.psum_scatter(partial_value, 'tp', scatter_dimension=0, tiled=True)  52.3 us
    pallas_call x1, Pallas kernels, front(): pl.pallas_call(functools.partial(front_kernel, heads), grid=(length // ro...  52.2 us
    pallas_call x1, Pallas kernels, back_out(): pl.pallas_call(back_out_kernel, grid=(length // rows,), in_specs=[row(dqk...  42 us
    pallas_call x1, Pallas kernels, back_in(): pl.pallas_call(back_in_kernel, grid=(length // rows,), in_specs=[row(widt...  30.1 us
  transfers between devices with their start and end apart: 3, of which 2 were waited for; matrix products, arithmetic and copies ran while one was open for 3% of the time, Pallas kernels for 40%

profile of v2, /device:TPU:0, one launch (start us, length us, event | category | flops | bytes accessed | tf_op | source)
XLA Modules:
  0.0 742.6 jit_solution(18016408815928014489)
XLA Ops:
  7.2 1.4 copy.36
  8.6 1.2 copy.37.refs_1_
  11.2 4.1 concatenate.14
  15.9 164.2 %gather_all.1 = (bf16[256,128]{1,0:T(8,128)(2,1)}, bf16[2048,1536]{1,0:T(8,128)(2,1)}, bf16[2048,2048]{1,0:T(8,128)(2,1)}, bf16[512,2048]{1,0:T(8,128)(2,1)}, bf...) custom-call(bf16[32,128]{1,0:T(8,128)(2,1)} %pad_bitcast_fusion.1.refs_0_, bf16[256,1536]{1,0:T(8,128)(2,1)} %copy.37.refs_1_, ...), custom_call_target="tpu_custom_call" | custom-call | tf_op jit(solution)/shard_map/gather_all/pallas_call | solution.py:665
  183.6 52.2 %front.1 = (bf16[2048,2048]{1,0:T(8,128)(2,1)}, bf16[2048,2048]{1,0:T(8,128)(2,1)}, bf16[2048,512]{1,0:T(8,128)(2,1)}, bf16[2048,512]{1,0:T(8,128)(2,1)}, bf16[2...) custom-call(bf16[2048,2048]{1,0:T(8,128)(2,1)} %get-tuple-element.45.x_ref, ...), custom_call_target="tpu_custom_call" | custom-call | flops 30064771072 | bytes 60000000 | tf_op jit(solution)/shard_map/front/pallas_call | solution.py:101
  235.8 17.8 %attend.1 = (bf16[2048,512]{1,0:T(8,128)(2,1)}, f32[2,2048]{1,0:T(2,128)}) custom-call(bf16[2048,512]{1,0:T(8,128)(2,1)} %get-tuple-element.49.q_ref, bf16[2048,512]{1,0:T(8,128)(2,1)} %get-tuple-element.50.k_ref, bf16[2048,512]{1,0:T(8,128)(2,1)} %get-tuple-element.51.v_ref), custom_call_target="tpu_custom_call" | custom-call | flops 4294967296 | bytes 8388608 | tf_op jit(solution)/shard_map/attend/pallas_call | solution.py:166
  253.6 76.7 %all-gather.2.cloned.1.call-done = bf16[1,2048,2048]{2,1,0:T(8,128)(2,1)} async-done(((bf16[1,512,2048]{2,1,0:T(8,128)(2,1)}), bf16[1,2048,2048]{2,1,0:T(8,128)(2,1)}) %all-gather.2.cloned.1.call-update) | async-done | bytes 8388624 | tf_op jit(solution)/shard_map/all_gather | solution.py:945
  330.2 30.1 %back_in.1 = (bf16[2048,512]{1,0:T(8,128)(2,1)}, bf16[2048,2048]{1,0:T(8,128)(2,1)}, f32[1,2048]{1,0:T(1,128)}) custom-call(bf16[2048,2048]{1,0:T(8,128)(2,1)} %bitcast.96, bf16[2048,2048]{1,0:T(8,128)(2,1)} %get-tuple-element.57.slope_ref, bf16[512,2048]{1,0:T(8,128)(2,1)} %get-tuple-element.54.wd_ref, bf16[2048,2048]{1,0:T(8,128)(2,1)} %get-tuple-element.55.w2_ref), custom_call_target="tpu_custom_call" | custom-call | flops 21474836480 | bytes 40000000 | tf_op jit(solution)/shard_map/back_in/pallas_call | solution.py:336
  360.4 28.1 %attend_back.1 = (bf16[2048,1536]{1,0:T(8,128)(2,1)}, f32[1,1536]{1,0:T(1,128)}) custom-call(bf16[2048,512]{1,0:T(8,128)(2,1)} %get-tuple-element.49.q_ref, bf16[2048,512]{1,0:T(8,128)(2,1)} %get-tuple-element.50.k_ref, bf16[2048,512]{1,0:T(8,128)(2,1)} %get-tuple-element.51.v_ref, bf16[2048,512]{1,0:T(8,128)(2,1)} %get-tuple-element.52.h_ref.o_ref.a_ref, ...), custom_call_target="tpu_custom_call" | custom-call | flops 10737418240 | bytes 20971520 | tf_op jit(solution)/shard_map/attend_back/pallas_call | solution.py:270
  388.4 42.0 %back_out.1 = (bf16[2048,2048]{1,0:T(8,128)(2,1)}, f32[4,2048]{1,0:T(4,128)}) custom-call(bf16[2048,1536]{1,0:T(8,128)(2,1)} %get-tuple-element.60.dqkv_ref.b_ref, bf16[2048,2048]{1,0:T(8,128)(2,1)} %get-tuple-element.61.dfc_ref.b_ref, bf16[2048,2048]{1,0:T(8,128)(2,1)} %get-tuple-element.45.x_ref, f32[2048,128]{1,0:T(8,128)} %get-tuple-element.62.stat_ref, ...), custom_call_target="tpu_custom_call" | custom-call | flops 30064771072 | bytes 50000000 | tf_op jit(solution)/shard_map/back_out/pallas_call | solution.py:376
  430.5 29.4 %out_proj.1 = bf16[2048,2048]{1,0:T(8,128)(2,1)} custom-call(bf16[2048,512]{1,0:T(8,128)(2,1)} %get-tuple-element.52.h_ref.o_ref.a_ref, bf16[2048,2048]{1,0:T(8,128)(2,1)} %get-tuple-element.53.a_ref, bf16[512,2048]{1,0:T(8,128)(2,1)} %get-tuple-element.54.wd_ref, bf16[2048,2048]{1,0:T(8,128)(2,1)} %get-tuple-element.55.w2_ref), custom_call_target="tpu_custom_call" | custom-call | flops 21474836480 | bytes 30000000 | tf_op jit(solution)/shard_map/out_proj/pallas_call | solution.py:303
  460.0 2.1 convert_reduce_fusion.2
  465.1 9.9 %weight_grad.5.refs_1_ = bf16[8,512,256]{2,1,0:T(8,128)(2,1)} custom-call(bf16[2048,512]{1,0:T(8,128)(2,1)} %get-tuple-element.52.h_ref.o_ref.a_ref, bf16[2048,2048]{1,0:T(8,128)(2,1)} %bitcast.97), custom_call_target="tpu_custom_call" | custom-call | flops 4294967296 | bytes 12582912 | tf_op jit(solution)/shard_map/weight_grad/pallas_call | solution.py:412
  475.0 18.4 %weight_grad.7 = bf16[2048,1536]{1,0:T(8,128)(2,1)} custom-call(bf16[2048,2048]{1,0:T(8,128)(2,1)} %get-tuple-element.65.a_ref, bf16[2048,1536]{1,0:T(8,128)(2,1)} %get-tuple-element.60.dqkv_ref.b_ref), custom_call_target="tpu_custom_call" | custom-call | flops 12884901888 | bytes 20971520 | tf_op jit(solution)/shard_map/weight_grad/pallas_call | solution.py:412
  493.4 24.1 %weight_grad.4.refs_0_ = bf16[8,2048,256]{2,1,0:T(8,128)(2,1)} custom-call(bf16[2048,2048]{1,0:T(8,128)(2,1)} %get-tuple-element.53.a_ref, bf16[2048,2048]{1,0:T(8,128)(2,1)} %bitcast.98), custom_call_target="tpu_custom_call" | custom-call | flops 17179869184 | bytes 25165824 | tf_op jit(solution)/shard_map/weight_grad/pallas_call | solution.py:412
  517.5 23.5 %weight_grad.6 = bf16[2048,2048]{1,0:T(8,128)(2,1)} custom-call(bf16[2048,2048]{1,0:T(8,128)(2,1)} %get-tuple-element.64.a_ref, bf16[2048,2048]{1,0:T(8,128)(2,1)} %get-tuple-element.61.dfc_ref.b_ref), custom_call_target="tpu_custom_call" | custom-call | flops 17179869184 | bytes 25165824 | tf_op jit(solution)/shard_map/weight_grad/pallas_call | solution.py:412
  541.0 120.6 %scatter_grads.1 = (f32[2048,256]{1,0:T(8,128)}, f32[512,256]{1,0:T(8,128)}, f32[256,2048]{1,0:T(8,128)}, f32[256,1536]{1,0:T(8,128)}, f32[32,128]{1,0:T(8,128)}) custom-call(bf16[8,2048,256]{2,1,0:T(8,128)(2,1)} %weight_grad.4.refs_0_, bf16[8,512,256]{2,1,0:T(8,128)(2,1)} %weight_grad.5.refs_1_, bf16[8,256,2048]{2,1,0:T(8,128)(2,1)} %bitcast.76, ...), custom_call_target="tpu_custom_call" | custom-call | tf_op jit(solution)/shard_map/scatter_grads/pallas_call | solution.py:858
  661.6 3.0 copy.41
  664.7 3.0 copy.43
  669.5 3.3 convert_reduce_fusion
  672.8 52.3 %reduce-scatter.3.cloned.1.call-done = bf16[512,2048]{1,0:T(8,128)(2,1)} async-done(((bf16[2048,2048]{1,0:T(8,128)(2,1)}), bf16[512,2048]{1,0:T(8,128)(2,1)}) %reduce-scatter.3.cloned.1.call-update) | async-done | bytes 2097168 | tf_op jit(solution)/shard_map/reduce_scatter | solution.py:957
  725.1 6.5 fusion.6
  733.0 1.3 copy.65
  734.4 1.3 copy.66
  (63 shorter events, 11.8 us)
Async XLA Ops:
  7.2 323.1 %all-gather.2.cloned.1.call-start = ((), (), s32[]{:S(2)}) async-start(), calls=%async_computation.3 | async-start | bytes 10485760 | tf_op jit(solution)/shard_map/all_gather | solution.py:945
  180.2 489.3 %reduce-scatter.5.cloned.1.call-start = ((), (), s32[]{:S(2)}) async-start(), calls=%async_computation.4 | async-start | bytes 10485760 | tf_op jit(solution)/shard_map/reduce_scatter | solution.py:966
  430.5 294.6 %reduce-scatter.3.cloned.1.call-start = ((), (), s32[]{:S(2)}) async-start(), calls=%async_computation.2 | async-start | bytes 10485760 | tf_op jit(solution)/shard_map/reduce_scatter | solution.py:957
  459.9 2.2 copy-start
  459.9 3.3 copy-start.6
  459.9 3.3 copy-start.7
  459.9 4.5 copy-start.4
  661.6 6.1 copy-start.5
  669.5 62.1 %copy-start.8 = (f32[256]{0:T(256)}, f32[256]{0:T(256)S(1)}, u32[]{:S(2)}) copy-start(f32[256]{0:T(256)S(1)} %get-tuple-element.169) | copy-start | bytes 3076
  725.1 7.1 copy-start.3
  725.1 7.9 %copy-start.2 = (f32[256,2048]{1,0:T(8,128)S(1)}, f32[256,2048]{1,0:T(8,128)}, u32[]{:S(2)}) copy-start(f32[256,2048]{1,0:T(8,128)} %get-tuple-element.170) | copy-start | bytes 6291460
  731.7 2.7 copy-start.1
Sparse Core Ops, SparseCore 0:
  180.3 149.8 all-gather.1
  430.6 146.8 reduce-scatter.4
  579.9 145.1 reduce-scatter.2

commit v3 on v1

v3 whole, which is shorter than its diff:
```python
import functools
import math

import jax
import jax.numpy as jnp
import numpy as np
from jax import lax
from jax.experimental import pallas as pl
from jax.experimental.pallas import tpu as pltpu
from jax.sharding import PartitionSpec as P

MESH = pl.DeviceIdType.MESH
EPSILON = 1e-05
MASKED = -1e30
HD = 256
ROT = 64
VMEM_LIMIT = 60 * 1024 * 1024
LOG2E = 1.4426950408889634


def low(value):
    return value.astype(jnp.bfloat16)


def dot_nn(a, b):
    return lax.dot_general(a, b, (((1,), (0,)), ((), ())), preferred_element_type=jnp.float32)


def dot_nt(a, b):
    return lax.dot_general(a, b, (((1,), (1,)), ((), ())), preferred_element_type=jnp.float32)


def dot_tn(a, b):
    return lax.dot_general(a, b, (((0,), (0,)), ((), ())), preferred_element_type=jnp.float32)


def rotary_tables(length):
    half = ROT // 2
    exponent = np.arange(half, dtype=np.float32) * np.float32(2.0 / ROT)
    inverse = np.exp(exponent * np.float32(-math.log(10000.0)), dtype=np.float32)
    angle = np.arange(length, dtype=np.float32)[:, None] * inverse[None, :]
    cosine = np.ones((length, 128), np.float32)
    sine = np.zeros((length, 128), np.float32)
    cosine[:, :half] = cosine[:, half:ROT] = np.cos(angle)
    sine[:, :half] = -np.sin(angle)
    sine[:, half:ROT] = np.sin(angle)
    return jnp.asarray(cosine), jnp.asarray(sine)


def turned(part):
    half = ROT // 2
    lane = lax.broadcasted_iota(jnp.int32, part.shape, 1)
    return jnp.where(
        lane < half, pltpu.roll(part, 128 - half, 1), pltpu.roll(part, half, 1)
    )


def ring_place(chip, chips):
    half = chips // 2
    return jnp.where(chip < half, chip, 3 * half - 1 - chip)


def shard_view(ref, kind, owner, part, extent):
    axis = 1 if kind == "mid" else 0
    rows = extent[axis]
    first, size = (0, rows) if part == 0 else ((part - 1) * (rows // 2), rows // 2)
    if kind == "row":
        return ref.at[pl.ds(owner * rows + first, size)]
    if kind == "mid":
        return ref.at[:, pl.ds(owner * rows + first, size)]
    return ref.at[pl.ds(first, size), pl.ds(owner * extent[1], extent[1])]


def own_view(ref, kind, part, extent):
    if part == 0:
        return ref
    axis = 1 if kind == "mid" else 0
    half = extent[axis] // 2
    at = pl.ds((part - 1) * half, half)
    return ref.at[:, at] if kind == "mid" else ref.at[at]


def picked(tp, values):
    out = values[0]
    for i in range(1, len(values)):
        out = jnp.where(tp == i, values[i], out)
    return out


def order_of(line):
    return [sorted(range(line), key=lambda p: (abs(p - z), p)) for z in range(line)]


def head_kernel(cfg, *refs):
    chips, line, heads, n_q, n_b = cfg
    hops = chips // 2
    refs = list(refs)

    def take(n):
        out, refs[:n] = refs[:n], []
        return out

    shards = take(5)
    x_ref, cot_ref, cos_ref, sin_ref = take(4)
    (x_all, cot_all, n1_out, n2_out, q_out, k_out, v_out, act_out, slope_out,
     stat_out, head_out, lse_out, part_out, dh_out, dfc_out, land_out, acc_out, dqkv_out, e_out,
     hidden_out, vec_out, sfc_out, sq_out, ln_out) = take(24)
    fulls = take(5)
    small_ref, wq_ref, w1_ref, wd_ref, w2_ref = fulls
    kvec, bq_ref, b1_ref, k_buf, v_buf, sq_ref, ln_ref = take(7)
    (ring_send, ring_recv, pair_send, pair_recv, line_send, line_recv, local,
     sum_send, sum_recv, keep) = refs
    kinds = ["row", "mid", "row", "col", "col"]
    extents = [s.shape for s in shards]
    count = 5
    dp = lax.axis_index("dp")
    tp = lax.axis_index("tp")
    dp_count = 2 * chips
    core = lax.rem(dp, 2)
    place = ring_place(lax.div(dp, 2), chips)
    length = x_ref.shape[0]
    total_len = length * line
    width = x_ref.shape[1]

    def device(ring_pos):
        return ring_place(lax.rem(ring_pos + chips, chips), chips) * 2 + core

    right, left = device(place + 1), device(place - 1)
    sibling = dp + 1 - 2 * core
    barrier = pltpu.get_barrier_semaphore()
    for partner in (right, left, sibling):
        pl.semaphore_signal(barrier, 1, device_id={"dp": partner}, device_id_type=MESH)

    @pl.when(tp > 0)
    def _():
        pl.semaphore_signal(barrier, 1, device_id={"tp": tp - 1}, device_id_type=MESH)

    @pl.when(tp < line - 1)
    def _():
        pl.semaphore_signal(barrier, 1, device_id={"tp": tp + 1}, device_id_type=MESH)

    pl.semaphore_wait(barrier, 3 + jnp.where(tp > 0, 1, 0) + jnp.where(tp < line - 1, 1, 0))

    def ring_copy(a, way, hop, arriving=False):
        back = hop + 1 if arriving else hop
        owner = device(place - back) if way == 0 else device(place + back)
        part = 0 if hop < hops - 1 else 1 + way
        view = shard_view(fulls[a], kinds[a], owner, part, extents[a])
        own = hop == 0 and not arriving
        return pltpu.make_async_remote_copy(
            src_ref=own_view(shards[a], kinds[a], part, extents[a]) if own else view,
            dst_ref=view,
            send_sem=ring_send.at[a, way, hop],
            recv_sem=ring_recv.at[a, way, hop],
            device_id={"dp": right if way == 0 else left},
            device_id_type=MESH,
        )

    def pair_copy(a, slot, arriving=False):
        if slot == 0:
            owner, part = dp, 0
        else:
            hop, way = divmod(slot - 1, 2)
            owner = device(place - 1 - hop) if way == 0 else device(place + 1 + hop)
            part = 0 if hop < hops - 1 else 1 + way
        if arriving:
            owner = owner + 1 - 2 * core
        view = shard_view(fulls[a], kinds[a], owner, part, extents[a])
        return pltpu.make_async_remote_copy(
            src_ref=shards[a] if slot == 0 and not arriving else view,
            dst_ref=view,
            send_sem=pair_send.at[a, slot],
            recv_sem=pair_recv.at[a, slot],
            device_id={"dp": sibling},
            device_id_type=MESH,
        )

    def rows_of(piece):
        return pl.ds(pl.multiple_of(piece * length, length), length)

    def line_copy(b, way, hop, arriving=False):
        back = hop + 1 if arriving else hop
        piece = tp - back if way == 0 else tp + back
        view = (x_all, cot_all)[b].at[rows_of(piece)]
        to = tp + 1 if way == 0 else tp - 1
        if arriving:
            to = tp - 1 if way == 0 else tp + 1
        return pltpu.make_async_remote_copy(
            src_ref=(x_ref, cot_ref)[b] if hop == 0 and not arriving else view,
            dst_ref=view,
            send_sem=line_send.at[b, way, hop],
            recv_sem=line_recv.at[b, way, hop],
            device_id={"tp": to},
            device_id_type=MESH,
        )

    def sends(way, hop):
        return (tp < line - 1) & (tp >= hop) if way == 0 else (tp > 0) & (tp + hop < line)

    def arrives(way, hop):
        return tp - 1 - hop >= 0 if way == 0 else tp + 1 + hop < line

    def start_line(b, hop):
        for way in range(2):
            @pl.when(sends(way, hop))
            def _():
                line_copy(b, way, hop).start()

    def step_line(b, hop):
        for way in range(2):
            @pl.when(arrives(way, hop))
            def _():
                line_copy(b, way, hop, True).wait_recv()

            if hop + 1 < line - 1:
                @pl.when(sends(way, hop + 1))
                def _():
                    line_copy(b, way, hop + 1).start()

    start_line(0, 0)
    for a in range(count):
        for way in range(2):
            ring_copy(a, way, 0).start()
        pair_copy(a, 0).start()
    locals_ = [
        pltpu.make_async_copy(
            shards[a], shard_view(fulls[a], kinds[a], dp, 0, extents[a]), local.at[a])
        for a in range(count)
    ]
    locals_.append(pltpu.make_async_copy(x_ref, x_all.at[rows_of(tp)], local.at[count]))
    locals_.append(pltpu.make_async_copy(cot_ref, cot_all.at[rows_of(tp)], local.at[count + 1]))
    for copy in locals_:
        copy.start()
    line_hop = 0
    for hop in range(hops):
        for a in range(count):
            for way in range(2):
                ring_copy(a, way, hop, True).wait_recv()
                if hop + 1 < hops:
                    ring_copy(a, way, hop + 1).start()
                pair_copy(a, 1 + 2 * hop + way).start()
            if a == count // 2 and line_hop < line - 2:
                step_line(0, line_hop)
                line_hop += 1
    for a in range(count):
        locals_[a].wait()
        for slot in range(1 + 2 * hops):
            pair_copy(a, slot, True).wait_recv()

    small_rows = extents[0][0]
    per = width // dp_count // 128
    for d in range(dp_count):
        block = small_ref[d * small_rows : (d + 1) * small_rows].astype(jnp.float32)
        for vec in range(6):
            for r in range(per):
                at = (d * per + r) * 128
                row = vec * per + r
                kvec[vec : vec + 1, at : at + 128] = block[row : row + 1]
    span = 128 * dp_count
    lane = lax.broadcasted_iota(jnp.int32, (128, span), 0)
    col = lax.broadcasted_iota(jnp.int32, (128, span), 1)
    mixed = jnp.zeros((16, span), jnp.float32)
    for d in range(dp_count):
        hot = jnp.where(col == lane * dp_count + d, 1.0, 0.0).astype(jnp.bfloat16)
        mixed += dot_nn(small_ref[d * small_rows + 16 : d * small_rows + 32], hot)
    for ref, first, n in ((bq_ref, 0, n_q), (b1_ref, n_q, n_b)):
        for r in range(n):
            wide = min(span, ref.shape[1] - r * span)
            ref[0:1, r * span : r * span + wide] = mixed[first + r : first + r + 1, :wide]

    def front_body(x_blk, cos_blk, sin_blk, n1, n2, q, k, v, act, slope, stat):
        x = x_blk[...].astype(jnp.float32)
        mean = jnp.mean(x, axis=1, keepdims=True)
        centered = x - mean
        rstd = lax.rsqrt(jnp.mean(centered * centered, axis=1, keepdims=True) + EPSILON)
        xhat = centered * rstd
        n1[...] = low(xhat * kvec[2:3] + kvec[3:4])
        n2[...] = low(xhat * kvec[4:5] + kvec[5:6])
        lanes = lax.broadcasted_iota(jnp.int32, stat.shape, 1)
        stat[...] = jnp.where(lanes == 0, mean, rstd)
        cosine, sine = cos_blk[...], sin_blk[...]
        qw = heads * HD
        for which, out in enumerate((q, k, v)):
            for head in range(heads):
                cols = slice(head * HD, (head + 1) * HD)
                bias = slice(which * qw + head * HD, which * qw + (head + 1) * HD)
                raw = dot_nn(n1[...], wq_ref[which, :, cols]) + bq_ref[:, bias]
                if which < 2:
                    first = raw[:, :128]
                    first = first * cosine + turned(first) * sine
                    out[:, head * HD : head * HD + 128] = low(first)
                    out[:, head * HD + 128 : (head + 1) * HD] = low(raw[:, 128:])
                else:
                    out[:, cols] = low(raw)
        step = 256
        for at in range(0, w1_ref.shape[1], step):
            u = dot_nn(n2[...], w1_ref[:, at : at + step]) + b1_ref[:, at : at + step]
            cdf = 0.5 * (1.0 + lax.erf(u * (1.0 / math.sqrt(2.0))))
            pdf = jnp.exp(-0.5 * u * u) * (1.0 / math.sqrt(2.0 * math.pi))
            act[:, at : at + step] = low(u * cdf)
            slope[:, at : at + step] = low(cdf + u * pdf)

    block = min(256, length)
    wblock = min(512, length)

    def spec(n):
        return pl.BlockSpec((block, n), lambda i: (i, 0))

    qw, ff = heads * HD, w1_ref.shape[1]
    front_outs = (n1_out, n2_out, q_out, k_out, v_out, act_out, slope_out, stat_out)
    front_pipe = pltpu.emit_pipeline(
        front_body,
        grid=(length // block,),
        in_specs=[spec(width), spec(128), spec(128)],
        out_specs=[spec(ref.shape[1]) for ref in front_outs],
    )
    table = order_of(line)

    def piece_at(k):
        return picked(tp, [table[z][k] for z in range(line)])

    locals_[count].wait()
    for k in range(line):
        if k > 0:
            for hop in range(line_hop, k):
                step_line(0, hop)
                line_hop = hop + 1
        if k == line - 1:
            start_line(1, 0)
        at = rows_of(piece_at(k))
        front_pipe(
            x_all.at[at], cos_ref.at[at], sin_ref.at[at], *[ref.at[at] for ref in front_outs])

    kv_copies = [
        pltpu.make_async_copy(k_out, k_buf, local.at[0]),
        pltpu.make_async_copy(v_out, v_buf, local.at[1]),
    ]
    for copy in kv_copies:
        copy.start()
    for copy in kv_copies:
        copy.wait()
    qblock = min(512, total_len)
    scale = LOG2E * HD ** -0.5

    def attend_body(q_blk, o_blk, lse_blk):
        i = pl.program_id(0)
        qs = [q_blk[:, h * HD : (h + 1) * HD] for h in range(heads)]

        def one(h, j, state, diagonal):
            top, total, acc = state
            rows = pl.ds(pl.multiple_of(j * qblock, qblock), qblock)
            key = k_buf[rows, h * HD : (h + 1) * HD]
            value = v_buf[rows, h * HD : (h + 1) * HD]
            s = dot_nt(key, qs[h]) * scale
            if diagonal:
                kp = lax.broadcasted_iota(jnp.int32, s.shape, 0)
                qp = lax.broadcasted_iota(jnp.int32, s.shape, 1)
                s = jnp.where(kp <= qp, s, MASKED)
            new_top = jnp.maximum(top, jnp.max(s, axis=0, keepdims=True))
            p = jnp.exp2(s - new_top)
            shrink = jnp.exp2(top - new_top)
            total = total * shrink + jnp.sum(p, axis=0, keepdims=True)
            acc = acc * shrink + dot_tn(value, low(p))
            return new_top, total, acc

        def start():
            return (
                jnp.full((1, qblock), MASKED, jnp.float32),
                jnp.zeros((1, qblock), jnp.float32),
                jnp.zeros((HD, qblock), jnp.float32),
            )

        def step(j, states):
            return tuple(one(h, j, states[h], False) for h in range(heads))

        states = lax.fori_loop(0, i, step, tuple(start() for _ in range(heads)))
        states = [one(h, i, states[h], True) for h in range(heads)]
        for h in range(heads):
            top, total, acc = states[h]
            o_blk[:, h * HD : (h + 1) * HD] = low((acc / total).T)
            lse_blk[h : h + 1, :] = top + jnp.log2(total)

    pltpu.emit_pipeline(
        attend_body,
        grid=(total_len // qblock,),
        in_specs=[pl.BlockSpec((qblock, qw), lambda i: (i, 0))],
        out_specs=[
            pl.BlockSpec((qblock, qw), lambda i: (i, 0)),
            pl.BlockSpec((heads, qblock), lambda i: (0, i)),
        ],
    )(q_out, head_out, lse_out)
    step_line(1, 0)
    cot_hop = 1

    def out_body(h_blk, a_blk, o_blk):
        step = 512
        for at in range(0, o_blk.shape[1], step):
            o_blk[:, at : at + step] = low(
                dot_nn(h_blk[...], wd_ref[:, at : at + step])
                + dot_nn(a_blk[...], w2_ref[:, at : at + step]))

    out_pipe = pltpu.emit_pipeline(
        out_body, grid=(length // block,), in_specs=[spec(qw), spec(ff)], out_specs=[spec(width)])

    def sum_copy(way, step, from_acc):
        dist = line - step
        piece = tp + dist if way == 0 else tp - dist
        src = acc_out.at[way, step - 2] if from_acc else part_out.at[rows_of(piece)]
        return pltpu.make_async_remote_copy(
            src_ref=src,
            dst_ref=land_out.at[way, step - 1],
            send_sem=sum_send.at[way, step - 1],
            recv_sem=sum_recv.at[way, step - 1],
            device_id={"tp": tp + 1 if way == 0 else tp - 1},
            device_id_type=MESH,
        )

    def sum_sends(way, step):
        dist = line - step
        return tp + dist < line if way == 0 else tp - dist >= 0

    def sum_first(way):
        return tp == 0 if way == 0 else tp == line - 1

    def sum_arrival(way, step):
        view = land_out.at[way, step - 1]
        return pltpu.make_async_remote_copy(
            src_ref=view, dst_ref=view,
            send_sem=sum_send.at[way, step - 1], recv_sem=sum_recv.at[way, step - 1],
            device_id={"tp": tp - 1 if way == 0 else tp + 1}, device_id_type=MESH)

    def sum_arrives(way, step):
        dist = line - step
        if way == 0:
            return (tp >= 1) & (tp - 1 + dist < line)
        return (tp + 1 < line) & (tp + 1 - dist >= 0)

    def add_body(a_blk, b_blk, o_blk):
        o_blk[...] = low(a_blk[...].astype(jnp.float32) + b_blk[...].astype(jnp.float32))

    add_pipe = pltpu.emit_pipeline(
        add_body, grid=(length // block,), in_specs=[spec(width)] * 2, out_specs=[spec(width)])

    def start_sum(step):
        for way in range(2):
            dist = line - step
            piece = tp + dist if way == 0 else tp - dist

            @pl.when(sum_sends(way, step) & sum_first(way))
            def _():
                sum_copy(way, step, False).start()

            if step > 1:
                @pl.when(sum_arrives(way, step - 1))
                def _():
                    sum_arrival(way, step - 1).wait_recv()

                @pl.when(sum_sends(way, step) & jnp.logical_not(sum_first(way)))
                def _():
                    add_pipe(
                        part_out.at[rows_of(piece)], land_out.at[way, step - 2],
                        acc_out.at[way, step - 2])
                    sum_copy(way, step, True).start()

    for k in range(line - 1, -1, -1):
        at = rows_of(piece_at(k))
        out_pipe(head_out.at[at], act_out.at[at], part_out.at[at])
        if k == line - 1:
            start_sum(1)

    sfc_ref = b1_ref
    for row in range(1):
        sfc_ref[...] = jnp.zeros_like(sfc_ref)

    def back_body(c_blk, slope_blk, dh_blk, dfc_blk):
        dh_blk[...] = low(dot_nt(c_blk[...], wd_ref[...]))
        step = 512
        for at in range(0, ff, step):
            d = low(dot_nt(c_blk[...], w2_ref[at : at + step, :])
                    * slope_blk[:, at : at + step].astype(jnp.float32))
            dfc_blk[:, at : at + step] = d
            sfc_ref[0:1, at : at + step] += jnp.sum(d.astype(jnp.float32), axis=0, keepdims=True)

    back_pipe = pltpu.emit_pipeline(
        back_body, grid=(length // block,), in_specs=[spec(width), spec(ff)],
        out_specs=[spec(qw), spec(ff)])
    locals_[count + 1].wait()
    sum_step = 2
    ln_ref[...] = jnp.zeros_like(ln_ref)

    def cot_sum_body(c_blk):
        ln_ref[4:5] += jnp.sum(c_blk[...].astype(jnp.float32), axis=0, keepdims=True)

    pltpu.emit_pipeline(
        cot_sum_body, grid=(length // block,), in_specs=[spec(width)], out_specs=[])(cot_ref)
    for k in range(line):
        for hop in range(cot_hop, k):
            step_line(1, hop)
            cot_hop = hop + 1
        if k == line - 1:
            while sum_step < line - 1:
                start_sum(sum_step)
                sum_step += 1
            for hop in range(cot_hop, line - 1):
                step_line(1, hop)
        at = rows_of(piece_at(k))
        back_pipe(cot_all.at[at], slope_out.at[at], dh_out.at[at], dfc_out.at[at])
    def attend_back(q_buf, o_buf, do_buf, lse_buf, dq_acc, dk_acc, dv_acc, delta, loaded):
        copies = [
            pltpu.make_async_copy(q_out, q_buf, loaded.at[0]),
            pltpu.make_async_copy(head_out, o_buf, loaded.at[1]),
            pltpu.make_async_copy(dh_out, do_buf, loaded.at[2]),
            pltpu.make_async_copy(lse_out, lse_buf, loaded.at[3]),
        ]
        for copy in copies:
            copy.start()
        dq_acc[...] = jnp.zeros_like(dq_acc)
        for copy in copies:
            copy.wait()
        blocks = total_len // qblock
        scale = HD ** -0.5
        for i in range(blocks):
            rows = slice(i * qblock, (i + 1) * qblock)
            for h in range(heads):
                cols = slice(h * HD, (h + 1) * HD)
                inner = jnp.sum(
                    do_buf[rows, cols].astype(jnp.float32) * o_buf[rows, cols].astype(jnp.float32),
                    axis=1, keepdims=True)
                delta[h : h + 1, rows] = jnp.broadcast_to(inner, (qblock, 128)).T[0:1]

        def one(h, i, j, diagonal):
            cols = slice(h * HD, (h + 1) * HD)
            qrows = pl.ds(pl.multiple_of(i * qblock, qblock), qblock)
            krows = pl.ds(pl.multiple_of(j * qblock, qblock), qblock)
            query, grad = q_buf[qrows, cols], do_buf[qrows, cols]
            key, value = k_buf[krows, cols], v_buf[krows, cols]
            s = dot_nt(key, query) * (scale * LOG2E)
            p = jnp.exp2(s - lse_buf[h : h + 1, qrows])
            if diagonal:
                kp = lax.broadcasted_iota(jnp.int32, s.shape, 0)
                qp = lax.broadcasted_iota(jnp.int32, s.shape, 1)
                p = jnp.where(kp <= qp, p, 0.0)
            dp_blk = dot_nt(value, grad)
            ds = low(p * (dp_blk - delta[h : h + 1, qrows]))
            dv = dot_nn(low(p), grad)
            dk = dot_nn(ds, query)
            dq_acc[qrows, cols] += dot_tn(ds, key)
            if diagonal:
                dv_acc[krows, cols] = dv
                dk_acc[krows, cols] = dk
            else:
                dv_acc[krows, cols] += dv
                dk_acc[krows, cols] += dk

        def outer(j, carry):
            for h in range(heads):
                one(h, j, j, True)

            def inner(i, c):
                for h in range(heads):
                    one(h, i, j, False)
                return c

            lax.fori_loop(j + 1, blocks, inner, 0)
            return carry

        lax.fori_loop(0, blocks, outer, 0)
        sq_ref[...] = jnp.zeros_like(sq_ref)

        def finish_body(cos_blk, sin_blk, out_blk):
            rows = pl.ds(pl.multiple_of(pl.program_id(0) * block, block), block)
            cosine, sine = cos_blk[...], sin_blk[...]
            for which, acc in enumerate((dq_acc, dk_acc, dv_acc)):
                for h in range(heads):
                    at = which * qw + h * HD
                    g = acc[rows, h * HD : (h + 1) * HD]
                    if which < 2:
                        g = g * scale
                        first = g[:, :128]
                        first = first * cosine - turned(first) * sine
                        out_blk[:, at : at + 128] = low(first)
                        out_blk[:, at + 128 : at + HD] = low(g[:, 128:])
                    else:
                        out_blk[:, at : at + HD] = low(g)
                    sq_ref[:, at : at + HD] += jnp.sum(
                        out_blk[:, at : at + HD].astype(jnp.float32), axis=0, keepdims=True)

        pltpu.emit_pipeline(
            finish_body, grid=(total_len // block,), in_specs=[spec(128), spec(128)],
            out_specs=[spec(3 * qw)],
        )(cos_ref, sin_ref, dqkv_out)

    pl.run_scoped(
        attend_back,
        pltpu.VMEM((total_len, qw), jnp.bfloat16),
        pltpu.VMEM((total_len, qw), jnp.bfloat16),
        pltpu.VMEM((total_len, qw), jnp.bfloat16),
        pltpu.VMEM((heads, total_len), jnp.float32),
        pltpu.VMEM((total_len, qw), jnp.float32),
        pltpu.VMEM((total_len, qw), jnp.float32),
        pltpu.VMEM((total_len, qw), jnp.float32),
        pltpu.VMEM((heads, total_len), jnp.float32),
        pltpu.SemaphoreType.DMA((4,)),
    )
    while sum_step < line:
        start_sum(sum_step)
        sum_step += 1


    def e_body(dqkv_blk, dfc_blk, x_blk, stat_blk, e_blk):
        mean, rstd = stat_blk[:, 0:1], stat_blk[:, 1:2]
        step = 512
        for at in range(0, width, step):
            cols = slice(at, at + step)
            d1 = dot_nt(dqkv_blk[:, :qw], wq_ref[0, cols, :])
            d1 += dot_nt(dqkv_blk[:, qw : 2 * qw], wq_ref[1, cols, :])
            d1 += dot_nt(dqkv_blk[:, 2 * qw :], wq_ref[2, cols, :])
            d2 = dot_nt(dfc_blk[...], w1_ref[cols, :])
            xhat = (x_blk[:, cols].astype(jnp.float32) - mean) * rstd
            e_blk[:, cols] = low(d1 * kvec[2:3, cols] + d2 * kvec[4:5, cols])
            ln_ref[0:1, cols] += jnp.sum(d1 * xhat, axis=0, keepdims=True)
            ln_ref[1:2, cols] += jnp.sum(d1, axis=0, keepdims=True)
            ln_ref[2:3, cols] += jnp.sum(d2 * xhat, axis=0, keepdims=True)
            ln_ref[3:4, cols] += jnp.sum(d2, axis=0, keepdims=True)

    wspec = lambda n: pl.BlockSpec((wblock, n), lambda i: (i, 0))
    pltpu.emit_pipeline(
        e_body, grid=(total_len // wblock,),
        in_specs=[wspec(3 * qw), wspec(ff), wspec(width), wspec(128)], out_specs=[wspec(width)],
    )(dqkv_out, dfc_out, x_all, stat_out, e_out)
    ends = [
        pltpu.make_async_copy(kvec, vec_out, keep.at[0]),
        pltpu.make_async_copy(sfc_ref, sfc_out, keep.at[1]),
        pltpu.make_async_copy(sq_ref, sq_out, keep.at[2]),
        pltpu.make_async_copy(ln_ref, ln_out, keep.at[3]),
    ]
    for copy in ends:
        copy.start()

    def hidden_body(ways):
        def run(x_blk, part_blk, *blks):
            total = x_blk[...].astype(jnp.float32) + part_blk[...].astype(jnp.float32)
            for blk in blks[:-1]:
                total = total + blk[...].astype(jnp.float32)
            blks[-1][...] = low(total + kvec[0:1] + kvec[1:2])

        pltpu.emit_pipeline(
            run, grid=(length // block,), in_specs=[spec(width)] * (2 + len(ways)),
            out_specs=[spec(width)],
        )(x_ref, part_out.at[rows_of(tp)], *[land_out.at[w, line - 2] for w in ways], hidden_out)

    for way in range(2):
        @pl.when(sum_arrives(way, line - 1))
        def _():
            sum_arrival(way, line - 1).wait_recv()

    @pl.when(tp == 0)
    def _():
        hidden_body([1])

    @pl.when(tp == line - 1)
    def _():
        hidden_body([0])

    @pl.when((tp > 0) & (tp < line - 1))
    def _():
        hidden_body([0, 1])

    for step in range(1, line):
        for way in range(2):
            @pl.when(sum_sends(way, step))
            def _():
                sum_copy(way, step, False).wait_send()

    for a in range(count):
        for slot in range(1 + 2 * hops):
            pair_copy(a, slot).wait_send()
        for hop in range(hops):
            for way in range(2):
                ring_copy(a, way, hop).wait_send()
    for b in range(2):
        for hop in range(line - 1):
            for way in range(2):
                @pl.when(sends(way, hop))
                def _():
                    line_copy(b, way, hop).wait_send()
    for copy in ends:
        copy.wait()


def head(small, wq, w1, wd, w2, x, cot, cosine, sine, n_q, n_b, dp_count, tp_count, collective_id):
    piece, width = x.shape
    length = piece * tp_count
    qw, ff = wd.shape[0], w2.shape[0]
    heads = qw // HD
    chips = dp_count // 2
    hops = chips // 2
    bf, f32 = jnp.bfloat16, jnp.float32
    sds = jax.ShapeDtypeStruct
    steps = max(tp_count - 1, 1)
    out_shape = [
        sds((length, width), bf), sds((length, width), bf),
        sds((length, width), bf), sds((length, width), bf),
        sds((length, qw), bf), sds((length, qw), bf), sds((length, qw), bf),
        sds((length, ff), bf), sds((length, ff), bf), sds((length, 128), f32),
        sds((length, qw), bf), sds((heads, length), f32), sds((length, width), bf),
        sds((length, qw), bf), sds((length, ff), bf),
        sds((2, steps, piece, width), bf), sds((2, steps, piece, width), bf),
        sds((length, 3 * qw), bf), sds((length, width), bf), sds((piece, width), bf),
        sds((8, width), f32), sds((1, ff), f32), sds((1, 3 * qw), f32), sds((8, width), f32),
    ]
    dma = pltpu.SemaphoreType.DMA
    hbm = pl.BlockSpec(memory_space=pl.ANY)
    line = max(tp_count - 1, 1)
    return pl.pallas_call(
        functools.partial(head_kernel, (chips, tp_count, heads, n_q, n_b)),
        out_shape=out_shape,
        in_specs=[hbm] * 9,
        out_specs=[hbm] * len(out_shape),
        scratch_shapes=[
            pltpu.VMEM((small.shape[0] * dp_count, 128), bf),
            pltpu.VMEM((3, width, qw), bf),
            pltpu.VMEM((width, ff), bf),
            pltpu.VMEM((qw, width), bf),
            pltpu.VMEM((ff, width), bf),
            pltpu.VMEM((8, width), f32),
            pltpu.VMEM((1, 3 * qw), f32),
            pltpu.VMEM((1, ff), f32),
            pltpu.VMEM((length, qw), bf),
            pltpu.VMEM((length, qw), bf),
            pltpu.VMEM((1, 3 * qw), f32),
            pltpu.VMEM((8, width), f32),
            dma((5, 2, hops)), dma((5, 2, hops)),
            dma((5, 1 + 2 * hops)), dma((5, 1 + 2 * hops)),
            dma((2, 2, line)), dma((2, 2, line)), dma((7,)),
            dma((2, line)), dma((2, line)), dma((4,)),
        ],
        compiler_params=pltpu.CompilerParams(
            collective_id=collective_id, has_side_effects=True,
            vmem_limit_bytes=62 * 1024 * 1024),
        name="head",
    )(small, wq, w1, wd, w2, x, cot, cosine, sine)


def tail_kernel(cfg, *refs):
    chips, line = cfg
    hops = chips // 2
    refs = list(refs)

    def take(n):
        out, refs[:n] = refs[:n], []
        return out

    act, heads_in, cot, n1, n2, dfc, dqkv, line_ref, flat_ref = take(9)
    own_fc2, own_dense, own_fc1, own_qkv, own_small = take(5)
    held, paired, landed, first_landed = take(4)
    small, s_held, s_paired, s_landed, line_land = take(5)
    (pair_send, pair_recv, ring_send, ring_recv, s_load, s_pair_send, s_pair_recv, s_ring_send,
     s_ring_recv, line_send, line_recv) = refs
    ff, qw = act.shape[1], heads_in.shape[1]
    length = act.shape[0]
    rows = held.shape[1]
    dp = lax.axis_index("dp")
    tp = lax.axis_index("tp")
    core = lax.rem(dp, 2)
    place = ring_place(lax.div(dp, 2), chips)

    def chip_at(ring_pos):
        return ring_place(lax.rem(ring_pos + chips, chips), chips)

    right, left = chip_at(place + 1) * 2 + core, chip_at(place - 1) * 2 + core
    sibling = dp + 1 - 2 * core
    barrier = pltpu.get_barrier_semaphore()
    for partner in (right, left, sibling):
        pl.semaphore_signal(barrier, 1, device_id={"dp": partner}, device_id_type=MESH)
    for n in range(1, line):
        pl.semaphore_signal(
            barrier, 1, device_id={"tp": lax.rem(tp + n, line)}, device_id_type=MESH)
    pl.semaphore_wait(barrier, 3 + line - 1)

    def line_copy(n):
        return pltpu.make_async_remote_copy(
            src_ref=line_ref, dst_ref=line_land.at[n - 1],
            send_sem=line_send.at[n - 1], recv_sem=line_recv.at[n - 1],
            device_id={"tp": lax.rem(tp + n, line)}, device_id_type=MESH)

    for n in range(1, line):
        line_copy(n).start()

    offsets = [hops]
    for near in range(hops - 1, 0, -1):
        offsets += [near, -near]
    offsets.append(0)
    own = chips - 1
    spans = [(0, ff), (ff, qw), (ff + qw, ff), (2 * ff + qw, 3 * qw)]

    def f32(value):
        return value.astype(jnp.float32)

    def over_rows(count, body):
        step = min(count, 32)

        def run(t, carry):
            body(pl.multiple_of(t * step, step), step)
            return carry

        lax.fori_loop(0, count // step, run, 0)

    def pair_arrival(slot, unit):
        at, wide = spans[unit]
        view = paired.at[slot, :, pl.ds(at, wide)]
        return pltpu.make_async_remote_copy(
            src_ref=view, dst_ref=view,
            send_sem=pair_send.at[slot, unit], recv_sem=pair_recv.at[slot, unit],
            device_id={"dp": sibling}, device_id_type=MESH)

    def pair_sum(slot, unit):
        at, wide = spans[unit]
        cols = slice(at, at + wide)
        pair_arrival(slot, unit).wait_recv()

        def body(r, n):
            r = pl.ds(r, n)
            held[slot, r, cols] = low(f32(held[slot, r, cols]) + f32(paired[slot, r, cols]))

        over_rows(rows, body)

    def slot_of(way, step):
        return offsets.index((hops - step) * (1 if way == 0 or step == 0 else -1))

    def ring_rows(way, step):
        return (way * (rows // 2), rows // 2) if step == 0 else (0, rows)

    def ring_copy(way, step, unit):
        at, wide = spans[unit]
        first, n = ring_rows(way, step)
        view = held.at[slot_of(way, step), pl.ds(first, n), pl.ds(at, wide)]
        if step == 0:
            dst = first_landed.at[pl.ds(first, n), pl.ds(at, wide)]
        else:
            dst = landed.at[way, step - 1, :, pl.ds(at, wide)]
        return pltpu.make_async_remote_copy(
            src_ref=view, dst_ref=dst,
            send_sem=ring_send.at[way, step, unit], recv_sem=ring_recv.at[way, step, unit],
            device_id={"dp": right if way == 0 else left}, device_id_type=MESH)

    def add_landed(way, step, unit):
        at, wide = spans[unit]
        cols = slice(at, at + wide)
        slot = slot_of(way, step + 1)
        first, n = ring_rows(way, step)
        ring_copy(way, step, unit).wait_recv()

        def body(r, size):
            r = pl.ds(pl.multiple_of(r + first, 16), size)
            if step == 0:
                moved = first_landed[r, cols]
            else:
                moved = landed[way, step - 1, r, cols]
            held[slot, r, cols] = low(f32(held[slot, r, cols]) + f32(moved))

        over_rows(n, body)

    def ring_after(slot, units):
        for step in range(hops):
            for way in range(2):
                if slot_of(way, step) != slot or slot == own:
                    continue
                for unit in units:
                    if step > 0:
                        add_landed(way, step - 1, unit)
                    ring_copy(way, step, unit).start()

    def compute(big, mid, lhs, turn, out, lhs_sem, big_sem, mid_sem):
        loads = [(cot, 0, slot) for slot in range(chips)]
        loads += [(src, 2, slot) for slot in range(chips) for src in (n2, n1)]

        def lhs_load(i):
            src, _, slot = loads[i]
            chip = chip_at(place + offsets[slot])
            cols = pl.ds(pl.multiple_of(chip * 2 * rows, 128), 2 * rows)
            return pltpu.make_async_copy(src.at[:, cols], lhs.at[i % 2], lhs_sem.at[i % 2])

        phase_loads = (
            (pltpu.make_async_copy(act, big, big_sem.at[0]),
             pltpu.make_async_copy(heads_in, mid.at[:, pl.ds(0, qw)], mid_sem.at[0])),
            (pltpu.make_async_copy(dfc, big, big_sem.at[1]),
             pltpu.make_async_copy(dqkv, mid, mid_sem.at[1])),
        )
        lhs_load(0).start()
        for copy in phase_loads[0]:
            copy.start()
        busy = [None, None]
        counter = 0
        pending = []

        def product(i, slot, unit, rhs):
            nonlocal counter
            at, wide = spans[unit]
            which = counter % 2
            counter += 1
            if busy[which] is not None:
                busy[which].wait_send()
            step = 512 if wide % 512 == 0 else 256
            for col in range(0, wide, step):
                out[which, :, col : col + step] = low(
                    dot_nn(turn[...], rhs[:, col : col + step]))
            mine = pl.ds(pl.multiple_of(core * rows, 16), rows)
            held[slot, :, at : at + wide] = out[which, mine, :wide]
            theirs = pl.ds(pl.multiple_of((1 - core) * rows, 16), rows)
            copy = pltpu.make_async_remote_copy(
                src_ref=out.at[which, theirs, pl.ds(0, wide)],
                dst_ref=paired.at[slot, :, pl.ds(at, wide)],
                send_sem=pair_send.at[slot, unit], recv_sem=pair_recv.at[slot, unit],
                device_id={"dp": sibling}, device_id_type=MESH)
            copy.start()
            busy[which] = copy
            while pending:
                pair_sum(*pending.pop(0))
            pending.append((slot, unit))

        def settle():
            while pending:
                pair_sum(*pending.pop(0))

        def left_side(i):
            lhs_load(i).wait()
            if i + 1 < len(loads):
                lhs_load(i + 1).start()
            turn[...] = lhs[i % 2].T

        for phase in range(2):
            units = (0, 1) if phase == 0 else (2, 3)
            for slot in range(chips):
                if phase == 0:
                    left_side(slot)
                    if slot == 0:
                        for copy in phase_loads[0]:
                            copy.wait()
                    product(slot, slot, 0, big)
                    product(slot, slot, 1, mid)
                else:
                    i = chips + 2 * slot
                    left_side(i)
                    if slot == 0:
                        phase_loads[1][0].wait()
                    product(i, slot, 2, big)
                    left_side(i + 1)
                    if slot == 0:
                        phase_loads[1][1].wait()
                    product(i + 1, slot, 3, mid)
                if slot == 0:
                    settle()
                    ring_after(0, units)
                elif slot == chips - 2:
                    settle()
                    for ready in range(1, chips - 1):
                        ring_after(ready, units)
            if phase == 0:
                for copy in phase_loads[1]:
                    copy.start()
        settle()
        for copy in busy:
            copy.wait_send()

    pl.run_scoped(
        compute,
        pltpu.VMEM((length, ff), jnp.bfloat16),
        pltpu.VMEM((length, 3 * qw), jnp.bfloat16),
        pltpu.VMEM((2, length, 2 * rows), jnp.bfloat16),
        pltpu.VMEM((2 * rows, length), jnp.bfloat16),
        pltpu.VMEM((2, 2 * rows, max(ff, 3 * qw)), jnp.bfloat16),
        pltpu.SemaphoreType.DMA((2,)),
        pltpu.SemaphoreType.DMA((2,)),
        pltpu.SemaphoreType.DMA((2,)),
    )

    for n in range(1, line):
        line_copy(n).wait_recv()
    total = line_ref[...]
    for n in range(1, line):
        total = total + line_land[n - 1]
    rows_z = line_ref.shape[1]
    small[:, :rows_z] = total
    small[:, rows_z:] = flat_ref[...]
    s_rows = small.shape[1]

    def s_pair(slot):
        chip = chip_at(place + offsets[slot])
        return pltpu.make_async_remote_copy(
            src_ref=small.at[chip * 2 + 1 - core], dst_ref=s_paired.at[slot],
            send_sem=s_pair_send.at[slot], recv_sem=s_pair_recv.at[slot],
            device_id={"dp": sibling}, device_id_type=MESH)

    def s_keep(slot):
        chip = chip_at(place + offsets[slot])
        return pltpu.make_async_copy(small.at[chip * 2 + core], s_held.at[slot], s_load.at[slot])

    def s_ring(way, step):
        n = s_rows // 2 if step == 0 else s_rows
        first = way * n if step == 0 else 0
        return pltpu.make_async_remote_copy(
            src_ref=s_held.at[slot_of(way, step), pl.ds(first, n)],
            dst_ref=s_landed.at[way, step, pl.ds(first, n)],
            send_sem=s_ring_send.at[way, step], recv_sem=s_ring_recv.at[way, step],
            device_id={"dp": right if way == 0 else left}, device_id_type=MESH)

    for slot in range(chips):
        s_keep(slot).start()
        s_pair(slot).start()
    for slot in range(chips):
        s_keep(slot).wait()
        s_pair(slot).wait_recv()
        s_held[slot] += s_paired[slot]
        for step in range(hops):
            for way in range(2):
                if slot_of(way, step) != slot or slot == own:
                    continue
                if step > 0:
                    n = s_rows // 2 if step == 1 else s_rows
                    first = way * n if step == 1 else 0
                    s_ring(way, step - 1).wait_recv()
                    s_held[slot, first : first + n] += s_landed[way, step - 1, first : first + n]
                s_ring(way, step).start()
    for way in range(2):
        s_ring(way, hops - 1).wait_recv()
    own_small[...] = s_held[own] + s_landed[0, hops - 1] + s_landed[1, hops - 1]

    def finish(wide_buf, tall_buf, done):
        targets = [
            (0, [own_fc2]), (1, [own_dense]), (2, [own_fc1]),
            (3, [own_qkv.at[w] for w in range(3)]),
        ]
        last = {}

        def total_at(unit, at, size):
            cols = slice(at, at + size)
            value = f32(held[own, :, cols])
            if hops == 1:
                return value + f32(first_landed[:, cols])
            return value + f32(landed[0, hops - 2, :, cols]) + f32(landed[1, hops - 2, :, cols])

        for unit, outs in targets:
            at, wide = spans[unit]
            for way in range(2):
                ring_copy(way, hops - 1, unit).wait_recv()
            if unit < 2:
                if "tall" in last:
                    last["tall"].wait()
                for col in range(0, wide, 256):
                    tall_buf[col : col + 256, :] = total_at(unit, at + col, 256).T
                copy = pltpu.make_async_copy(tall_buf.at[pl.ds(0, wide)], outs[0], done.at[0])
                copy.start()
                last["tall"] = copy
            else:
                if "wide" in last:
                    for copy in last["wide"]:
                        copy.wait()
                for col in range(0, wide, 256):
                    wide_buf[:, col : col + 256] = total_at(unit, at + col, 256)
                each = wide // len(outs)
                copies = [
                    pltpu.make_async_copy(
                        wide_buf.at[:, pl.ds(w * each, each)], out, done.at[1 + w])
                    for w, out in enumerate(outs)
                ]
                for copy in copies:
                    copy.start()
                last["wide"] = copies
        last["tall"].wait()
        for copy in last["wide"]:
            copy.wait()

    pl.run_scoped(
        finish,
        pltpu.VMEM((rows, max(ff, 3 * qw)), jnp.float32),
        pltpu.VMEM((max(ff, qw), rows), jnp.float32),
        pltpu.SemaphoreType.DMA((4,)),
    )
    for way in range(2):
        for step in range(hops):
            for unit in range(4):
                ring_copy(way, step, unit).wait_send()
            s_ring(way, step).wait_send()
    for slot in range(chips):
        s_pair(slot).wait_send()
    for n in range(1, line):
        line_copy(n).wait_send()


def tail(act, heads_in, cot, n1, n2, dfc, dqkv, line_sums, flat_sums, dp_count, tp_count, collective_id):
    chips = dp_count // 2
    hops = chips // 2
    length, ff = act.shape
    qw = heads_in.shape[1]
    rows = cot.shape[1] // dp_count
    cols = 2 * ff + 4 * qw
    rows_s = line_sums.shape[1] + flat_sums.shape[1]
    bf, f32 = jnp.bfloat16, jnp.float32
    dma = pltpu.SemaphoreType.DMA
    hbm = pl.BlockSpec(memory_space=pl.ANY)
    vm = pl.BlockSpec(memory_space=pltpu.VMEM)
    line = max(tp_count - 1, 1)
    sds = jax.ShapeDtypeStruct
    return pl.pallas_call(
        functools.partial(tail_kernel, (chips, tp_count)),
        out_shape=[
            sds((ff, rows), f32), sds((qw, rows), f32), sds((rows, ff), f32),
            sds((3, rows, qw), f32), sds((rows_s, 128), f32),
        ],
        in_specs=[hbm] * 7 + [vm, vm],
        out_specs=[hbm] * 4 + [vm],
        scratch_shapes=[
            pltpu.VMEM((chips, rows, cols), bf),
            pltpu.VMEM((chips, rows, cols), bf),
            pltpu.VMEM((2, max(hops - 1, 1), rows, cols), bf),
            pltpu.VMEM((rows, cols), bf),
            pltpu.VMEM((dp_count, rows_s, 128), f32),
            pltpu.VMEM((chips, rows_s, 128), f32),
            pltpu.VMEM((chips, rows_s, 128), f32),
            pltpu.VMEM((2, hops, rows_s, 128), f32),
            pltpu.VMEM((line,) + line_sums.shape, f32),
            dma((chips, 4)), dma((chips, 4)), dma((2, hops, 4)), dma((2, hops, 4)),
            dma((chips,)), dma((chips,)), dma((chips,)), dma((2, hops)), dma((2, hops)),
            dma((line,)), dma((line,)),
        ],
        compiler_params=pltpu.CompilerParams(
            collective_id=collective_id, has_side_effects=True,
            vmem_limit_bytes=62 * 1024 * 1024),
        cost_estimate=pl.CostEstimate(
            flops=2 * length * cot.shape[1] * cols, bytes_accessed=400_000_000, transcendentals=0),
        name="tail",
    )(act, heads_in, cot, n1, n2, dfc, dqkv, line_sums, flat_sums)


def pack_small(wide, narrow):
    rows = []
    first = jnp.concatenate([part.reshape(-1, 128) for part in wide], axis=0)
    rows.append(jnp.pad(first, ((0, 16 - first.shape[0]), (0, 0))))
    count = 0
    for part in narrow:
        flat = part.reshape(-1)
        need = -(-flat.size // 128)
        rows.append(jnp.pad(flat, (0, need * 128 - flat.size)).reshape(need, 128))
        count += need
    rows.append(jnp.zeros((16 - count, 128), jnp.bfloat16))
    return jnp.concatenate(rows, axis=0)


def by_owner(rows, dp_count):
    count = -(-rows.shape[1] // 2048) * 16
    padded = jnp.pad(rows, ((0, 0), (0, count * 128 - rows.shape[1])))
    return padded.reshape(dp_count, count, 128)


def body(
    hidden_in,
    triple_projection_weight,
    triple_projection_bias,
    attention_out_weight,
    b_dense,
    feedforward_in_weight,
    feedforward_in_bias,
    feedforward_out_weight,
    b_fc2,
    ln1_gain,
    ln1_bias,
    ln2_gain,
    ln2_bias,
    grad_out,
):
    _, piece_len, width = hidden_in.shape
    tp_count = lax.axis_size("tp")
    dp_count = lax.axis_size("dp")
    length = piece_len * tp_count
    cosine, sine = rotary_tables(length)
    small = pack_small(
        [b_dense, b_fc2, ln1_gain, ln1_bias, ln2_gain, ln2_bias],
        [triple_projection_bias, feedforward_in_bias],
    )
    n_q = -(-triple_projection_bias.size // 128)
    n_b = -(-feedforward_in_bias.size // 128)
    outs = head(
        small,
        triple_projection_weight.transpose(1, 0, 2),
        feedforward_in_weight,
        attention_out_weight,
        feedforward_out_weight,
        hidden_in[0],
        grad_out[0],
        cosine,
        sine,
        n_q,
        n_b,
        dp_count,
        tp_count,
        0,
    )
    _, cot_seq, norm_one, norm_two = outs[:4]
    act, head_out, d_fc = outs[7], outs[10], outs[14]
    d_qkv, e_sum, hidden_out, vectors, sum_bfc1, sum_bqkv, ln_sums = outs[17:]
    e_piece = lax.psum_scatter(e_sum, "tp", scatter_dimension=0, tiled=True).astype(jnp.float32)

    cot_piece = grad_out[0].astype(jnp.float32)
    line_sums = ln_sums[:5].reshape(5, dp_count, -1).transpose(1, 0, 2).reshape(dp_count, -1)
    flat_sums = jnp.concatenate([sum_bqkv, sum_bfc1], axis=1).reshape(-1, dp_count).T
    line_rows, flat_rows = by_owner(line_sums, dp_count), by_owner(flat_sums, dp_count)
    own_fc2, own_dense, own_fc1, own_qkv, own_small = tail(
        act, head_out, cot_seq, norm_one, norm_two, d_fc, d_qkv, line_rows, flat_rows,
        dp_count, tp_count, 1,
    )
    e_piece, own_small = lax.optimization_barrier((e_piece, own_small))
    own_line = own_small[: line_rows.shape[1]].reshape(-1)[: line_sums.shape[1]].reshape(5, -1)
    own_flat = own_small[line_rows.shape[1] :].reshape(-1)[: flat_sums.shape[1]]
    split = sum_bqkv.size // dp_count

    x_own = hidden_in[0].astype(jnp.float32)
    mean = jnp.mean(x_own, axis=-1, keepdims=True)
    centered = x_own - mean
    rstd = lax.rsqrt(jnp.mean(centered * centered, axis=-1, keepdims=True) + EPSILON)
    xhat = centered * rstd
    back = (
        e_piece
        - jnp.mean(e_piece, axis=-1, keepdims=True)
        - xhat * jnp.mean(e_piece * xhat, axis=-1, keepdims=True)
    ) * rstd
    grad_in = (cot_piece + back)[None]
    return (
        hidden_out[None],
        grad_in,
        own_qkv.transpose(1, 0, 2),
        own_flat[:split].reshape(triple_projection_bias.shape),
        own_dense,
        own_line[4],
        own_fc1,
        own_flat[split:].reshape(feedforward_in_bias.shape),
        own_fc2,
        own_line[4],
        own_line[0],
        own_line[1],
        own_line[2],
        own_line[3],
    )


def solution(mesh):
    return jax.shard_map(
        body,
        mesh=mesh,
        in_specs=(
            P("dp", "tp", None),
            P("dp", None, "tp"),
            P(None, "tp", "dp"),
            P("tp", "dp"),
            P("dp"),
            P("dp", "tp"),
            P("tp", "dp"),
            P("tp", "dp"),
            P("dp"),
            P("dp"),
            P("dp"),
            P("dp"),
            P("dp"),
            P("dp", "tp", None),
        ),
        out_specs=(
            P("dp", "tp", None),
            P("dp", "tp", None),
            P("dp", None, "tp"),
            P(None, "tp", "dp"),
            P("tp", "dp"),
            P("dp"),
            P("dp", "tp"),
            P("tp", "dp"),
            P("tp", "dp"),
            P("dp"),
            P("dp"),
            P("dp"),
            P("dp"),
            P("dp"),
        ),
        check_vma=False,
    )
```

time: 1190 us -> 595 us (0.50)
  Pallas kernels: 0 us -> 536 us
  waiting for transfers between devices: 492 us -> 6.73 us
  matrix products: 374 us -> 0 us
  other arithmetic: 123 us -> 16.9 us
  blocking collectives: 93.9 us -> 0 us
  local copies, waits for them, and re-layouts: 77.4 us -> 13.1 us
    pallas_call x0 -> x2, Pallas kernels: none -> 536 us  [the longest x1 404 us: head(): pl.pallas_call(functools.partial(head_kernel, (chips, tp_count, heads, n_...]
    dot_general x36 -> x0, matrix products: 374 us -> none  [the longest x1 32.4 us: body(): jnp.einsum('ld,fd->lf', cot_seq, full_fc2, preferred_element_type=jnp.flo...]
    all_gather x6 -> x0, waiting for transfers between devices: 275 us -> none  [the longest x1 127 us: body(): cot_seq = lax.all_gather(grad_out, 'tp', axis=1, tiled=True)[0]]
    reduce_scatter x5 -> x0, waiting for transfers between devices: 144 us -> none  [the longest x1 144 us: body(): lax.psum_scatter(low(partial_value), 'tp', scatter_dimension=0, tiled=True)]
    psum x2 -> x0, blocking collectives: 67.6 us -> none  [the longest x1 41.5 us: body(): shared = lax.psum(shared, ('dp', 'tp')).reshape(5, dp_count, -1)]
    reduce_scatter x1, waiting for transfers between devices: 69.4 us -> 6.71 us  [body(): lax.psum_scatter(e_sum, 'tp', scatter_dimension=0, tiled=True)]
    convert_element_type x9 -> x1, other arithmetic: 36.8 us -> 4.13 us  [body(): lax.psum_scatter(e_sum, 'tp', scatter_dimension=0, tiled=True)]
    unnamed x169 -> x35, local copies, waits for them, and re-layouts: 35.6 us -> 7.82 us
  transfers between devices with their start and end apart: 12 -> 1, of which waited for: 5 -> 1; matrix products, arithmetic and copies ran while one was open for 47% -> 1% of each run, Pallas kernels for 0% -> 22%
where the time goes in v3:
time: 595 us; the launch traced here: 587 us
  Pallas kernels  536 us (90%)
  other arithmetic  16.9 us (3%)
  between operations  14.4 us (2%)
  local copies, waits for them, and re-layouts  13.1 us (2%)
  waiting for transfers between devices  6.73 us (1%)
    pallas_call x1, Pallas kernels, head(): pl.pallas_call(functools.partial(head_kernel, (chips, tp_count, heads, n_...  404 us
    pallas_call x1, Pallas kernels, tail(): pl.pallas_call(functools.partial(tail_kernel, (chips, tp_count)), out_sha...  131 us
  transfers between devices with their start and end apart: 1, of which 1 were waited for; matrix products, arithmetic and copies ran while one was open for 1% of the time, Pallas kernels for 22%

profile of v3, /device:TPU:0, one launch (start us, length us, event | category | flops | bytes accessed | tf_op | source)
XLA Modules:
  0.0 587.0 jit_solution(9884017380427786232)
XLA Ops:
  7.2 0.8 reshape.121
  8.1 0.7 reduce
  8.8 1.4 concatenate.9
  10.2 0.7 fusion.13.refs_0_
  10.9 404.3 %head.1 = (bf16[2048,2048]{1,0:T(8,128)(2,1)}, bf16[2048,2048]{1,0:T(8,128)(2,1)}, bf16[2048,2048]{1,0:T(8,128)(2,1)}, bf16[2048,2048]{1,0:T(8,128)(2,1)}, bf16[...) custom-call(bf16[32,128]{1,0:T(8,128)(2,1)} %fusion.13.refs_0_, ...), custom_call_target="tpu_custom_call" | custom-call | tf_op jit(solution)/shard_map/head/pallas_call | solution.py:715
  415.3 0.6 copy-done.10
  416.2 0.9 copy.34.refs_8_
  417.2 0.6 copy.39
  417.8 131.5 %tail.1 = (f32[2048,256]{1,0:T(8,128)}, f32[512,256]{1,0:T(8,128)}, f32[256,2048]{1,0:T(8,128)}, f32[3,256,512]{2,1,0:T(8,128)}, f32[32,128]{1,0:T(8,128)}) custom-call(bf16[2048,2048]{1,0:T(8,128)(2,1)} %get-tuple-element.35.refs_0_, bf16[2048,512]{1,0:T(8,128)(2,1)} %get-tuple-element.36.refs_1_, bf16[2048,2048]{1,0:T(8,128)(2,1)} %get-tuple-element.37.refs_2_, ...), custom_call_target="tpu_custom_call" | custom-call | flops 51539607552 | bytes 400000000 | tf_op jit(solution)/shard_map/tail/pallas_call | solution.py:1105
  549.3 1.9 convert_reduce_fusion
  551.3 2.4 fusion.9
  553.7 6.7 %reduce-scatter.2.cloned.1.call-done = bf16[512,2048]{1,0:T(8,128)(2,1)} async-done(((bf16[2048,2048]{1,0:T(8,128)(2,1)}), bf16[512,2048]{1,0:T(8,128)(2,1)}) %reduce-scatter.2.cloned.1.call-update) | async-done | bytes 2097168 | tf_op jit(solution)/shard_map/reduce_scatter | solution.py:1202
  560.4 4.1 convert_element_type.18
  564.6 0.6 slice_bitcast_fusion
  565.2 0.6 slice.58
  565.8 0.6 slice.59
  566.4 3.8 fusion.14
  570.2 3.2 fusion.8
  573.5 0.6 copy.47
  574.0 1.3 copy.48
  575.4 1.1 copy.49
  576.5 0.8 copy.50
  577.3 1.3 copy.51
  578.6 1.3 copy.52
  (40 shorter events, 0.6 us)
Async XLA Ops:
  7.2 553.2 %reduce-scatter.2.cloned.1.call-start = ((), (), s32[]{:S(2)}) async-start(), calls=%async_computation.1 | async-start | bytes 10485760 | tf_op jit(solution)/shard_map/reduce_scatter | solution.py:1202
  415.2 0.7 copy-start.10
  415.2 0.7 copy-start.11
  415.2 1.9 copy-start.8
  551.3 13.3 %copy-start.9 = (f32[32,128]{1,0:T(8,128)S(1)}, f32[32,128]{1,0:T(8,128)}, u32[]{:S(2)}) copy-start(f32[32,128]{1,0:T(8,128)} %get-tuple-element.48) | copy-start | bytes 49156
  551.3 15.1 %copy-start = (bf16[1,512,2048]{2,1,0:T(8,128)(2,1)S(1)}, bf16[1,512,2048]{2,1,0:T(8,128)(2,1)}, u32[]{:S(2)}) copy-start(bf16[1,512,2048]{2,1,0:T(8,128)(2,1)} %param.16) | copy-start | bytes 6291460
  565.1 8.3 %copy-start.12 = (f32[256]{0:T(256)}, f32[256]{0:T(256)S(1)}, u32[]{:S(2)}) copy-start(f32[256]{0:T(256)S(1)} %get-tuple-element.110) | copy-start | bytes 3076
  565.2 5.0 copy-start.1
  565.2 5.0 copy-start.2
  570.2 3.8 copy-start.3
  573.5 1.9 copy-start.6
  573.5 3.0 copy-start.7
  574.0 3.3 copy-start.5
  575.4 3.3 copy-start.4
Sparse Core Ops, SparseCore 0:
  415.4 144.9 reduce-scatter.1

commit v4 on v3

--- a/solution.py
+++ b/solution.py
@@ -217,11 +217,7 @@
                 def _():
                     line_copy(b, way, hop + 1).start()
 
-    start_line(0, 0)
-    for a in range(count):
-        for way in range(2):
-            ring_copy(a, way, 0).start()
-        pair_copy(a, 0).start()
+    early, late = range(3), range(3, count)
     locals_ = [
         pltpu.make_async_copy(
             shards[a], shard_view(fulls[a], kinds[a], dp, 0, extents[a]), local.at[a])
@@ -229,23 +225,37 @@
     ]
     locals_.append(pltpu.make_async_copy(x_ref, x_all.at[rows_of(tp)], local.at[count]))
     locals_.append(pltpu.make_async_copy(cot_ref, cot_all.at[rows_of(tp)], local.at[count + 1]))
-    for copy in locals_:
-        copy.start()
-    line_hop = 0
-    for hop in range(hops):
-        for a in range(count):
+
+    def start_ring(group):
+        for a in group:
+            for way in range(2):
+                ring_copy(a, way, 0).start()
+            pair_copy(a, 0).start()
+
+    def step_ring(group, hop):
+        for a in group:
             for way in range(2):
                 ring_copy(a, way, hop, True).wait_recv()
                 if hop + 1 < hops:
                     ring_copy(a, way, hop + 1).start()
                 pair_copy(a, 1 + 2 * hop + way).start()
-            if a == count // 2 and line_hop < line - 2:
-                step_line(0, line_hop)
-                line_hop += 1
-    for a in range(count):
-        locals_[a].wait()
-        for slot in range(1 + 2 * hops):
-            pair_copy(a, slot, True).wait_recv()
+
+    def end_ring(group):
+        for a in group:
+            locals_[a].wait()
+            for slot in range(1 + 2 * hops):
+                pair_copy(a, slot, True).wait_recv()
+
+    start_line(0, 0)
+    start_ring(early)
+    for copy in locals_:
+        copy.start()
+    step_ring(early, 0)
+    start_ring(late)
+    step_line(0, 0)
+    for hop in range(1, hops):
+        step_ring(early, hop)
+    end_ring(early)
 
     small_rows = extents[0][0]
     per = width // dp_count // 128
@@ -321,15 +331,20 @@
 
     locals_[count].wait()
     for k in range(line):
-        if k > 0:
-            for hop in range(line_hop, k):
-                step_line(0, hop)
-                line_hop = hop + 1
+        if k == 1:
+            step_ring(late, 0)
+        if k == line - 1:
+            for hop in range(1, hops):
+                step_ring(late, hop)
+        if k > 1:
+            step_line(0, k - 1)
         if k == line - 1:
             start_line(1, 0)
         at = rows_of(piece_at(k))
         front_pipe(
             x_all.at[at], cos_ref.at[at], sin_ref.at[at], *[ref.at[at] for ref in front_outs])
+
+    end_ring(late)
 
     kv_copies = [
         pltpu.make_async_copy(k_out, k_buf, local.at[0]),
@@ -439,7 +454,8 @@
         o_blk[...] = low(a_blk[...].astype(jnp.float32) + b_blk[...].astype(jnp.float32))
 
     add_pipe = pltpu.emit_pipeline(
-        add_body, grid=(length // block,), in_specs=[spec(width)] * 2, out_specs=[spec(width)])
+        add_body, grid=(length // 128,), in_specs=[pl.BlockSpec((128, width), lambda i: (i, 0))] * 2,
+        out_specs=[pl.BlockSpec((128, width), lambda i: (i, 0))])
 
     def start_sum(step):
         for way in range(2):
@@ -485,7 +501,6 @@
         back_body, grid=(length // block,), in_specs=[spec(width), spec(ff)],
         out_specs=[spec(qw), spec(ff)])
     locals_[count + 1].wait()
-    sum_step = 2
     ln_ref[...] = jnp.zeros_like(ln_ref)
 
     def cot_sum_body(c_blk):
@@ -494,15 +509,11 @@
     pltpu.emit_pipeline(
         cot_sum_body, grid=(length // block,), in_specs=[spec(width)], out_specs=[])(cot_ref)
     for k in range(line):
+        if 2 <= k < line - 1:
+            start_sum(k)
         for hop in range(cot_hop, k):
             step_line(1, hop)
             cot_hop = hop + 1
-        if k == line - 1:
-            while sum_step < line - 1:
-                start_sum(sum_step)
-                sum_step += 1
-            for hop in range(cot_hop, line - 1):
-                step_line(1, hop)
         at = rows_of(piece_at(k))
         back_pipe(cot_all.at[at], slope_out.at[at], dh_out.at[at], dfc_out.at[at])
     def attend_back(q_buf, o_buf, do_buf, lse_buf, dq_acc, dk_acc, dv_acc, delta, loaded):
@@ -564,7 +575,10 @@
             lax.fori_loop(j + 1, blocks, inner, 0)
             return carry
 
-        lax.fori_loop(0, blocks, outer, 0)
+        middle = blocks // 2
+        lax.fori_loop(0, middle, outer, 0)
+        start_sum(line - 1)
+        lax.fori_loop(middle, blocks, outer, 0)
         sq_ref[...] = jnp.zeros_like(sq_ref)
 
         def finish_body(cos_blk, sin_blk, out_blk):
@@ -602,10 +616,6 @@
         pltpu.VMEM((heads, total_len), jnp.float32),
         pltpu.SemaphoreType.DMA((4,)),
     )
-    while sum_step < line:
-        start_sum(sum_step)
-        sum_step += 1
-
 
     def e_body(dqkv_blk, dfc_blk, x_blk, stat_blk, e_blk):
         mean, rstd = stat_blk[:, 0:1], stat_blk[:, 1:2]

time: 595 us -> 571 us (0.960)
  Pallas kernels: 536 us -> 512 us
    pallas_call x1, Pallas kernels: 404 us -> 376 us  [head(): pl.pallas_call(functools.partial(head_kernel, (chips, tp_count, heads, n_...]
  transfers between devices with their start and end apart: 1 -> 1, of which waited for: 1 -> 1; matrix products, arithmetic and copies ran while one was open for 1% -> 1% of each run, Pallas kernels for 22% -> 24%
where the time goes in v4:
time: 571 us; the launch traced here: 563 us
  Pallas kernels  512 us (90%)
  other arithmetic  16.9 us (3%)
  between operations  14.4 us (3%)
  local copies, waits for them, and re-layouts  13.1 us (2%)
  waiting for transfers between devices  6.39 us (1%)
    pallas_call x1, Pallas kernels, head(): pl.pallas_call(functools.partial(head_kernel, (chips, tp_count, heads, n_...  376 us
    pallas_call x1, Pallas kernels, tail(): pl.pallas_call(functools.partial(tail_kernel, (chips, tp_count)), out_sha...  135 us
  transfers between devices with their start and end apart: 1, of which 1 were waited for; matrix products, arithmetic and copies ran while one was open for 1% of the time, Pallas kernels for 24%

profile of v4, /device:TPU:0, one launch (start us, length us, event | category | flops | bytes accessed | tf_op | source)
XLA Modules:
  0.0 562.6 jit_solution(7499072351696783213)
XLA Ops:
  7.2 0.8 reshape.121
  8.1 0.7 reduce
  8.8 1.4 concatenate.9
  10.2 0.7 fusion.13.refs_0_
  10.9 376.5 %head.1 = (bf16[2048,2048]{1,0:T(8,128)(2,1)}, bf16[2048,2048]{1,0:T(8,128)(2,1)}, bf16[2048,2048]{1,0:T(8,128)(2,1)}, bf16[2048,2048]{1,0:T(8,128)(2,1)}, bf16[...) custom-call(bf16[32,128]{1,0:T(8,128)(2,1)} %fusion.13.refs_0_, ...), custom_call_target="tpu_custom_call" | custom-call | tf_op jit(solution)/shard_map/head/pallas_call | solution.py:725
  387.4 0.6 copy-done.10
  388.3 0.9 copy.34.refs_8_
  389.3 0.6 copy.39
  390.0 135.3 %tail.1 = (f32[2048,256]{1,0:T(8,128)}, f32[512,256]{1,0:T(8,128)}, f32[256,2048]{1,0:T(8,128)}, f32[3,256,512]{2,1,0:T(8,128)}, f32[32,128]{1,0:T(8,128)}) custom-call(bf16[2048,2048]{1,0:T(8,128)(2,1)} %get-tuple-element.35.refs_0_, bf16[2048,512]{1,0:T(8,128)(2,1)} %get-tuple-element.36.refs_1_, bf16[2048,2048]{1,0:T(8,128)(2,1)} %get-tuple-element.37.refs_2_, ...), custom_call_target="tpu_custom_call" | custom-call | flops 51539607552 | bytes 400000000 | tf_op jit(solution)/shard_map/tail/pallas_call | solution.py:1115
  525.3 1.9 convert_reduce_fusion
  527.3 2.4 fusion.9
  529.7 6.4 %reduce-scatter.2.cloned.1.call-done = bf16[512,2048]{1,0:T(8,128)(2,1)} async-done(((bf16[2048,2048]{1,0:T(8,128)(2,1)}), bf16[512,2048]{1,0:T(8,128)(2,1)}) %reduce-scatter.2.cloned.1.call-update) | async-done | bytes 2097168 | tf_op jit(solution)/shard_map/reduce_scatter | solution.py:1212
  536.1 4.1 convert_element_type.18
  540.2 0.6 slice_bitcast_fusion
  540.9 0.6 slice.58
  541.4 0.6 slice.59
  542.1 3.8 fusion.14
  545.9 3.2 fusion.8
  549.1 0.6 copy.47
  549.7 1.3 copy.48
  551.0 1.1 copy.49
  552.2 0.8 copy.50
  553.0 1.3 copy.51
  554.3 1.3 copy.52
  (40 shorter events, 0.6 us)
Async XLA Ops:
  7.2 528.9 %reduce-scatter.2.cloned.1.call-start = ((), (), s32[]{:S(2)}) async-start(), calls=%async_computation.1 | async-start | bytes 10485760 | tf_op jit(solution)/shard_map/reduce_scatter | solution.py:1212
  387.3 0.7 copy-start.10
  387.4 0.7 copy-start.11
  387.4 1.9 copy-start.8
  527.3 13.0 %copy-start.9 = (f32[32,128]{1,0:T(8,128)S(1)}, f32[32,128]{1,0:T(8,128)}, u32[]{:S(2)}) copy-start(f32[32,128]{1,0:T(8,128)} %get-tuple-element.48) | copy-start | bytes 49156
  527.3 14.8 %copy-start = (bf16[1,512,2048]{2,1,0:T(8,128)(2,1)S(1)}, bf16[1,512,2048]{2,1,0:T(8,128)(2,1)}, u32[]{:S(2)}) copy-start(bf16[1,512,2048]{2,1,0:T(8,128)(2,1)} %param.16) | copy-start | bytes 6291460
  540.8 8.3 %copy-start.12 = (f32[256]{0:T(256)}, f32[256]{0:T(256)S(1)}, u32[]{:S(2)}) copy-start(f32[256]{0:T(256)S(1)} %get-tuple-element.110) | copy-start | bytes 3076
  540.9 5.0 copy-start.1
  540.9 5.0 copy-start.2
  545.9 3.8 copy-start.3
  549.1 1.9 copy-start.6
  549.1 3.0 copy-start.7
  549.7 3.3 copy-start.5
  551.0 3.3 copy-start.4
Sparse Core Ops, SparseCore 0:
  387.5 148.5 reduce-scatter.1

commit v5 on v4

--- a/solution.py
+++ b/solution.py
@@ -1209,7 +1209,7 @@
     _, cot_seq, norm_one, norm_two = outs[:4]
     act, head_out, d_fc = outs[7], outs[10], outs[14]
     d_qkv, e_sum, hidden_out, vectors, sum_bfc1, sum_bqkv, ln_sums = outs[17:]
-    e_piece = lax.psum_scatter(e_sum, "tp", scatter_dimension=0, tiled=True).astype(jnp.float32)
+    e_piece = lax.psum_scatter(e_sum, "tp", scatter_dimension=0, tiled=True)
 
     cot_piece = grad_out[0].astype(jnp.float32)
     line_sums = ln_sums[:5].reshape(5, dp_count, -1).transpose(1, 0, 2).reshape(dp_count, -1)
@@ -1219,7 +1219,12 @@
         act, head_out, cot_seq, norm_one, norm_two, d_fc, d_qkv, line_rows, flat_rows,
         dp_count, tp_count, 1,
     )
+    nothing = own_small[-1, -1]
+    own_fc2, own_dense, own_fc1, own_qkv = [
+        own + nothing for own in (own_fc2, own_dense, own_fc1, own_qkv)
+    ]
     e_piece, own_small = lax.optimization_barrier((e_piece, own_small))
+    e_piece = e_piece.astype(jnp.float32)
     own_line = own_small[: line_rows.shape[1]].reshape(-1)[: line_sums.shape[1]].reshape(5, -1)
     own_flat = own_small[line_rows.shape[1] :].reshape(-1)[: flat_sums.shape[1]]
     split = sum_bqkv.size // dp_count

time: 571 us -> 565 us (0.989)
  waiting for transfers between devices: 6.39 us -> 0.02 us
    reduce_scatter x1, waiting for transfers between devices: 6.38 us -> 0.01 us  [body(): e_piece = lax.psum_scatter(e_sum, 'tp', scatter_dimension=0, tiled=True)]
    add x0 -> x3, other arithmetic: none -> 5.98 us  [body(): own + nothing]
  transfers between devices with their start and end apart: 1 -> 1, of which waited for: 1 -> 0; matrix products, arithmetic and copies ran while one was open for 1% -> 3% of each run, Pallas kernels for 24% -> 24%
where the time goes in v5:
time: 565 us; the launch traced here: 557 us
  Pallas kernels  512 us (91%)
  other arithmetic  20.3 us (4%)
  between operations  14.4 us (3%)
  local copies, waits for them, and re-layouts  9.92 us (2%)
    pallas_call x1, Pallas kernels, head(): pl.pallas_call(functools.partial(head_kernel, (chips, tp_count, heads, n_...  376 us
    pallas_call x1, Pallas kernels, tail(): pl.pallas_call(functools.partial(tail_kernel, (chips, tp_count)), out_sha...  136 us
  transfers between devices with their start and end apart: 1, of which 0 were waited for; matrix products, arithmetic and copies ran while one was open for 3% of the time, Pallas kernels for 24%

profile of v5, /device:TPU:0, one launch (start us, length us, event | category | flops | bytes accessed | tf_op | source)
XLA Modules:
  0.0 556.7 jit_solution(242686628704497590)
XLA Ops:
  7.2 0.8 reshape.121
  8.1 0.7 reduce
  8.8 1.4 concatenate.9
  10.2 0.7 fusion.12.refs_0_
  10.9 376.4 %head.1 = (bf16[2048,2048]{1,0:T(8,128)(2,1)}, bf16[2048,2048]{1,0:T(8,128)(2,1)}, bf16[2048,2048]{1,0:T(8,128)(2,1)}, bf16[2048,2048]{1,0:T(8,128)(2,1)}, bf16[...) custom-call(bf16[32,128]{1,0:T(8,128)(2,1)} %fusion.12.refs_0_, ...), custom_call_target="tpu_custom_call" | custom-call | tf_op jit(solution)/shard_map/head/pallas_call | solution.py:725
  387.4 0.6 copy-done.10
  388.1 0.1 reshape.127
  388.3 0.9 copy.34.refs_8_
  389.3 0.6 copy.39
  389.9 135.6 %tail.1 = (f32[2048,256]{1,0:T(8,128)}, f32[512,256]{1,0:T(8,128)}, f32[256,2048]{1,0:T(8,128)}, f32[3,256,512]{2,1,0:T(8,128)}, f32[32,128]{1,0:T(8,128)}) custom-call(bf16[2048,2048]{1,0:T(8,128)(2,1)} %get-tuple-element.35.refs_0_, bf16[2048,512]{1,0:T(8,128)(2,1)} %get-tuple-element.36.refs_1_, bf16[2048,2048]{1,0:T(8,128)(2,1)} %get-tuple-element.37.refs_2_, ...), custom_call_target="tpu_custom_call" | custom-call | flops 51539607552 | bytes 400000000 | tf_op jit(solution)/shard_map/tail/pallas_call | solution.py:1115
  525.5 1.4 slice.52
  526.9 2.1 convert_reduce_fusion.1
  529.0 2.3 fusion.7
  531.3 1.6 broadcast_add_fusion.2
  532.9 1.9 add_bitcast_fusion
  534.9 2.3 broadcast_add_fusion
  537.2 2.1 broadcast_add_fusion.1
  539.3 0.6 slice_bitcast_fusion
  539.9 0.6 slice.62
  540.5 0.6 slice.63
  541.1 3.3 convert_reduce_fusion
  544.5 3.3 fusion.6
  547.8 0.6 copy.43
  548.3 1.3 copy.44
  (40 shorter events, 0.4 us)
Async XLA Ops:
  7.2 532.1 %reduce-scatter.2.cloned.1.call-start = ((), (), s32[]{:S(2)}) async-start(), calls=%async_computation.1 | async-start | bytes 10485760 | tf_op jit(solution)/shard_map/reduce_scatter | solution.py:1212
  387.3 0.7 copy-start.10
  387.3 0.7 copy-start.11
  387.3 1.9 copy-start.8
  525.5 5.8 %copy-start.7 = (f32[512,256]{1,0:T(8,128)S(1)}, f32[512,256]{1,0:T(8,128)}, u32[]{:S(2)}) copy-start(f32[512,256]{1,0:T(8,128)} %get-tuple-element.49) | copy-start | bytes 1572868
  525.5 7.4 %copy-start.6 = (f32[3,256,512]{2,1,0:T(8,128)S(1)}, f32[3,256,512]{2,1,0:T(8,128)}, u32[]{:S(2)}) copy-start(f32[3,256,512]{2,1,0:T(8,128)} %get-tuple-element.47) | copy-start | bytes 4718596
  526.9 8.0 %copy-start.5 = (f32[2048,256]{1,0:T(8,128)S(1)}, f32[2048,256]{1,0:T(8,128)}, u32[]{:S(2)}) copy-start(f32[2048,256]{1,0:T(8,128)} %get-tuple-element.51) | copy-start | bytes 6291460
  531.3 5.8 %copy-start.4 = (f32[256,2048]{1,0:T(8,128)S(1)}, f32[256,2048]{1,0:T(8,128)}, u32[]{:S(2)}) copy-start(f32[256,2048]{1,0:T(8,128)} %get-tuple-element.50) | copy-start | bytes 6291460
  534.9 4.4 copy-start.9
  534.9 6.2 %copy-start = (bf16[1,512,2048]{2,1,0:T(8,128)(2,1)S(1)}, bf16[1,512,2048]{2,1,0:T(8,128)(2,1)}, u32[]{:S(2)}) copy-start(bf16[1,512,2048]{2,1,0:T(8,128)(2,1)} %param.16) | copy-start | bytes 6291460
  539.8 7.9 %copy-start.12 = (f32[256]{0:T(256)}, f32[256]{0:T(256)S(1)}, u32[]{:S(2)}) copy-start(f32[256]{0:T(256)S(1)} %get-tuple-element.110) | copy-start | bytes 3076
  539.9 4.5 copy-start.1
  539.9 4.5 copy-start.2
  544.5 3.9 copy-start.3
Sparse Core Ops, SparseCore 0:
  387.5 148.7 reduce-scatter.1
